TPU v7x, 32 devices: a whole 2x2x4 slice. The times are simulated.
32 devices in a mesh: images: 8 (over y, x, core), rows: 4 (over z).
Axes of the slice: x: 2, y: 2, z: 4, core: 2. Of those that a mesh axis runs over, the one named last changes fastest.
Arguments:
- tokens: bfloat16 [16, 16, 32, 1152], P('images', 'rows'), may hold values from -6 to 6
- cotangent: bfloat16 [16, 16, 32, 1152], P('images', 'rows'), may hold values from -6 to 6
- heights: int32 [16], P('images'), may hold values from 8 to 16, as said below
- widths: int32 [16], P('images'), may hold values from 12 to 32, as said below
- timesteps: int32 [16], P('images'), may hold values from 0 to 999
- rel_index: int32 [5, 63], replicated, may hold values from 0 to 255
- ln1_gain: bfloat16 [1152], replicated, may hold values from 0.5 to 1.5
- ln1_bias: bfloat16 [1152], replicated, may hold values from -4 to 4
- w_qkv: bfloat16 [1152, 3456], P('images', 'rows'), may hold values from -0.1875 to 0.1875
- w_time: bfloat16 [1152, 2304], P('images', 'rows'), may hold values from -0.1875 to 0.1875
- rel_table: bfloat16 [256, 16], replicated, may hold values from -6 to 6
- w_out: bfloat16 [1152, 1152], P('images', 'rows'), may hold values from -1.5 to 1.5
- out_bias: bfloat16 [1152], replicated, may hold values from -4 to 4
- ln2_gain: bfloat16 [1152], replicated, may hold values from 0.5 to 1.5
- ln2_bias: bfloat16 [1152], replicated, may hold values from -4 to 4
- w_fc1: bfloat16 [1152, 4608], P('images', 'rows'), may hold values from -0.1875 to 0.1875
- fc1_bias: bfloat16 [4608], replicated, may hold values from -4 to 4
- w_fc2: bfloat16 [4608, 1152], P('images', 'rows'), may hold values from -0.09375 to 0.09375
- fc2_bias: bfloat16 [1152], replicated, may hold values from -4 to 4
Outputs:
- mixed: bfloat16 [16, 16, 32, 1152], P('images', 'rows')
- grad_tokens: bfloat16 [16, 16, 32, 1152], P('images', 'rows')
- grad_ln1_gain: float32 [1152], replicated
- grad_ln1_bias: float32 [1152], replicated
- grad_w_qkv: float32 [1152, 3456], P('images', 'rows')
- grad_w_time: float32 [1152, 2304], P('images', 'rows')
- grad_rel_table: float32 [256, 16], replicated
- grad_w_out: float32 [1152, 1152], P('images', 'rows')
- grad_out_bias: float32 [1152], replicated
- grad_ln2_gain: float32 [1152], replicated
- grad_ln2_bias: float32 [1152], replicated
- grad_w_fc1: float32 [1152, 4608], P('images', 'rows')
- grad_fc1_bias: float32 [4608], replicated
- grad_w_fc2: float32 [4608, 1152], P('images', 'rows')
- grad_fc2_bias: float32 [1152], replicated
Inputs may be any that keep to these rules, and one draw needn't show every extreme that they name: `heights`: in each block of 2 images of one images index, one image has the height 16 and another the height 16 / 2. `widths`: each image's height times width lies between 192 and 320; in each block of 2 images of one images index, an image of height 16 / 2 has the width 32.
All inputs are finite; a program needn't handle non-finite values.
Results may differ from a plain program's by a relative error of at most 0.014.
Values may be sent and summed in bfloat16 or wider, within the bound.
No kernel may reach another device: no remote copies, remote signals or barrier semaphores. Data moves between devices by JAX's collectives and lax.ppermute only.
A program may use at most 192 MiB of HBM per device.

v0:
```python
import math

import jax
import jax.numpy as jnp
from jax import lax
from jax.sharding import PartitionSpec as P

HALO = 2


norm_eps = 1e-06
masked_score = -1000000000.0


def with_halo(cells, sides, width):
    for axis, dim in sides:
        count = lax.axis_size(axis)
        ends = count - 1
        head = lax.slice_in_dim(cells, 0, width, axis=dim)
        tail = lax.slice_in_dim(cells, cells.shape[dim] - width, cells.shape[dim], axis=dim)
        cells = jnp.concatenate(
            [
                lax.ppermute(tail, axis, [(i, (i + 1) % count) for i in range(ends)]),
                cells,
                lax.ppermute(head, axis, [((i + 1) % count, i) for i in range(ends)]),
            ],
            axis=dim,
        )
    return cells


def from_behind(block, axis, distance):
    devices = range(lax.axis_size(axis))
    route = [(i - distance, i) for i in devices if i - distance in devices]
    return lax.ppermute(block, axis, route)


def normalize(values):
    centre = values - jnp.mean(values, -1, keepdims=True)
    spread = jnp.mean(centre * centre, -1, keepdims=True)
    inverse = lax.rsqrt(spread + norm_eps)
    return (centre * inverse, inverse)


def norm_back(grad_hat, normal_part, inverse):
    first_mean = jnp.mean(grad_hat, -1, keepdims=True)
    second_mean = jnp.mean(grad_hat * normal_part, -1, keepdims=True)
    return inverse * (grad_hat - first_mean - normal_part * second_mean)


def time_features(steps, model_width):
    half_width = model_width // 2
    frequency = jnp.exp(-math.log(10000.0) * jnp.arange(half_width, dtype=jnp.float32) / half_width)
    phases = steps.astype(jnp.float32)[:, None] * frequency[None, :]
    return jnp.concatenate([jnp.cos(phases), jnp.sin(phases)], -1)


def gelu_tanh(values):
    return jax.nn.gelu(values, approximate=True)


def shards(
    tokens,
    cotangent,
    heights,
    widths,
    timesteps,
    rel_index,
    ln1_gain,
    ln1_bias,
    w_qkv,
    w_time,
    rel_table,
    w_out,
    out_bias,
    ln2_gain,
    ln2_bias,
    w_fc1,
    fc1_bias,
    w_fc2,
    fc2_bias,
):
    f32 = jnp.float32
    bf16 = jnp.bfloat16
    image_count, rows_here, grid_cols, model_width = tokens.shape
    head_count = rel_table.shape[1]
    head_dim = model_width // head_count
    score_scale = head_dim ** (-0.5)
    query_cells = rows_here * grid_cols
    key_rows = rows_here + 2 * HALO
    key_cells = key_rows * grid_cols
    slot_count = image_count * query_cells
    row_pieces = (
        lax.all_gather(w_qkv, "images", axis=0, tiled=True),
        lax.all_gather(w_time, "images", axis=0, tiled=True),
        lax.all_gather(w_out, "images", axis=0, tiled=True),
        lax.all_gather(w_fc1, "images", axis=0, tiled=True),
        lax.all_gather(w_fc2, "images", axis=0, tiled=True),
    )
    full_weights = (
        lax.all_gather(row_pieces[0], "rows", axis=1, tiled=True),
        lax.all_gather(row_pieces[1], "rows", axis=1, tiled=True),
        lax.all_gather(row_pieces[2], "rows", axis=1, tiled=True),
        lax.all_gather(row_pieces[3], "rows", axis=1, tiled=True),
        lax.all_gather(row_pieces[4], "rows", axis=1, tiled=True),
    )
    qkv_full, time_full, out_full, fc1_full, fc2_full = full_weights
    gain_one = ln1_gain.astype(f32)
    shift_one = ln1_bias.astype(f32)
    gain_two = ln2_gain.astype(f32)
    shift_two = ln2_bias.astype(f32)
    flat_tokens = tokens.astype(f32).reshape(slot_count, model_width)
    normal_one, inverse_one = normalize(flat_tokens)
    normed_low = (normal_one * gain_one + shift_one).astype(bf16)
    timing_low = time_features(timesteps, model_width).astype(bf16)
    projected = jnp.dot(normed_low, qkv_full, preferred_element_type=f32).reshape(
        image_count, query_cells, 3 * model_width
    )
    time_terms = jnp.dot(timing_low, time_full, preferred_element_type=f32)
    query_low = (projected[..., :model_width] + time_terms[:, None, :model_width]).astype(bf16)
    key_low = projected[..., model_width : 2 * model_width].astype(bf16)
    value_low = (projected[..., 2 * model_width :] + time_terms[:, None, model_width:]).astype(bf16)
    local_pairs = jnp.concatenate([key_low, value_low], -1).reshape(
        image_count, rows_here, grid_cols, 2 * model_width
    )
    extended = with_halo(local_pairs, (("rows", 1),), HALO)
    split_pairs = extended.reshape(image_count, key_cells, 2, head_count, head_dim)
    key_heads = split_pairs[:, :, 0]
    value_heads = split_pairs[:, :, 1]
    query_heads = query_low.reshape(image_count, query_cells, head_count, head_dim)
    row_base = lax.axis_index("rows") * rows_here
    query_row = jnp.arange(query_cells) // grid_cols
    query_col = jnp.arange(query_cells) % grid_cols
    key_row = jnp.arange(key_cells) // grid_cols - HALO
    key_col = jnp.arange(key_cells) % grid_cols
    row_gap = key_row[None, :] - query_row[:, None]
    col_gap = key_col[None, :] - query_col[:, None]
    window = jnp.abs(row_gap) <= HALO
    itself = jnp.arange(key_cells)[None, :] == jnp.arange(query_cells)[:, None] + HALO * grid_cols
    global_key = row_base + key_row
    key_ok = (
        (global_key[None, :] >= 0)
        & (global_key[None, :] < heights[:, None])
        & (key_col[None, :] < widths[:, None])
    )
    allowed = key_ok[:, None, :] & window[None] | itself[None]
    global_query = row_base + query_row
    valid = (global_query[None, :] < heights[:, None]) & (query_col[None, :] < widths[:, None])
    valid_mask = valid.reshape(slot_count, 1).astype(f32)
    offsets = (
        (jnp.clip(row_gap, -HALO, HALO) + HALO) * (2 * grid_cols - 1) + col_gap + grid_cols - 1
    )
    bucket_hits = (
        rel_index.reshape(-1)[:, None] == jnp.arange(rel_table.shape[0])[None, :]
    ).astype(f32)

    def expand(table_values):
        return jnp.dot(bucket_hits, table_values, precision=lax.Precision.HIGHEST).T[:, offsets]

    rel_bias, bias_pull = jax.vjp(expand, rel_table.astype(f32))

    def score_block():
        raw_scores = (
            jnp.einsum("iqhd,ikhd->ihqk", query_heads, key_heads, preferred_element_type=f32)
            * score_scale
            + rel_bias[None]
        )
        return jnp.where(allowed[:, None], raw_scores, masked_score)

    scores = score_block()
    top_score = jnp.max(scores, -1, keepdims=True)
    expo_scores = jnp.exp(scores - top_score)
    score_totals = jnp.sum(expo_scores, -1, keepdims=True)
    log_total = top_score + jnp.log(score_totals)
    prob_low = (expo_scores / score_totals).astype(bf16)
    attended = jnp.einsum("ihqk,ikhd->iqhd", prob_low, value_heads, preferred_element_type=f32)
    attended_low = attended.reshape(slot_count, model_width).astype(bf16)
    branch_out = jnp.dot(attended_low, out_full, preferred_element_type=f32) + out_bias.astype(f32)
    middle = flat_tokens + branch_out
    normal_two, inverse_two = normalize(middle)
    second_low = (normal_two * gain_two + shift_two).astype(bf16)
    hidden_pre = jnp.dot(second_low, fc1_full, preferred_element_type=f32) + fc1_bias.astype(f32)
    hidden_act, gelu_pull = jax.vjp(gelu_tanh, hidden_pre)
    hidden_low = hidden_act.astype(bf16)
    mlp_out = jnp.dot(hidden_low, fc2_full, preferred_element_type=f32) + fc2_bias.astype(f32)
    mixed = (valid_mask * (middle + mlp_out)).reshape(tokens.shape).astype(bf16)
    qkv_back, time_back, out_back, fc1_back, fc2_back = (
        qkv_full,
        time_full,
        out_full,
        fc1_full,
        fc2_full,
    )
    grad_out = cotangent.astype(f32).reshape(slot_count, model_width) * valid_mask
    grad_mlp_low = grad_out.astype(bf16)
    grad_fc2 = jnp.dot(hidden_low.T, grad_mlp_low, preferred_element_type=f32)
    grad_fc2_bias = jnp.sum(grad_mlp_low, 0, dtype=f32)
    grad_act = jnp.dot(grad_mlp_low, fc2_back.T, preferred_element_type=f32)
    grad_pre_low = gelu_pull(grad_act)[0].astype(bf16)
    grad_fc1 = jnp.dot(second_low.T, grad_pre_low, preferred_element_type=f32)
    grad_fc1_bias = jnp.sum(grad_pre_low, 0, dtype=f32)
    grad_second = jnp.dot(grad_pre_low, fc1_back.T, preferred_element_type=f32)
    grad_gain_two = jnp.sum(grad_second * normal_two, 0)
    grad_shift_two = jnp.sum(grad_second, 0)
    grad_middle = grad_out + norm_back(grad_second * gain_two, normal_two, inverse_two)
    grad_branch_low = grad_middle.astype(bf16)
    grad_out_weight = jnp.dot(attended_low.T, grad_branch_low, preferred_element_type=f32)
    grad_out_bias = jnp.sum(grad_branch_low, 0, dtype=f32)
    grad_att_low = jnp.dot(grad_branch_low, out_back.T, preferred_element_type=f32).astype(bf16)
    grad_att_heads = grad_att_low.reshape(image_count, query_cells, head_count, head_dim)
    rescored = score_block()
    prob_full = jnp.exp(rescored - log_total)
    prob_again = prob_full.astype(bf16)
    grad_prob = jnp.einsum(
        "iqhd,ikhd->ihqk", grad_att_heads, value_heads, preferred_element_type=f32
    )
    row_dots = jnp.sum(prob_full * grad_prob, -1, keepdims=True)
    grad_score = (prob_full * (grad_prob - row_dots)).astype(bf16)
    grad_query = (
        jnp.einsum("ihqk,ikhd->iqhd", grad_score, key_heads, preferred_element_type=f32)
        * score_scale
    )
    grad_key_ext = (
        jnp.einsum("ihqk,iqhd->ikhd", grad_score, query_heads, preferred_element_type=f32)
        * score_scale
    )
    grad_value_ext = jnp.einsum(
        "ihqk,iqhd->ikhd", prob_again, grad_att_heads, preferred_element_type=f32
    )
    grad_bias = jnp.sum(grad_score, 0, dtype=f32)
    grad_table = bias_pull(grad_bias)[0]
    grad_pairs = jnp.stack([grad_key_ext, grad_value_ext], 2).reshape(
        image_count, key_rows, grid_cols, 2 * model_width
    )
    upper_part = grad_pairs[:, :HALO]
    lower_part = grad_pairs[:, HALO + rows_here :]
    inner_part = grad_pairs[:, HALO : HALO + rows_here]
    from_below = from_behind(upper_part.astype(jnp.bfloat16), "rows", -1).astype(upper_part.dtype)
    from_above = from_behind(lower_part.astype(jnp.bfloat16), "rows", 1).astype(lower_part.dtype)
    inner_part = (
        inner_part
        + jnp.pad(from_below, ((0, 0), (rows_here - HALO, 0), (0, 0), (0, 0)))
        + jnp.pad(from_above, ((0, 0), (0, rows_here - HALO), (0, 0), (0, 0)))
    )
    grad_pair_low = inner_part.astype(bf16).reshape(slot_count, 2 * model_width)
    grad_query_low = grad_query.reshape(slot_count, model_width).astype(bf16)
    grad_proj_low = jnp.concatenate([grad_query_low, grad_pair_low], -1)
    grad_qkv = jnp.dot(normed_low.T, grad_proj_low, preferred_element_type=f32)
    query_sums = jnp.sum(
        grad_query_low.reshape(image_count, query_cells, model_width), 1, dtype=f32
    )
    value_sums = jnp.sum(
        grad_pair_low[:, model_width:].reshape(image_count, query_cells, model_width), 1, dtype=f32
    )
    time_rows = jnp.concatenate([query_sums, value_sums], -1)
    grad_time = jnp.dot(timing_low.astype(f32).T, time_rows, precision=lax.Precision.HIGHEST)
    grad_normed = jnp.dot(grad_proj_low, qkv_back.T, preferred_element_type=f32)
    grad_gain_one = jnp.sum(grad_normed * normal_one, 0)
    grad_shift_one = jnp.sum(grad_normed, 0)
    grad_input = grad_middle + norm_back(grad_normed * gain_one, normal_one, inverse_one)
    grad_tokens = grad_input.reshape(tokens.shape).astype(bf16)
    tile_sums = (
        lax.psum_scatter(
            grad_qkv.astype(jnp.bfloat16), "rows", scatter_dimension=1, tiled=True
        ).astype(jnp.float32),
        lax.psum_scatter(
            grad_time.astype(jnp.bfloat16), "rows", scatter_dimension=1, tiled=True
        ).astype(jnp.float32),
        lax.psum_scatter(
            grad_out_weight.astype(jnp.bfloat16), "rows", scatter_dimension=1, tiled=True
        ).astype(jnp.float32),
        lax.psum_scatter(
            grad_fc1.astype(jnp.bfloat16), "rows", scatter_dimension=1, tiled=True
        ).astype(jnp.float32),
        lax.psum_scatter(
            grad_fc2.astype(jnp.bfloat16), "rows", scatter_dimension=1, tiled=True
        ).astype(jnp.float32),
    )
    owned = (
        lax.psum_scatter(tile_sums[0], "images", scatter_dimension=0, tiled=True),
        lax.psum_scatter(tile_sums[1], "images", scatter_dimension=0, tiled=True),
        lax.psum_scatter(tile_sums[2], "images", scatter_dimension=0, tiled=True),
        lax.psum_scatter(tile_sums[3], "images", scatter_dimension=0, tiled=True),
        lax.psum_scatter(tile_sums[4], "images", scatter_dimension=0, tiled=True),
    )
    small_sums = lax.psum(
        (
            grad_gain_one,
            grad_shift_one,
            grad_table,
            grad_out_bias,
            grad_gain_two,
            grad_shift_two,
            grad_fc1_bias,
            grad_fc2_bias,
        ),
        ("images", "rows"),
    )
    return (
        mixed,
        grad_tokens,
        small_sums[0],
        small_sums[1],
        owned[0],
        owned[1],
        small_sums[2],
        owned[2],
        small_sums[3],
        small_sums[4],
        small_sums[5],
        owned[3],
        small_sums[6],
        owned[4],
        small_sums[7],
    )


def solution(mesh):
    placed = (
        P("images", "rows", None, None),
        P("images", "rows", None, None),
        P("images"),
        P("images"),
        P("images"),
        P(),
        P(),
        P(),
        P("images", "rows"),
        P("images", "rows"),
        P(),
        P("images", "rows"),
        P(),
        P(),
        P(),
        P("images", "rows"),
        P(),
        P("images", "rows"),
        P(),
    )
    return jax.shard_map(
        shards,
        mesh=mesh,
        in_specs=placed,
        out_specs=(
            P("images", "rows", None, None),
            P("images", "rows", None, None),
            P(),
            P(),
            P("images", "rows"),
            P("images", "rows"),
            P(),
            P("images", "rows"),
            P(),
            P(),
            P(),
            P("images", "rows"),
            P(),
            P("images", "rows"),
            P(),
        ),
        check_vma=False,
    )
```

profile of v0, /device:TPU:0, one launch (start us, length us, event | category | flops | bytes accessed | tf_op | source)
XLA Modules:
  0.0 1792.1 jit_solution(13558091948113852327)
XLA Ops:
  10.0 27.9 %all-gather.15.cloned.1.call-done = bf16[1152,576]{1,0:T(8,128)(2,1)} async-done(((bf16[144,576]{1,0:T(8,128)(2,1)}), bf16[1152,576]{1,0:T(8,128)(2,1)}) %all-gather.15.cloned.1.call-update) | async-done | bytes 1327120 | tf_op jit(solution)/shard_map/all_gather | solution.py:95
  37.9 2.6 copy.82
  40.6 27.0 %all-gather.11.cloned.1.call-done = bf16[1152,864]{1,0:T(8,128)(2,1)} async-done(((bf16[144,864]{1,0:T(8,128)(2,1)}), bf16[1152,864]{1,0:T(8,128)(2,1)}) %all-gather.11.cloned.1.call-update) | async-done | bytes 1990672 | tf_op jit(solution)/shard_map/all_gather | solution.py:94
  67.6 4.1 copy.81
  71.8 12.8 all_gather.34
  85.8 16.6 all-gather.27.cloned.1.call-done
  102.4 2.8 copy.90
  105.2 3.2 reshape.574
  108.5 25.9 %all-gather.21.cloned.1.call-done = bf16[1152,1152]{1,0:T(8,128)(2,1)} async-done(((bf16[144,1152]{1,0:T(8,128)(2,1)}), bf16[1152,1152]{1,0:T(8,128)(2,1)}) %all-gather.21.cloned.1.call-update) | async-done | bytes 2654224 | tf_op jit(solution)/shard_map/all_gather | solution.py:97
  136.7 98.3 %all-gather.17.cloned.1.call-done = bf16[1152,2304]{0,1:T(8,128)(2,1)} async-done(((bf16[1152,576]{0,1:T(8,128)(2,1)}), bf16[1152,2304]{0,1:T(8,128)(2,1)}) %all-gather.17.cloned.1.call-update) | async-done | bytes 5308432 | tf_op jit(solution)/shard_map/all_gather | solution.py:102
  235.0 4.0 fusion.71
  239.0 138.5 %all-gather.13.cloned.1.call-done = bf16[1152,3456]{0,1:T(8,128)(2,1)} async-done(((bf16[1152,864]{0,1:T(8,128)(2,1)}), bf16[1152,3456]{0,1:T(8,128)(2,1)}) %all-gather.13.cloned.1.call-update) | async-done | bytes 7962640 | tf_op jit(solution)/shard_map/all_gather | solution.py:101
  377.5 5.8 fusion
  386.1 5.6 collective-permute-start
  391.8 109.0 %gather_fusion = f32[32768,16]{1,0:T(8,128)} fusion(f32[16,315]{0,1:T(8,128)S(1)} %copy.86, s32[32768]{0:T(1024)S(1)} %broadcast_clamp_fusion), kind=kCustom, calls=%fused_computation | custom fusion | bytes 4325376 | tf_op jit(solution)/shard_map/jvp()/gather | solution.py:158
  500.9 11.1 copy.87
  513.4 3.2 pad_maximum_fusion.1
  516.6 11.2 reshape.547
  527.8 4.9 fusion.73
  532.8 3.0 copy.117
  535.8 4.5 copy.116
  540.3 3.1 fusion.77
  548.4 3.2 fusion.78
  551.8 80.1 %all-gather.25.cloned.1.call-done = bf16[4608,1152]{0,1:T(8,128)(2,1)} async-done(((bf16[4608,288]{0,1:T(8,128)(2,1)}), bf16[4608,1152]{0,1:T(8,128)(2,1)}) %all-gather.25.cloned.1.call-update) | async-done | bytes 10616848 | tf_op jit(solution)/shard_map/all_gather | solution.py:105
  632.0 8.8 fusion.79
  640.8 177.0 %all-gather.23.cloned.1.call-done = bf16[1152,4608]{1,0:T(8,128)(2,1)} async-done(((bf16[1152,1152]{1,0:T(8,128)(2,1)}), bf16[1152,4608]{1,0:T(8,128)(2,1)}) %all-gather.23.cloned.1.call-update) | async-done | bytes 10616848 | tf_op jit(solution)/shard_map/all_gather | solution.py:104
  817.8 11.0 convert_reduce_fusion
  831.0 6.0 convolution_convert_fusion
  837.0 8.8 multiply_reduce_fusion.1
  846.9 2.5 convolution_convert_fusion.4
  849.5 3.6 convolution_convert_fusion.5
  853.0 3.9 reshape.587
  858.9 3.7 multiply_reduce_fusion
  862.6 2.8 convert_reduce_fusion.1
  868.1 2.6 pad_maximum_fusion
  870.7 8.8 copy.95
  879.5 8.8 reshape.551
  888.3 2.6 convert.22
  897.2 22.5 %collective-permute-done.3 = bf16[2,2,32,2304]{3,2,1,0:T(8,128)(2,1)} collective-permute-done((bf16[2,2,32,2304]{3,2,1,0:T(8,128)(2,1)}, bf16[2,2,32,2304]{3,2,1,0:T(8,128)(2,1)}, u32[]{:S(2)}, u32[]{:S(2)}) %collective-permute-start.3) | collective-permute-done | bytes 589856 | tf_op jit(solution)/shard_map/ppermute | solution.py:35
  919.7 15.9 collective-permute-done.2
  937.9 6.2 convolution_convert_fusion.3
  944.3 2.8 copy.101
  947.1 2.9 reshape.576
  950.0 7.2 multiply_reduce_fusion.2
  957.2 5.6 convolution_convert_fusion.2
  962.9 8.8 convolution_convert_fusion.1
  971.7 14.9 copy.109
  986.7 41.4 %reduce-scatter.29.cloned.1.call-done = bf16[4608,288]{0,1:T(8,128)(2,1)} async-done(((bf16[4608,1152]{0,1:T(8,128)(2,1)}), bf16[4608,288]{0,1:T(8,128)(2,1)}) %reduce-scatter.29.cloned.1.call-update) | async-done | bytes 2654224 | tf_op jit(solution)/shard_map/reduce_scatter | solution.py:275
  1028.0 5.5 copy.111
  1033.6 50.5 %reduce-scatter.25.cloned.1.call-done = bf16[1152,288]{0,1:T(8,128)(2,1)} async-done(((bf16[1152,1152]{0,1:T(8,128)(2,1)}), bf16[1152,288]{0,1:T(8,128)(2,1)}) %reduce-scatter.25.cloned.1.call-update) | async-done | bytes 663568 | tf_op jit(solution)/shard_map/reduce_scatter | solution.py:269
  1084.1 2.6 copy.107
  1086.8 94.1 %reduce-scatter.23.cloned.1.call-done = bf16[1152,576]{0,1:T(8,128)(2,1)} async-done(((bf16[1152,2304]{0,1:T(8,128)(2,1)}), bf16[1152,576]{0,1:T(8,128)(2,1)}) %reduce-scatter.23.cloned.1.call-update) | async-done | bytes 1327120 | tf_op jit(solution)/shard_map/reduce_scatter | solution.py:266
  1180.9 3.1 copy.105
  1184.1 137.8 %reduce-scatter.21.cloned.1.call-done = bf16[1152,864]{0,1:T(8,128)(2,1)} async-done(((bf16[1152,3456]{0,1:T(8,128)(2,1)}), bf16[1152,864]{0,1:T(8,128)(2,1)}) %reduce-scatter.21.cloned.1.call-update) | async-done | bytes 1990672 | tf_op jit(solution)/shard_map/reduce_scatter | solution.py:263
  1321.9 4.3 copy.103
  1326.2 178.7 %reduce-scatter.37.cloned.1.call-done = bf16[1152,1152]{1,0:T(8,128)(2,1)} async-done(((bf16[4608,1152]{1,0:T(8,128)(2,1)}), bf16[1152,1152]{1,0:T(8,128)(2,1)}) %reduce-scatter.37.cloned.1.call-update) | async-done | bytes 2654224
  1504.9 5.4 copy.110
  1510.4 4.4 convert_element_type.237
  1516.1 10.2 copy.102
  1526.3 174.2 %scatter_custom_fusion = f32[16,315]{0,1:T(8,128)S(1)} fusion(s32[32768]{0:T(1024)} %bitcast.147, f32[32768,16]{1,0:T(8,128)} %bitcast.130, f32[]{:T(128)} %constant.115.clone.1), kind=kCustom, calls=%fused_computation.106 | custom fusion | flops 524288 | bytes 20672 | tf_op jit(solution)/shard_map/transpose(jvp())/scatter-add | solution.py:158
  1700.9 10.0 fusion.14
  1710.8 43.9 %all-reduce.2 = (f32[1152]{0:T(1024)}, f32[1152]{0:T(1024)}, f32[256,16]{0,1:T(8,128)}, f32[1152]{0:T(1024)}, f32[1152]{0:T(1024)}, /*index=5*/f32[1152]{0:T(1024)}, f32[4608]{0:T(1024)}, f32[1152]{0:T(1024)}) all-reduce(f32[1152]{0:T(1024)S(1)} %get-tuple-element.77, ...), channel_id=1, replica_groups=mesh['images'=8,'rows'=4] {'images','rows'}, use_global_device_ids=true, to_apply=%region_12.13 | all-reduce | flops 15616 | bytes 124928 | tf_op jit(solution)/shard_map/psum | solution.py:286
  1754.7 2.6 add_convert_fusion.1
  1759.7 25.5 %reduce-scatter.27.cloned.1.call-done = f32[144,1152]{1,0:T(8,128)} async-done(((f32[1152,1152]{1,0:T(8,128)}), f32[144,1152]{1,0:T(8,128)}) %reduce-scatter.27.cloned.1.call-update) | async-done | bytes 663568 | tf_op jit(solution)/shard_map/reduce_scatter | solution.py:283
  (195 shorter events, 36.7 us)
Async XLA Ops:
  7.2 128.9 %copy-start = (bf16[256,16]{0,1:T(8,128)(2,1)S(1)}, bf16[256,16]{0,1:T(8,128)(2,1)}, u32[]{:S(2)}) copy-start(bf16[256,16]{0,1:T(8,128)(2,1)} %param.29) | copy-start | bytes 24580
  7.2 30.7 %all-gather.15.cloned.1.call-start = ((), (), s32[]{:S(2)}) async-start(), calls=%async_computation.12 | async-start | bytes 1658880 | tf_op jit(solution)/shard_map/all_gather | solution.py:95
  7.9 59.7 %all-gather.11.cloned.1.call-start = ((), (), s32[]{:S(2)}) async-start(), calls=%async_computation.10 | async-start | bytes 2322432 | tf_op jit(solution)/shard_map/all_gather | solution.py:94
  8.7 93.7 %all-gather.27.cloned.1.call-start = ((), (), s32[]{:S(2)}) async-start(), calls=%async_computation.23 | async-start | bytes 3317760 | tf_op jit(solution)/shard_map/all_gather | solution.py:98
  9.4 125.0 %all-gather.21.cloned.1.call-start = ((), (), s32[]{:S(2)}) async-start(), calls=%async_computation.15 | async-start | bytes 2985984 | tf_op jit(solution)/shard_map/all_gather | solution.py:97
  10.0 225.0 %all-gather.17.cloned.1.call-start = ((), (), s32[]{:S(2)}) async-start(), calls=%async_computation.13 | async-start | bytes 6635520 | tf_op jit(solution)/shard_map/all_gather | solution.py:102
  40.5 31.2 %copy-start.24 = (bf16[144,288]{1,0:T(8,128)(2,1)S(1)}, bf16[144,288]{1,0:T(8,128)(2,1)}, u32[]{:S(2)}) copy-start(bf16[144,288]{1,0:T(8,128)(2,1)} %param.30) | copy-start | bytes 248836
  40.6 336.9 %all-gather.13.cloned.1.call-start = ((), (), s32[]{:S(2)}) async-start(), calls=%async_computation.11 | async-start | bytes 9953280 | tf_op jit(solution)/shard_map/all_gather | solution.py:101
  71.7 476.6 %all-gather.19.cloned.1.call-start = ((), (), s32[]{:S(2)}) async-start(), calls=%async_computation.14 | async-start | bytes 3317760 | tf_op jit(solution)/shard_map/all_gather | solution.py:103
  85.7 546.2 %all-gather.25.cloned.1.call-start = ((), (), s32[]{:S(2)}) async-start(), calls=%async_computation.17 | async-start | bytes 13271040 | tf_op jit(solution)/shard_map/all_gather | solution.py:105
  108.4 26.1 %copy-start.34 = (s32[5,63]{1,0:T(8,128)S(1)}, s32[5,63]{1,0:T(8,128)}, u32[]{:S(2)}) copy-start(s32[5,63]{1,0:T(8,128)} %param.24) | copy-start | bytes 3784
  108.4 26.4 %copy-start.28 = (bf16[1152]{0:T(1024)(128)(2,1)S(1)}, bf16[1152]{0:T(1024)(128)(2,1)}, u32[]{:S(2)}) copy-start(bf16[1152]{0:T(1024)(128)(2,1)} %param.26) | copy-start | bytes 6916
  108.4 26.4 %copy-start.29 = (bf16[1152]{0:T(1024)(128)(2,1)S(1)}, bf16[1152]{0:T(1024)(128)(2,1)}, u32[]{:S(2)}) copy-start(bf16[1152]{0:T(1024)(128)(2,1)} %param.25) | copy-start | bytes 6916
  108.4 26.4 %copy-start.8 = (bf16[2,4,32,1152]{3,2,1,0:T(8,128)(2,1)S(1)}, bf16[2,4,32,1152]{3,2,1,0:T(8,128)(2,1)}, u32[]{:S(2)}) copy-start(bf16[2,4,32,1152]{3,2,1,0:T(8,128)(2,1)} %param.19) | copy-start | bytes 1769476
  108.5 27.1 %copy-start.37 = (s32[2]{0:T(128)S(1)}, s32[2]{0:T(128)}, u32[]{:S(2)}) copy-start(s32[2]{0:T(128)} %param.23) | copy-start | bytes 28
  108.5 27.1 %copy-start.26 = (s32[2]{0:T(128)S(1)}, s32[2]{0:T(128)}, u32[]{:S(2)}) copy-start(s32[2]{0:T(128)} %param.22) | copy-start | bytes 28
  108.5 27.1 %copy-start.27 = (s32[2]{0:T(128)S(1)}, s32[2]{0:T(128)}, u32[]{:S(2)}) copy-start(s32[2]{0:T(128)} %param.21) | copy-start | bytes 28
  108.5 709.3 %all-gather.23.cloned.1.call-start = ((), (), s32[]{:S(2)}) async-start(), calls=%async_computation.16 | async-start | bytes 13271040 | tf_op jit(solution)/shard_map/all_gather | solution.py:104
  134.4 893.6 %reduce-scatter.29.cloned.1.call-start = ((), (), s32[]{:S(2)}) async-start(), calls=%async_computation.22 | async-start | bytes 13271040 | tf_op jit(solution)/shard_map/reduce_scatter | solution.py:275
  134.6 104.4 %copy-start.35 = (s32[315]{0:T(512)}, s32[315]{0:T(512)S(1)}, u32[]{:S(2)}) copy-start(s32[315]{0:T(512)S(1)} %eq.39) | copy-start | bytes 3784
  134.8 104.2 %copy-start.23 = (s32[16,2,8,128]{3,1,2,0:T(2,128)}, s32[16,2,8,128]{3,1,2,0:T(2,128)S(1)}, u32[]{:S(2)}) copy-start(s32[16,2,8,128]{3,1,2,0:T(2,128)S(1)} %copy.118) | copy-start | bytes 393220
  383.6 8.2 copy-start.30
  384.8 128.6 %collective-permute-start.1 = (bf16[2,2,32,2304]{3,2,1,0:T(8,128)(2,1)}, bf16[2,2,32,2304]{3,2,1,0:T(8,128)(2,1)}, u32[]{:S(2)}, u32[]{:S(2)}) collective-permute-start(bf16[2,2,32,2304]{3,2,1,0:T(8,128)(2,1)} %get-tuple-element.104), channel_id=1, source_target_pairs={{1,0},{2,1},{3,2},{5,4},{6,5},{7,6},{9,8},{10,9},{11,10},{13,12},{... | collective-permute-start | bytes 1769480 | tf_op jit(solution)/shard_map/ppermute | solution.py:25
  386.1 127.3 %collective-permute-start = (bf16[2,2,32,2304]{3,2,1,0:T(8,128)(2,1)}, bf16[2,2,32,2304]{3,2,1,0:T(8,128)(2,1)}, u32[]{:S(2)}, u32[]{:S(2)}) collective-permute-start(bf16[2,2,32,2304]{3,2,1,0:T(8,128)(2,1)} %get-tuple-element.103), channel_id=1, source_target_pairs={{0,1},{1,2},{2,3},{4,5},{5,6},{6,7},{8,9},{9,10},{10,11},{12,13},{... | collective-permute-start | bytes 1769480 | tf_op jit(solution)/shard_map/ppermute | solution.py:23
  500.9 11.2 copy-start.25
  500.9 11.2 copy-start.31
  500.9 11.2 copy-start.32
  500.9 11.2 copy-start.12
  513.4 27.0 %copy-start.15 = (bf16[2,128,1152]{1,2,0:T(8,128)(2,1)}, bf16[2,128,1152]{1,2,0:T(8,128)(2,1)S(1)}, u32[]{:S(2)}) copy-start(bf16[2,128,1152]{1,2,0:T(8,128)(2,1)S(1)} %copy.84) | copy-start | bytes 1769476
  535.8 7.6 copy-start.4
  543.4 4.3 copy-start.2
  543.4 2.1 copy-start.17
  548.3 3.2 copy-start.20
  548.4 83.6 %copy-start.22 = (bf16[256,1152]{1,0:T(8,128)(2,1)S(1)}, bf16[256,1152]{1,0:T(8,128)(2,1)}, u32[]{:S(2)}) copy-start(bf16[256,1152]{1,0:T(8,128)(2,1)} %fusion.40) | copy-start | bytes 1769476
  828.8 2.2 copy-start.38
  837.0 247.1 %reduce-scatter.25.cloned.1.call-start = ((), (), s32[]{:S(2)}) async-start(), calls=%async_computation.20 | async-start | bytes 3317760 | tf_op jit(solution)/shard_map/reduce_scatter | solution.py:269
  837.0 8.8 copy-start.13
  845.8 1.1 copy-start.21
  846.4 3.0 copy-start.6
  849.4 331.5 %reduce-scatter.23.cloned.1.call-start = ((), (), s32[]{:S(2)}) async-start(), calls=%async_computation.19 | async-start | bytes 6635520 | tf_op jit(solution)/shard_map/reduce_scatter | solution.py:266
  853.0 5.9 copy-start.18
  858.9 3.7 copy-start.10
  858.9 3.7 copy-start.3
  862.6 2.8 copy-start.16
  865.4 1.1 copy-start.11
  890.9 4.5 copy-start.5
  892.0 27.7 %collective-permute-start.3 = (bf16[2,2,32,2304]{3,2,1,0:T(8,128)(2,1)}, bf16[2,2,32,2304]{3,2,1,0:T(8,128)(2,1)}, u32[]{:S(2)}, u32[]{:S(2)}) collective-permute-start(bf16[2,2,32,2304]{3,2,1,0:T(8,128)(2,1)} %get-tuple-element.102), channel_id=1, source_target_pairs={{0,1},{1,2},{2,3},{4,5},{5,6},{6,7},{8,9},{9,10},{10,11},{12,13},{... | collective-permute-start | bytes 1769480 | tf_op jit(solution)/shard_map/ppermute | solution.py:35
  894.1 41.5 %collective-permute-start.2 = (bf16[2,2,32,2304]{3,2,1,0:T(8,128)(2,1)}, bf16[2,2,32,2304]{3,2,1,0:T(8,128)(2,1)}, u32[]{:S(2)}, u32[]{:S(2)}) collective-permute-start(bf16[2,2,32,2304]{3,2,1,0:T(8,128)(2,1)} %get-tuple-element.101), channel_id=1, source_target_pairs={{1,0},{2,1},{3,2},{5,4},{6,5},{7,6},{9,8},{10,9},{11,10},{13,12},{... | collective-permute-start | bytes 1769480 | tf_op jit(solution)/shard_map/ppermute | solution.py:35
  944.1 5.9 copy-start.9
  944.1 377.8 %reduce-scatter.21.cloned.1.call-start = ((), (), s32[]{:S(2)}) async-start(), calls=%async_computation.18 | async-start | bytes 9953280 | tf_op jit(solution)/shard_map/reduce_scatter | solution.py:263
  950.0 7.2 copy-start.19
  962.8 542.1 %reduce-scatter.37.cloned.1.call-start = ((), (), s32[]{:S(2)}) async-start(), calls=%async_computation.27 | async-start | bytes 13271040
  986.6 770.7 %reduce-scatter.39.cloned.1.call-start = ((), (), s32[]{:S(2)}) async-start(), calls=%async_computation.28 | async-start | bytes 7962624
  1033.5 726.1 %reduce-scatter.35.cloned.1.call-start = ((), (), s32[]{:S(2)}) async-start(), calls=%async_computation.26 | async-start | bytes 1990656
  1086.7 673.0 %reduce-scatter.33.cloned.1.call-start = ((), (), s32[]{:S(2)}) async-start(), calls=%async_computation.25 | async-start | bytes 3317760
  1184.0 575.7 %reduce-scatter.31.cloned.1.call-start = ((), (), s32[]{:S(2)}) async-start(), calls=%async_computation.24 | async-start | bytes 4644864
  1326.2 459.0 %reduce-scatter.27.cloned.1.call-start = ((), (), s32[]{:S(2)}) async-start(), calls=%async_computation.21 | async-start | bytes 5971968 | tf_op jit(solution)/shard_map/reduce_scatter | solution.py:283
  1514.8 0.7 copy-start.33
  1514.8 1.1 copy-start.14
  1516.1 184.4 %copy-start.36 = (s32[315]{0:T(512)S(1)}, s32[315]{0:T(512)}, u32[]{:S(2)}) copy-start(s32[315]{0:T(512)} %copy-done.35) | copy-start | bytes 3784
  1700.9 53.9 %copy-start.7 = (f32[256,1152]{1,0:T(8,128)S(1)}, f32[256,1152]{1,0:T(8,128)}, u32[]{:S(2)}) copy-start(f32[256,1152]{1,0:T(8,128)} %copy-done.6) | copy-start | bytes 3538948
  1754.7 30.4 %copy-start.1 = (bf16[256,16]{0,1:T(8,128)(2,1)S(1)}, bf16[256,16]{0,1:T(8,128)(2,1)}, u32[]{:S(2)}) copy-start(bf16[256,16]{0,1:T(8,128)(2,1)} %param.29) | copy-start | bytes 24580
Sparse Core Ops, SparseCore 0:
  9.9 27.9 all-gather.14
  39.8 27.7 all-gather.10
  69.5 32.8 all-gather.26
  104.1 30.2 all-gather.20
  135.8 99.1 all-gather.16
  236.4 141.0 all-gather.12
  379.6 64.5 all-gather.18
  445.8 186.0 all-gather.24
  633.5 184.2 all-gather.22
  837.1 190.9 reduce-scatter.28
  1030.5 53.5 reduce-scatter.24
  1086.3 94.4 reduce-scatter.22
  1183.2 138.6 reduce-scatter.20
  1324.2 180.6 reduce-scatter.36
  1508.3 66.5 reduce-scatter.38
  1579.0 39.4 reduce-scatter.34
  1622.7 45.2 reduce-scatter.32
  1672.2 51.4 reduce-scatter.30
  1728.1 57.0 reduce-scatter.26
where the time goes:
time: 1800 us; the launch traced here: 1790 us
  waiting for transfers between devices  1160 us (64%)
  local copies, waits for them, and re-layouts  244 us (14%)
  other arithmetic  200 us (11%)
  matrix products  105 us (6%)
  blocking collectives  56.6 us (3%)
    unnamed x24, waiting for transfers between devices  182 us
    all_gather x1, waiting for transfers between devices, shards(): lax.all_gather(row_pieces[3], 'rows', axis=1, tiled=True)  177 us
    scatter-add x1, other arithmetic, expand(): jnp.dot(bucket_hits, table_values, precision=lax.Precision.HIGHEST)  174 us
    all_gather x1, waiting for transfers between devices, shards(): lax.all_gather(row_pieces[0], 'rows', axis=1, tiled=True)  138 us
    reduce_scatter x1, waiting for transfers between devices, shards(): lax.psum_scatter(grad_qkv.astype(jnp.bfloat16), 'rows', scatter_dimension...  138 us
    gather x2, local copies, waits for them, and re-layouts, expand(): jnp.dot(bucket_hits, table_values, precision=lax.Precision.HIGHEST)  120 us
    all_gather x1, waiting for transfers between devices, shards(): lax.all_gather(row_pieces[1], 'rows', axis=1, tiled=True)  98.3 us
    reduce_scatter x1, waiting for transfers between devices, shards(): lax.psum_scatter(grad_time.astype(jnp.bfloat16), 'rows', scatter_dimensio...  94.1 us
  transfers between devices with their start and end apart: 23, of which 16 were waited for; matrix products, arithmetic and copies ran while one was open for 29% of the time, Pallas kernels for 0%

commit v1 on v0

v1 whole, which is shorter than its diff:
```python
import functools
import math

import jax
import jax.numpy as jnp
from jax import lax
from jax.experimental import pallas as pl
from jax.experimental.pallas import tpu as pltpu
from jax.sharding import PartitionSpec as P

HALO = 2
LANES = 128

norm_eps = 1e-06
masked_score = -1000000000.0

f32 = jnp.float32
bf16 = jnp.bfloat16

NN = (((1,), (0,)), ((), ()))
NT = (((1,), (1,)), ((), ()))
TN = (((0,), (0,)), ((), ()))


def dot(left, right, dims=NN):
    return lax.dot_general(left, right, dims, preferred_element_type=f32)


def normalize(values):
    centre = values - jnp.mean(values, -1, keepdims=True)
    spread = jnp.mean(centre * centre, -1, keepdims=True)
    inverse = lax.rsqrt(spread + norm_eps)
    return (centre * inverse, inverse)


def norm_back(grad_hat, normal_part, inverse):
    first_mean = jnp.mean(grad_hat, -1, keepdims=True)
    second_mean = jnp.mean(grad_hat * normal_part, -1, keepdims=True)
    return inverse * (grad_hat - first_mean - normal_part * second_mean)


def gelu_tanh(values):
    return jax.nn.gelu(values, approximate=True)


def window(head, head_dim, width):
    first, last = head * head_dim, (head + 1) * head_dim
    start = first // LANES * LANES
    stop = min(-(-last // LANES) * LANES, width)
    return first, last, start, stop


def lane_mask(first, last, start, stop, kind):
    lane = lax.broadcasted_iota(jnp.int32, (1, stop - start), 1) + start
    return jnp.where((lane >= first) & (lane < last), 1.0, 0.0).astype(kind)


def add_tiles(tiles, values, start, stop):
    for at in range(start, stop, LANES):
        part = values[:, at - start : min(at + LANES, stop) - start]
        tiles[at] = part if at not in tiles else tiles[at] + part


def store_tiles(ref, tiles, scale=None):
    for at, part in tiles.items():
        if scale is not None:
            part = part * scale
        ref[0, :, at : at + part.shape[1]] = part.astype(ref.dtype)


def attend_kernel(heads, scale, q_ref, k_ref, v_ref, bias_ref, allow_ref, o_ref, p_ref):
    width = q_ref.shape[-1]
    allowed = allow_ref[0] > 0.5
    tiles = {}
    for head in range(heads):
        span = window(head, width // heads, width)
        start, stop = span[2:]
        query = q_ref[0, :, start:stop] * lane_mask(*span, bf16)
        scores = dot(query, k_ref[0, :, start:stop], NT) * scale + bias_ref[head].astype(f32)
        scores = jnp.where(allowed, scores, masked_score)
        expo = jnp.exp(scores - jnp.max(scores, -1, keepdims=True))
        prob = (expo / jnp.sum(expo, -1, keepdims=True)).astype(bf16)
        p_ref[0, head] = prob
        out = dot(prob, v_ref[0, :, start:stop]) * lane_mask(*span, f32)
        add_tiles(tiles, out, start, stop)
    store_tiles(o_ref, tiles)


def attend_back_kernel(
    heads, scale, cols, q_ref, k_ref, v_ref, p_ref, do_ref, dq_ref, dk_ref, dv_ref, g_ref, sum_ref
):
    width = q_ref.shape[-1]
    rows = q_ref.shape[1] // cols
    step = pl.program_id(0)

    @pl.when(step == 0)
    def _():
        sum_ref[...] = jnp.zeros_like(sum_ref)

    dq_tiles, dk_tiles, dv_tiles = {}, {}, {}
    for head in range(heads):
        span = window(head, width // heads, width)
        start, stop = span[2:]
        mask = lane_mask(*span, bf16)
        query = q_ref[0, :, start:stop] * mask
        grad_out = do_ref[0, :, start:stop] * mask
        prob = p_ref[0, head]
        full = prob.astype(f32)
        grad_prob = dot(grad_out, v_ref[0, :, start:stop], NT)
        weighted = full * grad_prob
        grad_score = (weighted - full * jnp.sum(weighted, -1, keepdims=True)).astype(bf16)
        sum_ref[head] += grad_score.astype(f32)
        dq = dot(grad_score, k_ref[0, :, start:stop]) * lane_mask(*span, f32)
        add_tiles(dq_tiles, dq, start, stop)
        add_tiles(dk_tiles, dot(grad_score, query, TN), start, stop)
        add_tiles(dv_tiles, dot(prob, grad_out, TN), start, stop)
    store_tiles(dq_ref, dq_tiles, scale)
    store_tiles(dk_ref, dk_tiles, scale)
    store_tiles(dv_ref, dv_tiles)

    @pl.when(step == pl.num_programs(0) - 1)
    def _():
        for head in range(heads):
            total = sum_ref[head, :cols]
            for row in range(1, rows):
                part = sum_ref[head, row * cols : (row + 1) * cols]
                total += pltpu.roll(part, part.shape[1] - row * cols, 1)
            g_ref[head] = total


def per_image(*dims):
    return pl.BlockSpec((1,) + dims, lambda i: (i,) + (0,) * len(dims))


def whole(*dims):
    return pl.BlockSpec(dims, lambda i: (0,) * len(dims))


def attend(query, key, value, bias, allowed, scale):
    images, cells, width = query.shape
    heads, _, keys = bias.shape
    return pl.pallas_call(
        functools.partial(attend_kernel, heads, scale),
        grid=(images,),
        in_specs=[
            per_image(cells, width),
            per_image(keys, width),
            per_image(keys, width),
            whole(heads, cells, keys),
            per_image(cells, keys),
        ],
        out_specs=[per_image(cells, width), per_image(heads, cells, keys)],
        out_shape=[
            jax.ShapeDtypeStruct((images, cells, width), bf16),
            jax.ShapeDtypeStruct((images, heads, cells, keys), bf16),
        ],
        compiler_params=pltpu.CompilerParams(vmem_limit_bytes=32 << 20),
        cost_estimate=pl.CostEstimate(
            flops=4 * images * heads * cells * keys * 256,
            bytes_accessed=4 * images * heads * cells * keys,
            transcendentals=images * heads * cells * keys,
        ),
        name="attend",
    )(query, key, value, bias, allowed)


def attend_back(query, key, value, prob, grad_out, scale, cols):
    images, cells, width = query.shape
    _, heads, _, keys = prob.shape
    return pl.pallas_call(
        functools.partial(attend_back_kernel, heads, scale, cols),
        grid=(images,),
        in_specs=[
            per_image(cells, width),
            per_image(keys, width),
            per_image(keys, width),
            per_image(heads, cells, keys),
            per_image(cells, width),
        ],
        out_specs=[
            per_image(cells, width),
            per_image(keys, width),
            per_image(keys, width),
            whole(heads, cols, keys),
        ],
        out_shape=[
            jax.ShapeDtypeStruct((images, cells, width), bf16),
            jax.ShapeDtypeStruct((images, keys, width), bf16),
            jax.ShapeDtypeStruct((images, keys, width), bf16),
            jax.ShapeDtypeStruct((heads, cols, keys), f32),
        ],
        scratch_shapes=[pltpu.VMEM((heads, cells, keys), f32)],
        compiler_params=pltpu.CompilerParams(vmem_limit_bytes=32 << 20),
        cost_estimate=pl.CostEstimate(
            flops=8 * images * heads * cells * keys * 256,
            bytes_accessed=4 * images * heads * cells * keys,
            transcendentals=0,
        ),
        name="attend_back",
    )(query, key, value, prob, grad_out)


def shards(
    tokens,
    cotangent,
    heights,
    widths,
    timesteps,
    rel_index,
    ln1_gain,
    ln1_bias,
    w_qkv,
    w_time,
    rel_table,
    w_out,
    out_bias,
    ln2_gain,
    ln2_bias,
    w_fc1,
    fc1_bias,
    w_fc2,
    fc2_bias,
):
    here, rows_here, cols, width = tokens.shape
    cells = rows_here * cols
    slots = here * cells
    key_rows = rows_here + 2 * HALO
    keys = key_rows * cols
    head_count = rel_table.shape[1]
    head_dim = width // head_count
    scale = head_dim ** (-0.5)
    image_devices = lax.axis_size("images")
    tiles = lax.axis_size("rows")
    low = image_devices // 8
    chunk = width // 8
    quarter = width // 4
    ff_part = fc1_bias.shape[0] // 16
    place = lax.axis_index("images")
    tile = lax.axis_index("rows")
    bits = {"c": low, "x": 2 * low, "y": 4 * low}
    at_c, at_x, at_y = (place // bits[name] % 2 for name in "cxy")


    def partner(value, bit):
        route = [(d, d ^ bit) for d in range(image_devices)]
        return lax.ppermute(value, "images", route)

    def swap(value, name):
        return partner(value, bits[name])

    def pick(at, pair):
        return jnp.where(at == 0, pair[0], pair[1]), jnp.where(at == 0, pair[1], pair[0])

    def in_order(at, own, other):
        return jnp.concatenate(pick(at, (own, other)), 0)

    def with_partner(value, name):
        return jnp.concatenate([value, swap(value, name)], 0)

    def shift(value, step):
        return lax.ppermute(value, "rows", [(d, (d + step) % tiles) for d in range(tiles)])

    def tile_gather(value):
        parts = [value] + [shift(value, step) for step in range(1, tiles)]
        blocks = [lax.select_n((tile - at) % tiles, *parts) for at in range(tiles)]
        return jnp.concatenate(blocks, 1)

    def tile_scatter(value):
        size = value.shape[1] // tiles
        blocks = [value[:, at * size : (at + 1) * size] for at in range(tiles)]
        total = lax.select_n(tile, *blocks).astype(f32)
        for step in range(1, tiles):
            sent = lax.select_n((tile + step) % tiles, *blocks)
            total = total + shift(sent, step).astype(f32)
        return total

    low_groups = [[g * low + d for d in range(low)] for g in range(8)]
    plane_groups = [
        [(j * 2 + c) * low + d for j in range(4)] for c in range(2) for d in range(low)
    ]

    def low_gather(value):
        if low == 1:
            return value
        return lax.all_gather(value, "images", axis=0, tiled=True, axis_index_groups=low_groups)

    def low_scatter(value):
        if low == 1:
            return value
        return lax.psum_scatter(
            value, "images", scatter_dimension=0, tiled=True, axis_index_groups=low_groups
        )

    def plane_gather(value):
        return lax.all_gather(value, "images", axis=0, tiled=True, axis_index_groups=plane_groups)

    def plane_scatter(value):
        return lax.psum_scatter(
            value, "images", scatter_dimension=0, tiled=True, axis_index_groups=plane_groups
        )

    def halves(value, at):
        half = value.shape[0] // 2
        return pick(at, (value[:half], value[half:]))


    qkv_low = low_gather(w_qkv)
    qkv_pairs = qkv_low.reshape(chunk, -1, 2, chunk)
    mine, other = pick(at_c, (qkv_pairs[:, :, 0], qkv_pairs[:, :, 1]))
    qkv_block = in_order(at_c, mine.reshape(chunk, -1), swap(other.reshape(chunk, -1), "c"))
    qkv_rows = tile_gather(qkv_block)
    qkv_full = plane_gather(qkv_rows)

    fc1_low = low_gather(w_fc1).reshape(chunk, 2, 2 * ff_part)
    mine, other = pick(at_c, (fc1_low[:, 0], fc1_low[:, 1]))
    fc1_core = in_order(at_c, mine, swap(other, "c"))
    fc1_mine, fc1_other = pick(at_x, (fc1_core[:, :ff_part], fc1_core[:, ff_part:]))
    fc2_low = low_gather(w_fc2)
    fc2_mine, fc2_other = halves(fc2_low, at_x)
    fc1_swapped = swap(fc1_other, "x")
    fc2_swapped = swap(fc2_other, "x")
    fc1_block = in_order(at_x, fc1_mine, fc1_swapped)
    fc2_block = in_order(at_x, fc2_mine, fc2_swapped)
    out_block = low_gather(w_out)
    rest_rows = tile_gather(jnp.concatenate([out_block, fc1_block, fc2_block], 0))
    out_rows = rest_rows[:chunk]
    fc1_rows = rest_rows[chunk : chunk + 4 * chunk]
    fc2_rows = rest_rows[5 * chunk :]
    out_full = plane_gather(out_rows)
    fc1_full = in_order(at_y, fc1_rows, swap(fc1_rows, "y"))
    fc2_full = in_order(at_y, fc2_rows, swap(fc2_rows, "y"))


    gain_one, shift_one = ln1_gain.astype(f32), ln1_bias.astype(f32)
    gain_two, shift_two = ln2_gain.astype(f32), ln2_bias.astype(f32)
    flat_tokens = tokens.astype(f32).reshape(slots, width)
    normal_one, inverse_one = normalize(flat_tokens)
    normed = (normal_one * gain_one + shift_one).astype(bf16).reshape(tokens.shape)

    down = [(d, d + 1) for d in range(tiles - 1)]
    up = [(d + 1, d) for d in range(tiles - 1)]
    above = lax.ppermute(normed[:, rows_here - HALO :], "rows", down)
    below = lax.ppermute(normed[:, :HALO], "rows", up)
    normed_ext = jnp.concatenate([above, normed, below], 1)
    normed_all = with_partner(normed_ext, "c")
    images = 2 * here
    normed_mid = normed_all[:, HALO : HALO + rows_here].reshape(images * cells, width)
    normed_all = normed_all.reshape(images * keys, width)


    orders = [bits["c"], bits["x"], bits["y"]]
    orders += [1 << b for b in range(low.bit_length() - 1)]
    steps_all = timesteps
    for bit in orders:
        steps_all = jnp.concatenate([steps_all, partner(steps_all, bit)], 0)
    time_rows = w_time.shape[0]
    half_width = width // 2
    feature = place * time_rows + jnp.arange(time_rows)
    exponent = (feature % half_width).astype(f32)
    frequency = jnp.exp(-math.log(10000.0) * exponent / half_width)
    phases = steps_all.astype(f32)[:, None] * frequency[None, :]
    timing = jnp.where(feature[None, :] < half_width, jnp.cos(phases), jnp.sin(phases)).astype(bf16)
    time_part = dot(timing, w_time)
    for bit in orders[:0:-1]:
        half = time_part.shape[0] // 2
        time_part = time_part[:half] + partner(time_part[half:], bit)
    turned = jnp.concatenate([time_part[here:], time_part[:here]], 0)
    time_part = time_part + swap(turned, "c")
    time_pairs = tile_gather(time_part).reshape(images, -1, 2, chunk)
    time_mine = pick(at_c, (time_pairs[:, :, 0], time_pairs[:, :, 1]))[0].reshape(images, width)
    half = width // 2
    time_query, time_value = time_mine[:, :half], time_mine[:, half:]


    heights_all = with_partner(heights, "c")
    widths_all = with_partner(widths, "c")
    query_row = jnp.arange(cells) // cols
    query_col = jnp.arange(cells) % cols
    key_row = jnp.arange(keys) // cols - HALO
    key_col = jnp.arange(keys) % cols
    near = jnp.abs(key_row[None, :] - query_row[:, None]) <= HALO
    itself = jnp.arange(keys)[None, :] == jnp.arange(cells)[:, None] + HALO * cols
    global_key = tile * rows_here + key_row
    key_ok = (
        (global_key[None, :] >= 0)
        & (global_key[None, :] < heights_all[:, None])
        & (key_col[None, :] < widths_all[:, None])
    )
    allowed = (key_ok[:, None, :] & near[None] | itself[None]).astype(f32)
    global_query = tile * rows_here + query_row
    valid = (global_query[None, :] < heights[:, None]) & (query_col[None, :] < widths[:, None])
    valid_mask = valid.reshape(slots, 1).astype(f32)

    heads = head_count // 2
    gaps = 2 * HALO + 1
    spans = 2 * cols - 1
    exact = lax.Precision.HIGHEST
    bucket_hits = (
        rel_index.reshape(-1)[:, None] == jnp.arange(rel_table.shape[0])[None, :]
    ).astype(f32)
    table_pairs = rel_table.astype(f32).reshape(rel_table.shape[0], -1, 2, 2)
    table_mine = pick(at_c, (table_pairs[:, :, 0], table_pairs[:, :, 1]))[0].reshape(-1, heads)
    offset_values = jnp.dot(bucket_hits, table_mine, precision=exact).T
    col_step = jnp.arange(cols)[None, :] - jnp.arange(cols)[:, None] + cols - 1
    step_hits = (jnp.arange(spans)[:, None] == col_step.reshape(1, -1)).astype(f32)
    spread = jnp.dot(offset_values.reshape(heads * gaps, spans), step_hits, precision=exact)
    strip = spread.reshape(heads, gaps, cols, cols).transpose(0, 2, 1, 3)
    strip = strip.reshape(heads, cols, gaps * cols).astype(bf16)
    bias = jnp.concatenate(
        [
            jnp.pad(strip, ((0, 0), (0, 0), (r * cols, keys - (r + gaps) * cols)))
            for r in range(rows_here)
        ],
        1,
    )


    query = (
        dot(normed_mid, qkv_full[:, :half]).reshape(images, cells, half) + time_query[:, None]
    ).astype(bf16)
    key = dot(normed_all, qkv_full[:, half : 2 * half]).astype(bf16).reshape(images, keys, half)
    value = (
        dot(normed_all, qkv_full[:, 2 * half :]).reshape(images, keys, half) + time_value[:, None]
    ).astype(bf16)
    attended, prob = attend(query, key, value, bias, allowed, scale)
    attended = attended.reshape(images * cells, half)

    def core_sum(part):
        size = part.shape[0] // 2
        return part[:size] + swap(part[size:].astype(bf16), "c").astype(f32)

    def quad_sum(part):
        size = part.shape[0] // 2
        part = part[:size] + swap(part[size:].astype(bf16), "c").astype(f32)
        size = size // 2
        return part[:size] + swap(part[size:].astype(bf16), "x").astype(f32)

    def quad_all(value):
        return with_partner(with_partner(value, "x"), "c")

    middle = flat_tokens + core_sum(dot(attended, out_full)) + out_bias.astype(f32)
    normal_two, inverse_two = normalize(middle)
    second = quad_all((normal_two * gain_two + shift_two).astype(bf16))


    grad_out = cotangent.astype(f32).reshape(slots, width) * valid_mask
    grad_mlp_own = grad_out.astype(bf16)
    grad_mlp = quad_all(grad_mlp_own)
    member = at_c * 2 + at_x
    bias_parts = fc1_bias.astype(f32).reshape(tiles, 4, ff_part)
    bias_mine = lax.dynamic_index_in_dim(bias_parts, member, 1, keepdims=False).reshape(-1)
    hidden_pre = dot(second, fc1_full) + bias_mine
    hidden_act, gelu_pull = jax.vjp(gelu_tanh, hidden_pre)
    hidden = hidden_act.astype(bf16)
    grad_fc2 = dot(hidden, grad_mlp, TN).astype(bf16)
    grad_pre = gelu_pull(dot(grad_mlp, fc2_full, NT))[0].astype(bf16)
    grad_second = quad_sum(dot(grad_pre, fc1_full, NT))
    grad_fc1 = dot(second, grad_pre, TN).astype(bf16)
    mlp_out = quad_sum(dot(hidden, fc2_full)) + fc2_bias.astype(f32)
    mixed = (valid_mask * (middle + mlp_out)).reshape(tokens.shape).astype(bf16)
    grad_fc2_bias = jnp.sum(grad_mlp_own, 0, dtype=f32)
    grad_fc1_bias = jnp.sum(grad_pre, 0, dtype=f32)

    grad_gain_two = jnp.sum(grad_second * normal_two, 0)
    grad_shift_two = jnp.sum(grad_second, 0)
    grad_middle = grad_out + norm_back(grad_second * gain_two, normal_two, inverse_two)
    grad_branch_own = grad_middle.astype(bf16)
    grad_out_bias = jnp.sum(grad_branch_own, 0, dtype=f32)
    grad_branch = with_partner(grad_branch_own, "c")


    grad_out_weight = dot(attended, grad_branch, TN).astype(bf16)
    grad_att = dot(grad_branch, out_full, NT).astype(bf16).reshape(images, cells, half)
    grad_query, grad_key, grad_value, grad_strip = attend_back(
        query, key, value, prob, grad_att, scale, cols
    )
    flat_query = grad_query.reshape(images * cells, half)
    flat_key = grad_key.reshape(images * keys, half)
    flat_value = grad_value.reshape(images * keys, half)
    grad_qkv = jnp.concatenate(
        [
            dot(normed_mid, flat_query, TN).astype(bf16),
            dot(normed_all, flat_key, TN).astype(bf16),
            dot(normed_all, flat_value, TN).astype(bf16),
        ],
        1,
    )
    grad_mid = dot(flat_query, qkv_full[:, :half], NT).reshape(images, rows_here, cols, width)
    grad_ext = dot(flat_key, qkv_full[:, half : 2 * half], NT) + dot(
        flat_value, qkv_full[:, 2 * half :], NT
    )
    grad_ext = grad_ext.reshape(images, key_rows, cols, width) + jnp.pad(
        grad_mid, ((0, 0), (HALO, HALO), (0, 0), (0, 0))
    )
    grad_ext = core_sum(grad_ext)
    from_below = lax.ppermute(grad_ext[:, :HALO].astype(bf16), "rows", up).astype(f32)
    from_above = lax.ppermute(grad_ext[:, HALO + rows_here :].astype(bf16), "rows", down)
    from_above = from_above.astype(f32)
    rest = ((0, 0), (rows_here - HALO, 0), (0, 0), (0, 0))
    grad_normed = (
        grad_ext[:, HALO : HALO + rows_here]
        + jnp.pad(from_below, rest)
        + jnp.pad(from_above, (rest[0], rest[1][::-1], rest[2], rest[3]))
    ).reshape(slots, width)
    grad_gain_one = jnp.sum(grad_normed * normal_one, 0)
    grad_shift_one = jnp.sum(grad_normed, 0)
    grad_input = grad_middle + norm_back(grad_normed * gain_one, normal_one, inverse_one)
    grad_tokens = grad_input.reshape(tokens.shape).astype(bf16)


    grad_strip = grad_strip[:, :, : gaps * cols].reshape(heads, cols, gaps, cols)
    grad_strip = grad_strip.transpose(0, 2, 1, 3).reshape(heads * gaps, cols * cols)
    grad_offsets = lax.dot_general(grad_strip, step_hits, NT, precision=exact)
    grad_table = lax.dot_general(
        bucket_hits, grad_offsets.reshape(heads, gaps * spans), (((0,), (1,)), ((), ())),
        precision=exact,
    )


    sums = jnp.concatenate(
        [
            jnp.sum(grad_query, 1, dtype=f32),
            jnp.sum(grad_value, 1, dtype=f32),
        ],
        -1,
    )
    sums = tile_scatter(sums).reshape(images, -1, 1, chunk)
    sums_other = swap(jnp.concatenate([sums[here:], sums[:here]], 0), "c")
    sums = jnp.concatenate(pick(at_c, (sums, sums_other)), 2).reshape(images, -1)
    for bit in orders[1:]:
        sums = jnp.concatenate([sums, partner(sums, bit)], 0)
    grad_time = lax.dot_general(timing.astype(f32), sums, TN, precision=exact)


    def over_y(grad):
        kept, sent = halves(grad, at_y)
        return (kept.astype(f32) + swap(sent, "y").astype(f32)).astype(bf16)

    fc2_sum = tile_scatter(over_y(grad_fc2))
    fc1_sum = tile_scatter(over_y(grad_fc1))
    out_sum = tile_scatter(plane_scatter(grad_out_weight))
    qkv_sum = tile_scatter(plane_scatter(grad_qkv))

    kept, sent = halves(fc2_sum, at_x)
    fc2_own = in_order(at_x, kept, swap(sent.astype(bf16), "x").astype(f32))
    kept, sent = halves(fc1_sum, at_x)
    fc1_pair = jnp.concatenate(pick(at_x, (kept, swap(sent.astype(bf16), "x").astype(f32))), 1)
    kept, sent = halves(fc1_pair, at_c)
    fc1_own = jnp.concatenate(pick(at_c, (kept, swap(sent.astype(bf16), "c").astype(f32))), 1)
    kept, sent = halves(qkv_sum, at_c)
    other = swap(sent.astype(bf16), "c").astype(f32)
    pair = pick(at_c, (kept.reshape(chunk, -1, 1, chunk), other.reshape(chunk, -1, 1, chunk)))
    qkv_own = jnp.concatenate(pair, 2).reshape(chunk, -1)


    mine = (jnp.arange(4) == member).astype(f32)
    fc1_bias_all = grad_fc1_bias.reshape(tiles, 1, ff_part) * mine[None, :, None]
    core = (jnp.arange(2) == at_c).astype(f32)
    table_all = grad_table.reshape(-1, heads // 2, 1, 2) * core[None, None, :, None]
    small = [
        grad_gain_one,
        grad_shift_one,
        table_all.reshape(-1),
        grad_out_bias,
        grad_gain_two,
        grad_shift_two,
        fc1_bias_all.reshape(-1),
        grad_fc2_bias,
    ]
    total = jnp.concatenate(small)
    for bit in orders:
        total = total + partner(total, bit)
    for step in range(tiles.bit_length() - 1):
        route = [(d, d ^ (1 << step)) for d in range(tiles)]
        total = total + lax.ppermute(total, "rows", route)
    pieces = []
    for part in small:
        pieces.append(total[: part.shape[0]])
        total = total[part.shape[0] :]
    return (
        mixed,
        grad_tokens,
        pieces[0],
        pieces[1],
        low_scatter(qkv_own),
        grad_time,
        pieces[2].reshape(rel_table.shape),
        low_scatter(out_sum),
        pieces[3],
        pieces[4],
        pieces[5],
        low_scatter(fc1_own),
        pieces[6],
        low_scatter(fc2_own),
        pieces[7],
    )


def solution(mesh):
    tokens, image, weight = P("images", "rows", None, None), P("images"), P("images", "rows")
    return jax.shard_map(
        shards,
        mesh=mesh,
        in_specs=(
            tokens, tokens, image, image, image, P(), P(), P(), weight, weight,
            P(), weight, P(), P(), P(), weight, P(), weight, P(),
        ),
        out_specs=(
            tokens, tokens, P(), P(), weight, weight, P(), weight, P(), P(),
            P(), weight, P(), weight, P(),
        ),
        check_vma=False,
    )
```

time: 1800 us -> 613 us (0.34)
  the two profiles are of different devices: /device:TPU:0 before, /device:TPU:9 now
where the time goes in v1:
time: 613 us; the launch traced here: 604 us
  waiting for transfers between devices  248 us (40%)
  other arithmetic  83.9 us (14%)
  local copies, waits for them, and re-layouts  83.6 us (14%)
  starting transfers between devices  83.1 us (14%)
  matrix products  68.8 us (11%)
  Pallas kernels  20.6 us (3%)
  between operations  16.7 us (3%)
    ppermute x24, waiting for transfers between devices, shift(): lax.ppermute(value, 'rows', [(d, (d + step) % tiles) for d in range(tiles)])  86.8 us
    ppermute x38, waiting for transfers between devices, partner(): return lax.ppermute(value, 'images', route)  76.6 us
    ppermute x1, waiting for transfers between devices, shards(): above = lax.ppermute(normed[:, rows_here - HALO:], 'rows', down)  66.3 us
    dot_general x18, matrix products, dot(): return lax.dot_general(left, right, dims, preferred_element_type=f32)  60.2 us
    ppermute x38, starting transfers between devices, partner(): return lax.ppermute(value, 'images', route)  46.6 us
    unnamed x200, local copies, waits for them, and re-layouts  34.8 us
    ppermute x24, starting transfers between devices, shift(): lax.ppermute(value, 'rows', [(d, (d + step) % tiles) for d in range(tiles)])  24.9 us
  transfers between devices with their start and end apart: 72, of which 27 were waited for; matrix products, arithmetic and copies ran while one was open for 33% of the time, Pallas kernels for 3%

profile of v1, /device:TPU:9, one launch (start us, length us, event | category | flops | bytes accessed | tf_op | source)
XLA Modules:
  0.0 604.3 jit_solution(471783783908641525)
XLA Ops:
  28.1 4.8 collective-permute-done.4
  32.9 14.9 %collective-permute-start.7 = (s32[2]{0:T(128)}, s32[2]{0:T(128)}, u32[]{:S(2)}, u32[]{:S(2)}) collective-permute-start(s32[2]{0:T(128)} %param.23), channel_id=1, source_target_pairs={{0,4},{4,0},{8,12},{12,8},{16,20},{20,16},{24,28},{28,24},{1,5},{5... | collective-permute-start | bytes 32 | tf_op jit(solution)/shard_map/ppermute | solution.py:246
  47.8 5.6 collective-permute-done.5
  56.8 2.4 copy.153
  70.3 2.2 collective-permute-done.10
  73.3 2.4 collective-permute-done.11
  77.0 4.4 collective-permute-start.12
  87.9 2.3 collective-permute-start.22
  90.4 3.3 collective-permute-start
  93.8 2.4 collective-permute-start.1
  96.6 66.3 %collective-permute-done = bf16[2,2,32,1152]{3,2,1,0:T(8,128)(2,1)S(1)} collective-permute-done((bf16[2,2,32,1152]{3,2,1,0:T(8,128)(2,1)}, bf16[2,2,32,1152]{3,2,1,0:T(8,128)(2,1)S(1)}, u32[]{:S(2)}, u32[]{:S(2)}) %collective-permute-start) | collective-permute-done | bytes 294944 | tf_op jit(solution)/shard_map/ppermute | solution.py:342
  162.9 4.7 collective-permute-done.1
  169.3 2.3 copy.169
  171.6 2.3 copy.172
  173.9 2.3 copy.173
  176.2 4.1 select_select_fusion
  180.3 6.8 %concatenate.119 = bf16[1296,1152]{1,0:T(8,128)(2,1)} concatenate(bf16[1296,288]{1,0:T(8,128)(2,1)} %get-tuple-element.129, bf16[1296,288]{1,0:T(8,128)(2,1)} %get-tuple-element.128, bf16[1296,288]{1,0:T(8,128)(2,1)} %get-tuple-element.127, bf16[1296,288]{1,0:T(8,128)(2,1)} %get-tuple-element.126), dimensions={1} | concatenate | bytes 5971968 | tf_op jit(solution)/shard_map/concatenate | solution.py:266
  193.4 5.8 convolution_convert_fusion.6
  200.9 3.0 fusion.17.q_ref
  204.0 3.8 add_convert_fusion.2.v_ref
  207.8 8.5 %attend.1 = (bf16[4,128,576]{2,1,0:T(8,128)(2,1)S(1)}, bf16[4,8,128,256]{3,2,1,0:T(8,128)(2,1)S(1)}) custom-call(bf16[4,128,576]{2,1,0:T(8,128)(2,1)S(1)} %fusion.17.q_ref, bf16[4,256,576]{2,1,0:T(8,128)(2,1)S(1)} %bitcast.126, bf16[4,256,576]{2,1,0:T(8,128)(2,1)S(1)} %add_convert_fusion.2.v_ref, bf16[8,128,256]{2,1,0:T(8,128)(2,1)S(1)} %fusion.60.bias_ref, ...), custom_call_target="tpu_custom_call" | custom-call | flops 1073741824 | bytes 4194304 | tf_op jit(solution)/shard_map/attend/pallas_call | solution.py:142
  218.7 2.5 fusion.127
  231.4 25.8 %collective-permute-done.27 = bf16[576,1152]{1,0:T(8,128)(2,1)S(1)} collective-permute-done((bf16[576,1152]{1,0:T(8,128)(2,1)S(1)}, bf16[576,1152]{1,0:T(8,128)(2,1)S(1)}, u32[]{:S(2)}, u32[]{:S(2)}) %collective-permute-start.27) | collective-permute-done | bytes 1327136 | tf_op jit(solution)/shard_map/ppermute | solution.py:246
  257.2 2.2 broadcast_select_fusion.5
  271.0 18.3 %collective-permute-done.28 = bf16[576,1152]{1,0:T(8,128)(2,1)} collective-permute-done((bf16[576,1152]{1,0:T(8,128)(2,1)}, bf16[576,1152]{1,0:T(8,128)(2,1)}, u32[]{:S(2)}, u32[]{:S(2)}) %collective-permute-start.28) | collective-permute-done | bytes 1327136 | tf_op jit(solution)/shard_map/ppermute | solution.py:246
  291.3 4.8 convolution_add_fusion.2
  296.1 5.0 convolution_convert_fusion
  304.3 4.4 fusion.8
  308.8 2.2 copy-done.37
  312.1 2.2 collective-permute-start.29
  314.4 6.7 %convert_reduce_fusion = (f32[1152]{0:T(1024)S(1)}, bf16[1024,1152]{1,0:T(8,128)(2,1)S(1)}) fusion(f32[1024,1152]{1,0:T(8,128)S(1)} %convolution_add_fusion.2, bf16[576,1152]{1,0:T(8,128)(2,1)S(1)} %get-tuple-element.125, bf16[576,1152]{1,0:T(8,128)(2,1)S(1)} %get-tuple-element.124, bf16[512,1152]{1,0:T(8,128)(2,1)S(1)} %collective-permute-done.32, ...), kind=kOutput, calls=%fused_computation.12 | convolution fusion | flops 2756246528 | bytes 12096000 | tf_op jit(solution)/shard_map/dot_general | solution.py:26
  321.0 3.5 fusion.9
  327.2 5.0 convolution_convert_fusion.1
  335.1 2.3 slice_add_fusion.2
  343.9 20.7 %collective-permute-done.57 = bf16[576,1152]{1,0:T(8,128)(2,1)} collective-permute-done((bf16[576,1152]{1,0:T(8,128)(2,1)}, bf16[576,1152]{1,0:T(8,128)(2,1)}, u32[]{:S(2)}, u32[]{:S(2)}) %collective-permute-start.57) | collective-permute-done | bytes 1327136 | tf_op jit(solution)/shard_map/ppermute | solution.py:246
  368.9 11.4 %collective-permute-done.65 = bf16[576,288]{1,0:T(8,128)(2,1)S(1)} collective-permute-done((bf16[576,288]{1,0:T(8,128)(2,1)S(1)}, bf16[576,288]{1,0:T(8,128)(2,1)S(1)}, u32[]{:S(2)}, u32[]{:S(2)}) %collective-permute-start.65) | collective-permute-done | bytes 331808 | tf_op jit(solution)/shard_map/ppermute | solution.py:261
  380.2 3.1 collective-permute-start.59
  383.3 17.7 %collective-permute-done.66 = bf16[576,288]{1,0:T(8,128)(2,1)S(1)} collective-permute-done((bf16[576,288]{1,0:T(8,128)(2,1)S(1)}, bf16[576,288]{1,0:T(8,128)(2,1)S(1)}, u32[]{:S(2)}, u32[]{:S(2)}) %collective-permute-start.66) | collective-permute-done | bytes 331808 | tf_op jit(solution)/shard_map/ppermute | solution.py:261
  401.9 6.8 %collective-permute-done.58 = bf16[576,288]{1,0:T(8,128)(2,1)S(1)} collective-permute-done((bf16[576,288]{1,0:T(8,128)(2,1)S(1)}, bf16[576,288]{1,0:T(8,128)(2,1)S(1)}, u32[]{:S(2)}, u32[]{:S(2)}) %collective-permute-start.58) | collective-permute-done | bytes 331808 | tf_op jit(solution)/shard_map/ppermute | solution.py:261
  409.9 8.2 %collective-permute-done.59 = bf16[576,288]{1,0:T(8,128)(2,1)S(1)} collective-permute-done((bf16[576,288]{1,0:T(8,128)(2,1)S(1)}, bf16[576,288]{1,0:T(8,128)(2,1)S(1)}, u32[]{:S(2)}, u32[]{:S(2)}) %collective-permute-start.59) | collective-permute-done | bytes 331808 | tf_op jit(solution)/shard_map/ppermute | solution.py:261
  423.8 2.8 convert_reduce_fusion.5
  428.4 2.3 copy.190
  432.5 3.3 convolution_convert_fusion.2
  435.9 2.6 convolution_convert_fusion.7
  444.9 12.1 %attend_back.1 = (bf16[4,128,576]{2,1,0:T(8,128)(2,1)S(1)}, bf16[4,256,576]{2,1,0:T(8,128)(2,1)S(1)}, bf16[4,256,576]{2,1,0:T(8,128)(2,1)S(1)}, f32[8,32,256]{2,1,0:T(8,128)S(1)}) custom-call(bf16[4,128,576]{2,1,0:T(8,128)(2,1)S(1)} %copy-done.6, bf16[4,256,576]{2,1,0:T(8,128)(2,1)S(1)} %bitcast.127, bf16[4,256,576]{2,1,0:T(8,128)(2,1)S(1)} %copy-done.3, ...), custom_call_target="tpu_custom_call" | custom-call | flops 2147483648 | bytes 4194304 | tf_op jit(solution)/shard_map/attend_back/pallas_call | solution.py:170
  461.5 7.8 %pad_maximum_fusion = bf16[1152,1728]{0,1:T(8,128)(2,1)} fusion(bf16[1152,576]{0,1:T(8,128)(2,1)S(1)} %convolution_convert_fusion.3, bf16[1152,576]{0,1:T(8,128)(2,1)S(1)} %convolution_convert_fusion.4, bf16[1152,576]{0,1:T(8,128)(2,1)S(1)} %convolution_convert_fusion.5), kind=kLoop, calls=%fused_computation.16 | loop fusion | flops 11943936 | bytes 7962624 | tf_op jit(solution)/shard_map/concatenate | solution.py:480
  469.4 6.5 %copy.195 = bf16[1152,1728]{1,0:T(8,128)(2,1)} copy(bf16[1152,1728]{0,1:T(8,128)(2,1)} %pad_maximum_fusion) | data formatting | bytes 7962624
  480.4 3.2 collective-permute-start.49
  485.3 2.2 fusion.22
  487.6 2.2 convolution_add_fusion.1
  489.8 4.4 convolution_add_fusion
  501.8 2.4 fusion.114
  507.0 3.5 collective-permute-start.38
  512.0 2.6 mul.284
  521.0 2.7 fusion.48
  528.2 2.9 collective-permute-done.56
  533.3 2.9 collective-permute-done.41
  536.7 3.1 collective-permute-done.42
  539.9 10.1 %reduce-scatter.4.cloned.1.call-done = bf16[288,1728]{1,0:T(8,128)(2,1)} async-done(((bf16[1152,1728]{1,0:T(8,128)(2,1)}), bf16[288,1728]{1,0:T(8,128)(2,1)}) %reduce-scatter.4.cloned.1.call-update) | async-done | bytes 995344
  550.0 2.4 fusion.118
  556.5 2.3 select_select_fusion.12
  564.8 3.1 collective-permute-done.44
  567.9 19.9 %collective-permute-done.45 = bf16[288,432]{0,1:T(8,128)(2,1)} collective-permute-done((bf16[288,432]{0,1:T(8,128)(2,1)}, bf16[288,432]{0,1:T(8,128)(2,1)}, u32[]{:S(2)}, u32[]{:S(2)}) %collective-permute-start.45) | collective-permute-done | bytes 248864 | tf_op jit(solution)/shard_map/ppermute | solution.py:261
  587.8 3.4 collective-permute-done.46
  (499 shorter events, 169.5 us)
Async XLA Ops:
  7.2 186.2 %all-gather.3.cloned.1.call-start = ((), (), s32[]{:S(2)}) async-start(), calls=%async_computation.1 | async-start | bytes 5160960 | tf_op jit(solution)/shard_map/all_gather | solution.py:295
  10.7 65.0 %collective-permute-start.18 = (bf16[144,576]{1,0:T(8,128)(2,1)}, bf16[144,576]{1,0:T(8,128)(2,1)}, u32[]{:S(2)}, u32[]{:S(2)}) collective-permute-start(bf16[144,576]{1,0:T(8,128)(2,1)} %select_bitcast_fusion), channel_id=1, source_target_pairs={{0,4},{4,0},{8,12},{12,8},{16,20},{20,16},{24,28},{28,24},{1,5},{5... | collective-permute-start | bytes 497672 | tf_op jit(solution)/shard_map/ppermute | solution.py:246
  12.6 73.3 %collective-permute-start.20 = (bf16[288,288]{1,0:T(8,128)(2,1)}, bf16[288,288]{1,0:T(8,128)(2,1)S(1)}, u32[]{:S(2)}, u32[]{:S(2)}) collective-permute-start(bf16[288,288]{1,0:T(8,128)(2,1)} %broadcast_select_fusion.6), channel_id=1, source_target_pairs={{0,8},{4,12},{8,0},{12,4},{16,24},{20,28},{24,16},{28,20},{1,9},{5... | collective-permute-start | bytes 497672 | tf_op jit(solution)/shard_map/ppermute | solution.py:246
  16.3 6.3 %collective-permute-start.3 = (bf16[144,432]{0,1:T(8,128)(2,1)S(1)}, bf16[144,432]{0,1:T(8,128)(2,1)S(1)}, u32[]{:S(2)}, u32[]{:S(2)}) collective-permute-start(bf16[144,432]{0,1:T(8,128)(2,1)S(1)} %bitcast.149), channel_id=1, source_target_pairs={{0,4},{4,0},{8,12},{12,8},{16,20},{20,16},{24,28},{28,24},{1,5},{5... | collective-permute-start | bytes 373256 | tf_op jit(solution)/shard_map/ppermute | solution.py:246
  23.5 9.4 %collective-permute-start.4 = (bf16[288,432]{0,1:T(8,128)(2,1)}, bf16[288,432]{0,1:T(8,128)(2,1)S(1)}, u32[]{:S(2)}, u32[]{:S(2)}) collective-permute-start(bf16[288,432]{0,1:T(8,128)(2,1)} %pad_maximum_fusion.27), channel_id=1, source_target_pairs={{0,1},{1,2},{2,3},{3,0},{4,5},{5,6},{6,7},{7,4},{8,9},{9,10},{10,1... | collective-permute-start | bytes 746504 | tf_op jit(solution)/shard_map/ppermute | solution.py:261
  24.8 28.6 %collective-permute-start.5 = (bf16[288,432]{0,1:T(8,128)(2,1)}, bf16[288,432]{0,1:T(8,128)(2,1)S(1)}, u32[]{:S(2)}, u32[]{:S(2)}) collective-permute-start(bf16[288,432]{0,1:T(8,128)(2,1)} %pad_maximum_fusion.27), channel_id=1, source_target_pairs={{0,2},{1,3},{2,0},{3,1},{4,6},{5,7},{6,4},{7,5},{8,10},{9,11},{10,... | collective-permute-start | bytes 746504 | tf_op jit(solution)/shard_map/ppermute | solution.py:261
  25.8 29.8 %collective-permute-start.6 = (bf16[288,432]{0,1:T(8,128)(2,1)}, bf16[288,432]{0,1:T(8,128)(2,1)S(1)}, u32[]{:S(2)}, u32[]{:S(2)}) collective-permute-start(bf16[288,432]{0,1:T(8,128)(2,1)} %pad_maximum_fusion.27), channel_id=1, source_target_pairs={{0,3},{1,0},{2,1},{3,2},{4,7},{5,4},{6,5},{7,6},{8,11},{9,8},{10,9... | collective-permute-start | bytes 746504 | tf_op jit(solution)/shard_map/ppermute | solution.py:261
  32.9 27.6 %collective-permute-start.7 = (s32[2]{0:T(128)}, s32[2]{0:T(128)}, u32[]{:S(2)}, u32[]{:S(2)}) collective-permute-start(s32[2]{0:T(128)} %param.23), channel_id=1, source_target_pairs={{0,4},{4,0},{8,12},{12,8},{16,20},{20,16},{24,28},{28,24},{1,5},{5... | collective-permute-start | bytes 32 | tf_op jit(solution)/shard_map/ppermute | solution.py:246
  53.4 19.1 %collective-permute-start.16 = (s32[2]{0:T(128)}, s32[2]{0:T(128)}, u32[]{:S(2)}, u32[]{:S(2)}) collective-permute-start(s32[2]{0:T(128)} %param.21), channel_id=1, source_target_pairs={{0,4},{4,0},{8,12},{12,8},{16,20},{20,16},{24,28},{28,24},{1,5},{5... | collective-permute-start | bytes 32 | tf_op jit(solution)/shard_map/ppermute | solution.py:246
  55.7 25.8 %collective-permute-start.17 = (s32[2]{0:T(128)}, s32[2]{0:T(128)}, u32[]{:S(2)}, u32[]{:S(2)}) collective-permute-start(s32[2]{0:T(128)} %param.22), channel_id=1, source_target_pairs={{0,4},{4,0},{8,12},{12,8},{16,20},{20,16},{24,28},{28,24},{1,5},{5... | collective-permute-start | bytes 32 | tf_op jit(solution)/shard_map/ppermute | solution.py:246
  59.2 159.5 %all-gather.5.cloned.1.call-start = ((), (), s32[]{:S(2)}) async-start(), calls=%async_computation.2 | async-start | bytes 1658880 | tf_op jit(solution)/shard_map/all_gather | solution.py:295
  76.9 8.6 %collective-permute-start.19 = (bf16[288,288]{1,0:T(8,128)(2,1)S(1)}, bf16[288,288]{1,0:T(8,128)(2,1)S(1)}, u32[]{:S(2)}, u32[]{:S(2)}) collective-permute-start(bf16[288,288]{1,0:T(8,128)(2,1)S(1)} %broadcast_select_fusion.8), channel_id=1, source_target_pairs={{0,8},{4,12},{8,0},{12,4},{16,24},{20,28},{24,16},{28,20},{1,9},{5... | collective-permute-start | bytes 497672 | tf_op jit(solution)/shard_map/ppermute | solution.py:246
  77.0 5.2 collective-permute-start.12
  82.3 8.0 %collective-permute-start.13 = (f32[4,576]{1,0:T(4,128)S(1)}, f32[4,576]{1,0:T(4,128)S(1)}, u32[]{:S(2)}, u32[]{:S(2)}) collective-permute-start(f32[4,576]{1,0:T(4,128)S(1)} %add.453), channel_id=1, source_target_pairs={{0,1},{1,2},{2,3},{3,0},{4,5},{5,6},{6,7},{7,4},{8,9},{9,10},{10,1... | collective-permute-start | bytes 27656 | tf_op jit(solution)/shard_map/ppermute | solution.py:261
  82.3 8.1 %collective-permute-start.14 = (f32[4,576]{1,0:T(4,128)S(1)}, f32[4,576]{1,0:T(4,128)S(1)}, u32[]{:S(2)}, u32[]{:S(2)}) collective-permute-start(f32[4,576]{1,0:T(4,128)S(1)} %add.453), channel_id=1, source_target_pairs={{0,2},{1,3},{2,0},{3,1},{4,6},{5,7},{6,4},{7,5},{8,10},{9,11},{10,... | collective-permute-start | bytes 27656 | tf_op jit(solution)/shard_map/ppermute | solution.py:261
  84.1 9.6 %collective-permute-start.15 = (f32[4,576]{1,0:T(4,128)S(1)}, f32[4,576]{1,0:T(4,128)S(1)}, u32[]{:S(2)}, u32[]{:S(2)}) collective-permute-start(f32[4,576]{1,0:T(4,128)S(1)} %add.453), channel_id=1, source_target_pairs={{0,3},{1,0},{2,1},{3,2},{4,7},{5,4},{6,5},{7,6},{8,11},{9,8},{10,9... | collective-permute-start | bytes 27656 | tf_op jit(solution)/shard_map/ppermute | solution.py:261
  87.9 81.4 %collective-permute-start.21 = (bf16[1296,288]{0,1:T(8,128)(2,1)}, bf16[1296,288]{0,1:T(8,128)(2,1)}, u32[]{:S(2)}, u32[]{:S(2)}) collective-permute-start(bf16[1296,288]{0,1:T(8,128)(2,1)} %copy.168), channel_id=1, source_target_pairs={{0,1},{1,2},{2,3},{3,0},{4,5},{5,6},{6,7},{7,4},{8,9},{9,10},{10,1... | collective-permute-start | bytes 2239496 | tf_op jit(solution)/shard_map/ppermute | solution.py:261
  87.9 83.7 %collective-permute-start.22 = (bf16[1296,288]{0,1:T(8,128)(2,1)}, bf16[1296,288]{0,1:T(8,128)(2,1)}, u32[]{:S(2)}, u32[]{:S(2)}) collective-permute-start(bf16[1296,288]{0,1:T(8,128)(2,1)} %copy.168), channel_id=1, source_target_pairs={{0,2},{1,3},{2,0},{3,1},{4,6},{5,7},{6,4},{7,5},{8,10},{9,11},{10,... | collective-permute-start | bytes 2239496 | tf_op jit(solution)/shard_map/ppermute | solution.py:261
  90.3 83.6 %collective-permute-start.23 = (bf16[1296,288]{0,1:T(8,128)(2,1)}, bf16[1296,288]{0,1:T(8,128)(2,1)}, u32[]{:S(2)}, u32[]{:S(2)}) collective-permute-start(bf16[1296,288]{0,1:T(8,128)(2,1)} %copy.168), channel_id=1, source_target_pairs={{0,3},{1,0},{2,1},{3,2},{4,7},{5,4},{6,5},{7,6},{8,11},{9,8},{10,9... | collective-permute-start | bytes 2239496 | tf_op jit(solution)/shard_map/ppermute | solution.py:261
  90.4 72.5 %collective-permute-start = (bf16[2,2,32,1152]{3,2,1,0:T(8,128)(2,1)}, bf16[2,2,32,1152]{3,2,1,0:T(8,128)(2,1)S(1)}, u32[]{:S(2)}, u32[]{:S(2)}) collective-permute-start(bf16[2,2,32,1152]{3,2,1,0:T(8,128)(2,1)} %get-tuple-element.160), channel_id=1, source_target_pairs={{0,1},{1,2},{2,3},{4,5},{5,6},{6,7},{8,9},{9,10},{10,11},{12,13},{... | collective-permute-start | bytes 884744 | tf_op jit(solution)/shard_map/ppermute | solution.py:342
  93.8 73.8 %collective-permute-start.1 = (bf16[2,2,32,1152]{3,2,1,0:T(8,128)(2,1)}, bf16[2,2,32,1152]{3,2,1,0:T(8,128)(2,1)S(1)}, u32[]{:S(2)}, u32[]{:S(2)}) collective-permute-start(bf16[2,2,32,1152]{3,2,1,0:T(8,128)(2,1)} %get-tuple-element.161), channel_id=1, source_target_pairs={{1,0},{2,1},{3,2},{5,4},{6,5},{7,6},{9,8},{10,9},{11,10},{13,12},{... | collective-permute-start | bytes 884744 | tf_op jit(solution)/shard_map/ppermute | solution.py:343
  168.8 20.4 %collective-permute-start.2 = (bf16[2,8,32,1152]{3,2,1,0:T(8,128)(2,1)}, bf16[2,8,32,1152]{3,2,1,0:T(8,128)(2,1)}, u32[]{:S(2)}, u32[]{:S(2)}) collective-permute-start(bf16[2,8,32,1152]{3,2,1,0:T(8,128)(2,1)} %pad_maximum_fusion.13), channel_id=1, source_target_pairs={{0,4},{4,0},{8,12},{12,8},{16,20},{20,16},{24,28},{28,24},{1,5},{5... | collective-permute-start | bytes 3538952 | tf_op jit(solution)/shard_map/ppermute | solution.py:246
  188.9 327.6 %all-reduce.10.cloned.1.call-start = ((), (), s32[]{:S(2)}) async-start(), calls=%async_computation.4 | async-start | bytes 2654208
  221.3 6.6 %collective-permute-start.24 = (bf16[256,1152]{1,0:T(8,128)(2,1)S(1)}, bf16[256,1152]{1,0:T(8,128)(2,1)}, u32[]{:S(2)}, u32[]{:S(2)}) collective-permute-start(bf16[256,1152]{1,0:T(8,128)(2,1)S(1)} %slice.674), channel_id=1, source_target_pairs={{0,4},{4,0},{8,12},{12,8},{16,20},{20,16},{24,28},{28,24},{1,5},{5... | collective-permute-start | bytes 1769480 | tf_op jit(solution)/shard_map/ppermute | solution.py:246
  223.8 45.7 %collective-permute-start.31 = (bf16[256,1152]{1,0:T(8,128)(2,1)}, bf16[256,1152]{1,0:T(8,128)(2,1)}, u32[]{:S(2)}, u32[]{:S(2)}) collective-permute-start(bf16[256,1152]{1,0:T(8,128)(2,1)} %fusion.52), channel_id=1, source_target_pairs={{0,8},{4,12},{8,0},{12,4},{16,24},{20,28},{24,16},{28,20},{1,9},{5... | collective-permute-start | bytes 1769480 | tf_op jit(solution)/shard_map/ppermute | solution.py:246
  226.7 30.5 %collective-permute-start.27 = (bf16[576,1152]{1,0:T(8,128)(2,1)S(1)}, bf16[576,1152]{1,0:T(8,128)(2,1)S(1)}, u32[]{:S(2)}, u32[]{:S(2)}) collective-permute-start(bf16[576,1152]{1,0:T(8,128)(2,1)S(1)} %slice.423), channel_id=1, source_target_pairs={{0,16},{4,20},{8,24},{12,28},{16,0},{20,4},{24,8},{28,12},{1,17},{... | collective-permute-start | bytes 3981320 | tf_op jit(solution)/shard_map/ppermute | solution.py:246
  231.1 34.8 %collective-permute-start.25 = (bf16[256,1152]{1,0:T(8,128)(2,1)}, bf16[256,1152]{1,0:T(8,128)(2,1)}, u32[]{:S(2)}, u32[]{:S(2)}) collective-permute-start(bf16[256,1152]{1,0:T(8,128)(2,1)} %add_convert_fusion.3), channel_id=1, source_target_pairs={{0,8},{4,12},{8,0},{12,4},{16,24},{20,28},{24,16},{28,20},{1,9},{5... | collective-permute-start | bytes 1769480 | tf_op jit(solution)/shard_map/ppermute | solution.py:246
  259.4 29.9 %collective-permute-start.28 = (bf16[576,1152]{1,0:T(8,128)(2,1)}, bf16[576,1152]{1,0:T(8,128)(2,1)}, u32[]{:S(2)}, u32[]{:S(2)}) collective-permute-start(bf16[576,1152]{1,0:T(8,128)(2,1)} %get-tuple-element.130), channel_id=1, source_target_pairs={{0,16},{4,20},{8,24},{12,28},{16,0},{20,4},{24,8},{28,12},{1,17},{... | collective-permute-start | bytes 3981320 | tf_op jit(solution)/shard_map/ppermute | solution.py:246
  267.4 23.9 %collective-permute-start.26 = (bf16[512,1152]{1,0:T(8,128)(2,1)S(1)}, bf16[512,1152]{1,0:T(8,128)(2,1)S(1)}, u32[]{:S(2)}, u32[]{:S(2)}) collective-permute-start(bf16[512,1152]{1,0:T(8,128)(2,1)S(1)} %pad_maximum_fusion.14), channel_id=1, source_target_pairs={{0,4},{4,0},{8,12},{12,8},{16,20},{20,16},{24,28},{28,24},{1,5},{5... | collective-permute-start | bytes 3538952 | tf_op jit(solution)/shard_map/ppermute | solution.py:246
  270.9 25.2 %collective-permute-start.32 = (bf16[512,1152]{1,0:T(8,128)(2,1)S(1)}, bf16[512,1152]{1,0:T(8,128)(2,1)S(1)}, u32[]{:S(2)}, u32[]{:S(2)}) collective-permute-start(bf16[512,1152]{1,0:T(8,128)(2,1)S(1)} %pad_maximum_fusion.15), channel_id=1, source_target_pairs={{0,4},{4,0},{8,12},{12,8},{16,20},{20,16},{24,28},{28,24},{1,5},{5... | collective-permute-start | bytes 3538952 | tf_op jit(solution)/shard_map/ppermute | solution.py:246
  303.1 37.9 %collective-permute-start.63 = (bf16[576,1152]{1,0:T(8,128)(2,1)}, bf16[576,1152]{1,0:T(8,128)(2,1)}, u32[]{:S(2)}, u32[]{:S(2)}) collective-permute-start(bf16[576,1152]{1,0:T(8,128)(2,1)} %broadcast_select_fusion), channel_id=1, source_target_pairs={{0,16},{4,20},{8,24},{12,28},{16,0},{20,4},{24,8},{28,12},{1,17},{... | collective-permute-start | bytes 3981320 | tf_op jit(solution)/shard_map/ppermute | solution.py:246
  312.1 23.0 %collective-permute-start.29 = (bf16[512,1152]{1,0:T(8,128)(2,1)}, bf16[512,1152]{1,0:T(8,128)(2,1)}, u32[]{:S(2)}, u32[]{:S(2)}) collective-permute-start(bf16[512,1152]{1,0:T(8,128)(2,1)} %slice.671), channel_id=1, source_target_pairs={{0,4},{4,0},{8,12},{12,8},{16,20},{20,16},{24,28},{28,24},{1,5},{5... | collective-permute-start | bytes 3538952 | tf_op jit(solution)/shard_map/ppermute | solution.py:246
  327.1 10.7 %collective-permute-start.33 = (bf16[512,1152]{1,0:T(8,128)(2,1)}, bf16[512,1152]{1,0:T(8,128)(2,1)}, u32[]{:S(2)}, u32[]{:S(2)}) collective-permute-start(bf16[512,1152]{1,0:T(8,128)(2,1)} %slice.670), channel_id=1, source_target_pairs={{0,4},{4,0},{8,12},{12,8},{16,20},{20,16},{24,28},{28,24},{1,5},{5... | collective-permute-start | bytes 3538952 | tf_op jit(solution)/shard_map/ppermute | solution.py:246
  334.1 30.5 %collective-permute-start.57 = (bf16[576,1152]{1,0:T(8,128)(2,1)}, bf16[576,1152]{1,0:T(8,128)(2,1)}, u32[]{:S(2)}, u32[]{:S(2)}) collective-permute-start(bf16[576,1152]{1,0:T(8,128)(2,1)} %broadcast_select_fusion.1), channel_id=1, source_target_pairs={{0,16},{4,20},{8,24},{12,28},{16,0},{20,4},{24,8},{28,12},{1,17},{... | collective-permute-start | bytes 3981320 | tf_op jit(solution)/shard_map/ppermute | solution.py:246
  337.5 86.2 %collective-permute-start.30 = (bf16[256,1152]{1,0:T(8,128)(2,1)S(1)}, bf16[256,1152]{1,0:T(8,128)(2,1)S(1)}, u32[]{:S(2)}, u32[]{:S(2)}) collective-permute-start(bf16[256,1152]{1,0:T(8,128)(2,1)S(1)} %slice.673), channel_id=1, source_target_pairs={{0,8},{4,12},{8,0},{12,4},{16,24},{20,28},{24,16},{28,20},{1,9},{5... | collective-permute-start | bytes 1769480 | tf_op jit(solution)/shard_map/ppermute | solution.py:246
  340.4 82.3 %collective-permute-start.34 = (bf16[256,1152]{1,0:T(8,128)(2,1)S(1)}, bf16[256,1152]{1,0:T(8,128)(2,1)S(1)}, u32[]{:S(2)}, u32[]{:S(2)}) collective-permute-start(bf16[256,1152]{1,0:T(8,128)(2,1)S(1)} %slice.672), channel_id=1, source_target_pairs={{0,8},{4,12},{8,0},{12,4},{16,24},{20,28},{24,16},{28,20},{1,9},{5... | collective-permute-start | bytes 1769480 | tf_op jit(solution)/shard_map/ppermute | solution.py:246
  343.3 24.1 %collective-permute-start.64 = (bf16[576,288]{1,0:T(8,128)(2,1)S(1)}, bf16[576,288]{1,0:T(8,128)(2,1)S(1)}, u32[]{:S(2)}, u32[]{:S(2)}) collective-permute-start(bf16[576,288]{1,0:T(8,128)(2,1)S(1)} %get-tuple-element.133), channel_id=1, source_target_pairs={{0,1},{1,2},{2,3},{3,0},{4,5},{5,6},{6,7},{7,4},{8,9},{9,10},{10,1... | collective-permute-start | bytes 995336 | tf_op jit(solution)/shard_map/ppermute | solution.py:261
  343.4 36.9 %collective-permute-start.65 = (bf16[576,288]{1,0:T(8,128)(2,1)S(1)}, bf16[576,288]{1,0:T(8,128)(2,1)S(1)}, u32[]{:S(2)}, u32[]{:S(2)}) collective-permute-start(bf16[576,288]{1,0:T(8,128)(2,1)S(1)} %get-tuple-element.134), channel_id=1, source_target_pairs={{0,2},{1,3},{2,0},{3,1},{4,6},{5,7},{6,4},{7,5},{8,10},{9,11},{10,... | collective-permute-start | bytes 995336 | tf_op jit(solution)/shard_map/ppermute | solution.py:261
  364.6 36.4 %collective-permute-start.66 = (bf16[576,288]{1,0:T(8,128)(2,1)S(1)}, bf16[576,288]{1,0:T(8,128)(2,1)S(1)}, u32[]{:S(2)}, u32[]{:S(2)}) collective-permute-start(bf16[576,288]{1,0:T(8,128)(2,1)S(1)} %select_select_fusion.4), channel_id=1, source_target_pairs={{0,3},{1,0},{2,1},{3,2},{4,7},{5,4},{6,5},{7,6},{8,11},{9,8},{10,9... | collective-permute-start | bytes 995336 | tf_op jit(solution)/shard_map/ppermute | solution.py:261
  367.4 41.3 %collective-permute-start.58 = (bf16[576,288]{1,0:T(8,128)(2,1)S(1)}, bf16[576,288]{1,0:T(8,128)(2,1)S(1)}, u32[]{:S(2)}, u32[]{:S(2)}) collective-permute-start(bf16[576,288]{1,0:T(8,128)(2,1)S(1)} %get-tuple-element.135), channel_id=1, source_target_pairs={{0,1},{1,2},{2,3},{3,0},{4,5},{5,6},{6,7},{7,4},{8,9},{9,10},{10,1... | collective-permute-start | bytes 995336 | tf_op jit(solution)/shard_map/ppermute | solution.py:261
  380.2 37.9 %collective-permute-start.59 = (bf16[576,288]{1,0:T(8,128)(2,1)S(1)}, bf16[576,288]{1,0:T(8,128)(2,1)S(1)}, u32[]{:S(2)}, u32[]{:S(2)}) collective-permute-start(bf16[576,288]{1,0:T(8,128)(2,1)S(1)} %get-tuple-element.136), channel_id=1, source_target_pairs={{0,2},{1,3},{2,0},{3,1},{4,6},{5,7},{6,4},{7,5},{8,10},{9,11},{10,... | collective-permute-start | bytes 995336 | tf_op jit(solution)/shard_map/ppermute | solution.py:261
  401.0 19.0 %collective-permute-start.60 = (bf16[576,288]{1,0:T(8,128)(2,1)S(1)}, bf16[576,288]{1,0:T(8,128)(2,1)S(1)}, u32[]{:S(2)}, u32[]{:S(2)}) collective-permute-start(bf16[576,288]{1,0:T(8,128)(2,1)S(1)} %select_select_fusion.7), channel_id=1, source_target_pairs={{0,3},{1,0},{2,1},{3,2},{4,7},{5,4},{6,5},{7,6},{8,11},{9,8},{10,9... | collective-permute-start | bytes 995336 | tf_op jit(solution)/shard_map/ppermute | solution.py:261
  408.7 18.6 %collective-permute-start.67 = (bf16[288,288]{1,0:T(8,128)(2,1)S(1)}, bf16[288,288]{1,0:T(8,128)(2,1)S(1)}, u32[]{:S(2)}, u32[]{:S(2)}) collective-permute-start(bf16[288,288]{1,0:T(8,128)(2,1)S(1)} %select_convert_fusion), channel_id=1, source_target_pairs={{0,8},{4,12},{8,0},{12,4},{16,24},{20,28},{24,16},{28,20},{1,9},{5... | collective-permute-start | bytes 497672 | tf_op jit(solution)/shard_map/ppermute | solution.py:246
  421.7 9.0 %collective-permute-start.61 = (bf16[288,288]{1,0:T(8,128)(2,1)}, bf16[288,288]{1,0:T(8,128)(2,1)S(1)}, u32[]{:S(2)}, u32[]{:S(2)}) collective-permute-start(bf16[288,288]{1,0:T(8,128)(2,1)} %select_convert_fusion.1), channel_id=1, source_target_pairs={{0,8},{4,12},{8,0},{12,4},{16,24},{20,28},{24,16},{28,20},{1,9},{5... | collective-permute-start | bytes 497672 | tf_op jit(solution)/shard_map/ppermute | solution.py:246
  426.6 6.0 collective-permute-start.35
  432.5 43.3 %collective-permute-start.62 = (bf16[144,576]{1,0:T(8,128)(2,1)}, bf16[144,576]{1,0:T(8,128)(2,1)}, u32[]{:S(2)}, u32[]{:S(2)}) collective-permute-start(bf16[144,576]{1,0:T(8,128)(2,1)} %get-tuple-element.110), channel_id=1, source_target_pairs={{0,4},{4,0},{8,12},{12,8},{16,20},{20,16},{24,28},{28,24},{1,5},{5... | collective-permute-start | bytes 497672 | tf_op jit(solution)/shard_map/ppermute | solution.py:246
  435.8 114.2 %reduce-scatter.4.cloned.1.call-start = ((), (), s32[]{:S(2)}) async-start(), calls=%async_computation.3 | async-start | bytes 5160960
  480.4 18.1 %collective-permute-start.48 = (f32[4,288]{1,0:T(4,128)}, f32[4,288]{1,0:T(4,128)}, u32[]{:S(2)}, u32[]{:S(2)}) collective-permute-start(f32[4,288]{1,0:T(4,128)} %get-tuple-element.182), channel_id=1, source_target_pairs={{0,1},{1,2},{2,3},{3,0},{4,5},{5,6},{6,7},{7,4},{8,9},{9,10},{10,1... | collective-permute-start | bytes 13832 | tf_op jit(solution)/shard_map/ppermute | solution.py:261
  480.4 18.1 %collective-permute-start.49 = (f32[4,288]{1,0:T(4,128)}, f32[4,288]{1,0:T(4,128)}, u32[]{:S(2)}, u32[]{:S(2)}) collective-permute-start(f32[4,288]{1,0:T(4,128)} %get-tuple-element.183), channel_id=1, source_target_pairs={{0,2},{1,3},{2,0},{3,1},{4,6},{5,7},{6,4},{7,5},{8,10},{9,11},{10,... | collective-permute-start | bytes 13832 | tf_op jit(solution)/shard_map/ppermute | solution.py:261
  484.3 14.3 %collective-permute-start.50 = (f32[4,288]{1,0:T(4,128)}, f32[4,288]{1,0:T(4,128)}, u32[]{:S(2)}, u32[]{:S(2)}) collective-permute-start(f32[4,288]{1,0:T(4,128)} %select_select_fusion.24), channel_id=1, source_target_pairs={{0,3},{1,0},{2,1},{3,2},{4,7},{5,4},{6,5},{7,6},{8,11},{9,8},{10,9... | collective-permute-start | bytes 13832 | tf_op jit(solution)/shard_map/ppermute | solution.py:261
  496.0 5.9 collective-permute-start.36
  501.0 13.6 %collective-permute-start.52 = (f32[4,576]{1,0:T(4,128)S(1)}, f32[4,576]{1,0:T(4,128)S(1)}, u32[]{:S(2)}, u32[]{:S(2)}) collective-permute-start(f32[4,576]{1,0:T(4,128)S(1)} %reshape.710), channel_id=1, source_target_pairs={{0,8},{4,12},{8,0},{12,4},{16,24},{20,28},{24,16},{28,20},{1,9},{5... | collective-permute-start | bytes 27656 | tf_op jit(solution)/shard_map/ppermute | solution.py:246
  505.1 15.5 %collective-permute-start.37 = (bf16[2,2,32,1152]{3,2,1,0:T(8,128)(2,1)}, bf16[2,2,32,1152]{3,2,1,0:T(8,128)(2,1)}, u32[]{:S(2)}, u32[]{:S(2)}) collective-permute-start(bf16[2,2,32,1152]{3,2,1,0:T(8,128)(2,1)} %get-tuple-element.148), channel_id=1, source_target_pairs={{1,0},{2,1},{3,2},{5,4},{6,5},{7,6},{9,8},{10,9},{11,10},{13,12},{... | collective-permute-start | bytes 884744 | tf_op jit(solution)/shard_map/ppermute | solution.py:496
  507.0 13.8 %collective-permute-start.38 = (bf16[2,2,32,1152]{3,2,1,0:T(8,128)(2,1)}, bf16[2,2,32,1152]{3,2,1,0:T(8,128)(2,1)}, u32[]{:S(2)}, u32[]{:S(2)}) collective-permute-start(bf16[2,2,32,1152]{3,2,1,0:T(8,128)(2,1)} %get-tuple-element.149), channel_id=1, source_target_pairs={{0,1},{1,2},{2,3},{4,5},{5,6},{6,7},{8,9},{9,10},{10,11},{12,13},{... | collective-permute-start | bytes 884744 | tf_op jit(solution)/shard_map/ppermute | solution.py:497
  515.2 10.3 %collective-permute-start.53 = (f32[8,576]{1,0:T(8,128)}, f32[8,576]{1,0:T(8,128)}, u32[]{:S(2)}, u32[]{:S(2)}) collective-permute-start(f32[8,576]{1,0:T(8,128)} %pad_maximum_fusion.29), channel_id=1, source_target_pairs={{0,16},{4,20},{8,24},{12,28},{16,0},{20,4},{24,8},{28,12},{1,17},{... | collective-permute-start | bytes 55304 | tf_op jit(solution)/shard_map/ppermute | solution.py:246
  517.8 10.4 %collective-permute-start.54 = (bf16[144,288]{1,0:T(8,128)(2,1)S(1)}, bf16[144,288]{1,0:T(8,128)(2,1)S(1)}, u32[]{:S(2)}, u32[]{:S(2)}) collective-permute-start(bf16[144,288]{1,0:T(8,128)(2,1)S(1)} %get-tuple-element.137), channel_id=1, source_target_pairs={{0,1},{1,2},{2,3},{3,0},{4,5},{5,6},{6,7},{7,4},{8,9},{9,10},{10,1... | collective-permute-start | bytes 248840 | tf_op jit(solution)/shard_map/ppermute | solution.py:261
  518.6 9.6 %collective-permute-start.55 = (bf16[144,288]{1,0:T(8,128)(2,1)S(1)}, bf16[144,288]{1,0:T(8,128)(2,1)S(1)}, u32[]{:S(2)}, u32[]{:S(2)}) collective-permute-start(bf16[144,288]{1,0:T(8,128)(2,1)S(1)} %get-tuple-element.138), channel_id=1, source_target_pairs={{0,2},{1,3},{2,0},{3,1},{4,6},{5,7},{6,4},{7,5},{8,10},{9,11},{10,... | collective-permute-start | bytes 248840 | tf_op jit(solution)/shard_map/ppermute | solution.py:261
  520.6 10.4 %collective-permute-start.56 = (bf16[144,288]{1,0:T(8,128)(2,1)S(1)}, bf16[144,288]{1,0:T(8,128)(2,1)S(1)}, u32[]{:S(2)}, u32[]{:S(2)}) collective-permute-start(bf16[144,288]{1,0:T(8,128)(2,1)S(1)} %get-tuple-element.139), channel_id=1, source_target_pairs={{0,3},{1,0},{2,1},{3,2},{4,7},{5,4},{6,5},{7,6},{8,11},{9,8},{10,9... | collective-permute-start | bytes 248840 | tf_op jit(solution)/shard_map/ppermute | solution.py:261
  523.8 3.6 collective-permute-start.39
  527.5 5.6 collective-permute-start.40
  539.9 23.5 %collective-permute-start.43 = (f32[15616]{0:T(1024)S(1)}, f32[15616]{0:T(1024)S(1)}, u32[]{:S(2)}, u32[]{:S(2)}) collective-permute-start(f32[15616]{0:T(1024)S(1)} %add.499), channel_id=1, source_target_pairs={{0,2},{1,3},{2,0},{3,1},{4,6},{5,7},{6,4},{7,5},{8,10},{9,11},{10,... | collective-permute-start | bytes 187400 | tf_op jit(solution)/shard_map/ppermute | solution.py:575
  558.7 9.2 %collective-permute-start.44 = (bf16[288,432]{0,1:T(8,128)(2,1)}, bf16[288,432]{0,1:T(8,128)(2,1)}, u32[]{:S(2)}, u32[]{:S(2)}) collective-permute-start(bf16[288,432]{0,1:T(8,128)(2,1)} %get-tuple-element.140), channel_id=1, source_target_pairs={{0,1},{1,2},{2,3},{3,0},{4,5},{5,6},{6,7},{7,4},{8,9},{9,10},{10,1... | collective-permute-start | bytes 746504 | tf_op jit(solution)/shard_map/ppermute | solution.py:261
  559.7 28.1 %collective-permute-start.45 = (bf16[288,432]{0,1:T(8,128)(2,1)}, bf16[288,432]{0,1:T(8,128)(2,1)}, u32[]{:S(2)}, u32[]{:S(2)}) collective-permute-start(bf16[288,432]{0,1:T(8,128)(2,1)} %get-tuple-element.142), channel_id=1, source_target_pairs={{0,2},{1,3},{2,0},{3,1},{4,6},{5,7},{6,4},{7,5},{8,10},{9,11},{10,... | collective-permute-start | bytes 746504 | tf_op jit(solution)/shard_map/ppermute | solution.py:261
  561.3 29.9 %collective-permute-start.46 = (bf16[288,432]{0,1:T(8,128)(2,1)}, bf16[288,432]{0,1:T(8,128)(2,1)}, u32[]{:S(2)}, u32[]{:S(2)}) collective-permute-start(bf16[288,432]{0,1:T(8,128)(2,1)} %get-tuple-element.141), channel_id=1, source_target_pairs={{0,3},{1,0},{2,1},{3,2},{4,7},{5,4},{6,5},{7,6},{8,11},{9,8},{10,9... | collective-permute-start | bytes 746504 | tf_op jit(solution)/shard_map/ppermute | solution.py:261
  (98 other events, 970.5 us)
Sparse Core Ops, SparseCore 0:
  59.4 52.6 all-gather.2
  189.0 27.5 all-gather.4
  436.0 57.7 all-reduce.9
  497.1 52.8 reduce-scatter.3

commit v2 on v1

v2 whole, which is shorter than its diff:
```python
import functools
import math

import jax
import jax.numpy as jnp
from jax import lax
from jax.experimental import pallas as pl
from jax.experimental.layout import Layout, with_layout_constraint
from jax.experimental.pallas import tpu as pltpu
from jax.sharding import PartitionSpec as P

HALO = 2
LANES = 128

norm_eps = 1e-06
masked_score = -1000000000.0

f32 = jnp.float32
bf16 = jnp.bfloat16

NN = (((1,), (0,)), ((), ()))
NT = (((1,), (1,)), ((), ()))
TN = (((0,), (0,)), ((), ()))


def dot(left, right, dims=NN):
    return lax.dot_general(left, right, dims, preferred_element_type=f32)


def row_major(value):
    return with_layout_constraint(value, Layout(major_to_minor=tuple(range(value.ndim))))


def normalize(values):
    centre = values - jnp.mean(values, -1, keepdims=True)
    spread = jnp.mean(centre * centre, -1, keepdims=True)
    inverse = lax.rsqrt(spread + norm_eps)
    return (centre * inverse, inverse)


def norm_back(grad_hat, normal_part, inverse):
    first_mean = jnp.mean(grad_hat, -1, keepdims=True)
    second_mean = jnp.mean(grad_hat * normal_part, -1, keepdims=True)
    return inverse * (grad_hat - first_mean - normal_part * second_mean)


def gelu_tanh(values):
    return jax.nn.gelu(values, approximate=True)


def window(head, head_dim, width):
    first, last = head * head_dim, (head + 1) * head_dim
    start = first // LANES * LANES
    stop = min(-(-last // LANES) * LANES, width)
    return first, last, start, stop


def lane_mask(first, last, start, stop, kind):
    lane = lax.broadcasted_iota(jnp.int32, (1, stop - start), 1) + start
    return jnp.where((lane >= first) & (lane < last), 1.0, 0.0).astype(kind)


def add_tiles(tiles, values, start, stop):
    for at in range(start, stop, LANES):
        part = values[:, at - start : min(at + LANES, stop) - start]
        tiles[at] = part if at not in tiles else tiles[at] + part


def store_tiles(ref, tiles, scale=None, rows=slice(None), base=0):
    for at, part in tiles.items():
        if scale is not None:
            part = part * scale
        ref[0, rows, base + at : base + at + part.shape[1]] = part.astype(ref.dtype)


def attend_kernel(heads, scale, edge, qkv_ref, bias_ref, allow_ref, o_ref, p_ref):
    half = o_ref.shape[-1]
    cells = o_ref.shape[1]
    allowed = allow_ref[0] > 0.5
    queries = qkv_ref[0, edge : edge + cells, :half]
    key = qkv_ref[0, :, half : 2 * half]
    value = qkv_ref[0, :, 2 * half :]
    tiles = {}
    for head in range(heads):
        span = window(head, half // heads, half)
        start, stop = span[2:]
        query = queries[:, start:stop] * lane_mask(*span, bf16)
        scores = dot(query, key[:, start:stop], NT) * scale + bias_ref[head].astype(f32)
        scores = jnp.where(allowed, scores, masked_score)
        expo = jnp.exp(scores - jnp.max(scores, -1, keepdims=True))
        prob = (expo / jnp.sum(expo, -1, keepdims=True)).astype(bf16)
        p_ref[0, head] = prob
        out = dot(prob, value[:, start:stop]) * lane_mask(*span, f32)
        add_tiles(tiles, out, start, stop)
    store_tiles(o_ref, tiles)


def attend_back_kernel(heads, scale, edge, cols, qkv_ref, p_ref, do_ref, d_ref, g_ref, sum_ref):
    cells, half = do_ref.shape[1:]
    rows = cells // cols
    middle = slice(edge, edge + cells)
    step = pl.program_id(0)

    @pl.when(step == 0)
    def _():
        sum_ref[...] = jnp.zeros_like(sum_ref)

    queries = qkv_ref[0, middle, :half]
    key = qkv_ref[0, :, half : 2 * half]
    value = qkv_ref[0, :, 2 * half :]
    dq_tiles, dk_tiles, dv_tiles = {}, {}, {}
    for head in range(heads):
        span = window(head, half // heads, half)
        start, stop = span[2:]
        mask = lane_mask(*span, bf16)
        query = queries[:, start:stop] * mask
        grad_out = do_ref[0, :, start:stop] * mask
        prob = p_ref[0, head]
        full = prob.astype(f32)
        weighted = full * dot(grad_out, value[:, start:stop], NT)
        grad_score = (weighted - full * jnp.sum(weighted, -1, keepdims=True)).astype(bf16)
        sum_ref[head] += grad_score.astype(f32)
        dq = dot(grad_score, key[:, start:stop]) * lane_mask(*span, f32)
        add_tiles(dq_tiles, dq, start, stop)
        add_tiles(dk_tiles, dot(grad_score, query, TN), start, stop)
        add_tiles(dv_tiles, dot(prob, grad_out, TN), start, stop)
    d_ref[0, :edge, :half] = jnp.zeros((edge, half), bf16)
    d_ref[0, edge + cells :, :half] = jnp.zeros((edge, half), bf16)
    store_tiles(d_ref, dq_tiles, scale, middle)
    store_tiles(d_ref, dk_tiles, scale, base=half)
    store_tiles(d_ref, dv_tiles, base=2 * half)

    @pl.when(step == pl.num_programs(0) - 1)
    def _():
        for head in range(heads):
            total = sum_ref[head, :cols]
            for row in range(1, rows):
                part = sum_ref[head, row * cols : (row + 1) * cols]
                total += pltpu.roll(part, part.shape[1] - row * cols, 1)
            g_ref[head] = total


def per_image(*dims):
    return pl.BlockSpec((1,) + dims, lambda i: (i,) + (0,) * len(dims))


def whole(*dims):
    return pl.BlockSpec(dims, lambda i: (0,) * len(dims))


def attend(qkv, bias, allowed, scale):
    images, keys, width = qkv.shape
    heads, cells, _ = bias.shape
    half = width // 3
    return pl.pallas_call(
        functools.partial(attend_kernel, heads, scale, (keys - cells) // 2),
        grid=(images,),
        in_specs=[per_image(keys, width), whole(heads, cells, keys), per_image(cells, keys)],
        out_specs=[per_image(cells, half), per_image(heads, cells, keys)],
        out_shape=[
            jax.ShapeDtypeStruct((images, cells, half), bf16),
            jax.ShapeDtypeStruct((images, heads, cells, keys), bf16),
        ],
        compiler_params=pltpu.CompilerParams(vmem_limit_bytes=32 << 20),
        cost_estimate=pl.CostEstimate(
            flops=4 * images * heads * cells * keys * 256,
            bytes_accessed=4 * images * heads * cells * keys,
            transcendentals=images * heads * cells * keys,
        ),
        name="attend",
    )(qkv, bias, allowed)


def attend_back(qkv, prob, grad_out, scale, cols):
    images, keys, width = qkv.shape
    heads = prob.shape[1]
    cells, half = grad_out.shape[1:]
    return pl.pallas_call(
        functools.partial(attend_back_kernel, heads, scale, (keys - cells) // 2, cols),
        grid=(images,),
        in_specs=[per_image(keys, width), per_image(heads, cells, keys), per_image(cells, half)],
        out_specs=[per_image(keys, width), whole(heads, cols, keys)],
        out_shape=[
            jax.ShapeDtypeStruct((images, keys, width), bf16),
            jax.ShapeDtypeStruct((heads, cols, keys), f32),
        ],
        scratch_shapes=[pltpu.VMEM((heads, cells, keys), f32)],
        compiler_params=pltpu.CompilerParams(vmem_limit_bytes=32 << 20),
        cost_estimate=pl.CostEstimate(
            flops=8 * images * heads * cells * keys * 256,
            bytes_accessed=4 * images * heads * cells * keys,
            transcendentals=0,
        ),
        name="attend_back",
    )(qkv, prob, grad_out)


def on_blocks(kernel, spot, values, shapes, name):
    block = pl.BlockSpec(memory_space=pltpu.VMEM)
    return pl.pallas_call(
        kernel,
        in_specs=[pl.BlockSpec(memory_space=pltpu.SMEM)] + [block] * len(values),
        out_specs=[block] * len(shapes),
        out_shape=[jax.ShapeDtypeStruct(shape, kind) for shape, kind in shapes],
        compiler_params=pltpu.CompilerParams(vmem_limit_bytes=32 << 20),
        name=name,
    )(spot, *values)


def for_each(value, count, body):
    for at in range(count):
        pl.when(value == at)(functools.partial(body, at))


def source_row(spot, group, size, by_core):
    side = jnp.bitwise_xor(spot[1], group >> 1)
    core = jnp.bitwise_xor(spot[2], group & 1) if by_core else group & 1
    return pl.multiple_of((side * 2 + core) * size, 16)


def split_core_kernel(spot, w_ref, keep_ref, send_ref):
    half = keep_ref.shape[1]

    def body(core):
        keep_ref[...] = w_ref[:, core * half : (core + 1) * half]
        send_ref[...] = w_ref[:, (1 - core) * half : (2 - core) * half]

    for_each(spot[2], 2, body)


def split_side_kernel(spot, own_ref, got_ref, fc2_ref, keep1_ref, keep2_ref, send_ref):
    rows, wide = own_ref.shape
    part = wide // 2

    def body(side):
        for at, ref in enumerate((own_ref, got_ref)):
            lanes = slice(at * part, (at + 1) * part)
            keep1_ref[:, lanes] = ref[:, side * part : (side + 1) * part]
            send_ref[:, lanes] = ref[:, (1 - side) * part : (2 - side) * part]
        for at in range(2):
            first = (side * 2 + at) * rows
            other = ((1 - side) * 2 + at) * rows
            keep2_ref[:, at * part : (at + 1) * part] = fc2_ref[first : first + rows]
            send_ref[:, wide + at * part : wide + (at + 1) * part] = fc2_ref[other : other + rows]

    for_each(spot[1], 2, body)


def fill_lanes(ref, first):
    if first < ref.shape[-1]:
        ref[:, first:] = jnp.zeros((ref.shape[0], ref.shape[-1] - first), ref.dtype)


def join_side_kernel(spot, out_ref, keep1_ref, keep2_ref, got_ref, one_ref, two_ref):
    part = out_ref.shape[1]
    wide = keep1_ref.shape[1]
    one_ref[:, :part] = out_ref[...]
    one_ref[:, part : part + wide] = keep1_ref[...]
    one_ref[:, part + wide : part + 2 * wide] = got_ref[:, :wide]
    fill_lanes(one_ref, part + 2 * wide)
    two_ref[:, :wide] = keep2_ref[...]
    two_ref[:, wide:] = got_ref[:, wide:]


def unpack_kernel(by_core, lead, sides, spot, pieces, *outs):
    rows = pieces.shape[1] // sides
    part = outs[-1].shape[1] // 4
    for block in range(4):
        lanes = slice(block * part, (block + 1) * part)
        if lead:
            outs[0][:, lanes] = pieces[block, :, :part]
        for side in range(sides):
            base = jnp.bitwise_xor(spot[3], side) * 4 * rows if sides > 1 else 0
            for group in range(4):
                first = (group + lead) * part
                row = base + source_row(spot, group, rows, by_core)
                outs[-1][pl.ds(pl.multiple_of(row, 16), rows), lanes] = pieces[
                    block, side * rows : (side + 1) * rows, first : first + part
                ]


def pack_kernel(by_core, spot, grad_ref, got_ref, out):
    rows = out.shape[1]
    part = grad_ref.shape[1] // 4
    base = spot[3] * got_ref.shape[0]
    for block in range(4):
        lanes = slice(block * part, (block + 1) * part)
        for group in range(4):
            row = source_row(spot, group, rows, by_core)
            own = grad_ref[pl.ds(pl.multiple_of(base + row, 16), rows), lanes]
            total = own.astype(f32) + got_ref[pl.ds(row, rows), lanes].astype(f32)
            out[block, :, group * part : (group + 1) * part] = total.astype(out.dtype)


def split_sums_kernel(spot, one, two, keep1_ref, keep2_ref, send_ref):
    wide = keep1_ref.shape[1]
    keep1_ref[...] = one[:, :wide]
    keep2_ref[...] = two[:, :wide]
    send_ref[:, :wide] = one[:, wide:]
    send_ref[:, wide:] = two[:, wide:]


def turn_core_kernel(spot, keep1_ref, got_ref, send_ref):
    part = send_ref.shape[1] // 2
    send_ref[:, :part] = keep1_ref[:, part:]
    send_ref[:, part:] = got_ref[:, part : 2 * part]


def finish_kernel(spot, keep1_ref, keep2_ref, side_ref, core_ref, fc1_ref, fc2_ref):
    rows, part = fc1_ref.shape[0], fc2_ref.shape[1]

    def body(place):
        core, side = place // 2, place % 2
        parts = {
            (core, side): keep1_ref[:, :part],
            (core, 1 - side): side_ref[:, :part],
            (1 - core, side): core_ref[:, :part],
            (1 - core, 1 - side): core_ref[:, part:],
        }
        for (c, x), value in parts.items():
            fc1_ref[:, (2 * c + x) * part : (2 * c + x + 1) * part] = value.astype(f32)
        for at in range(2):
            lanes = slice(at * part, (at + 1) * part)
            first, other = (side * 2 + at) * rows, ((1 - side) * 2 + at) * rows
            fc2_ref[first : first + rows] = keep2_ref[:, lanes].astype(f32)
            fc2_ref[other : other + rows] = side_ref[:, (2 + at) * part : (3 + at) * part].astype(f32)

    for_each(spot[2] * 2 + spot[1], 4, body)


def qkv_blocks(tile, rows, count):
    for block in range(4):
        for at in range(count):
            for core in range(2):
                yield (
                    block,
                    core,
                    slice((2 * at + core) * rows, (2 * at + core + 1) * rows),
                    slice((block * count + at) * rows, (block * count + at + 1) * rows),
                )


def unpack_qkv_kernel(spot, *refs):
    pieces, kept = refs[:4], refs[4:]
    rows, wide = pieces[0].shape

    def body(place):
        tile, mine = place // 2, place % 2
        for block, core, there, here in qkv_blocks(tile, rows, wide // (2 * rows)):
            kept[core != mine][:, here] = pieces[(tile - block) % 4][:, there]

    for_each(spot[0] * 2 + spot[2], 8, body)


def pack_qkv_kernel(spot, own_ref, got_ref, last_ref, *outs):
    rows, wide = outs[0].shape
    part = last_ref.shape[1] // 4
    wide = wide - part

    def body(place):
        tile, mine = place // 2, place % 2
        for block, core, there, here in qkv_blocks(tile, rows, wide // (2 * rows)):
            source = own_ref if core == mine else got_ref
            outs[(block - tile) % 4][:, there] = source[:, here]
        for block in range(4):
            lanes = slice(block * part, (block + 1) * part)
            outs[(block - tile) % 4][:, wide:] = last_ref[:, lanes]

    for_each(spot[0] * 2 + spot[2], 8, body)


def place_kernel(count, rows_ref, *refs):
    ins, out = refs[:count], refs[count]
    for at, ref in enumerate(ins):
        out[pl.ds(pl.multiple_of(rows_ref[at], 16), ref.shape[0])] = ref[...]


def place_rows(pieces, rows, name):
    height = sum(piece.shape[0] for piece in pieces)
    shape = (height, pieces[0].shape[1]), pieces[0].dtype
    kernel = functools.partial(place_kernel, len(pieces))
    return on_blocks(kernel, jnp.stack(rows).astype(jnp.int32), pieces, [shape], name)[0]


def shards(
    tokens,
    cotangent,
    heights,
    widths,
    timesteps,
    rel_index,
    ln1_gain,
    ln1_bias,
    w_qkv,
    w_time,
    rel_table,
    w_out,
    out_bias,
    ln2_gain,
    ln2_bias,
    w_fc1,
    fc1_bias,
    w_fc2,
    fc2_bias,
):
    here, rows_here, cols, width = tokens.shape
    cells = rows_here * cols
    slots = here * cells
    key_rows = rows_here + 2 * HALO
    keys = key_rows * cols
    head_count = rel_table.shape[1]
    head_dim = width // head_count
    scale = head_dim ** (-0.5)
    image_devices = lax.axis_size("images")
    tiles = lax.axis_size("rows")
    low = image_devices // 8
    chunk = width // 8
    quarter = width // 4
    ff_part = fc1_bias.shape[0] // 16
    place = lax.axis_index("images")
    tile = lax.axis_index("rows")
    bits = {"c": low, "x": 2 * low, "y": 4 * low}
    at_c, at_x, at_y = (place // bits[name] % 2 for name in "cxy")


    def partner(value, bit):
        route = [(d, d ^ bit) for d in range(image_devices)]
        return lax.ppermute(value, "images", route)

    def swap(value, name):
        return partner(value, bits[name])

    def pick(at, pair):
        return jnp.where(at == 0, pair[0], pair[1]), jnp.where(at == 0, pair[1], pair[0])

    def after(value, *others):
        return lax.optimization_barrier((value,) + others)[0]

    def all_after(values, *others):
        return list(lax.optimization_barrier(tuple(values) + others))[: len(values)]

    def with_partner(value, name):
        return jnp.concatenate([value, swap(value, name)], 0)

    def shift(value, step):
        return lax.ppermute(value, "rows", [(d, (d + step) % tiles) for d in range(tiles)])

    def tiles_all(value):
        return lax.all_gather(value, "rows", axis=0)

    def tiles_sum(value):
        return lax.psum_scatter(value, "rows", scatter_dimension=0)

    def shifts(value):
        return [shift(value, step) for step in range(1, tiles)]

    def tile_gather(value):
        for bit in (1, 2):
            other = lax.ppermute(value, "rows", [(d, d ^ bit) for d in range(tiles)])
            value = jnp.concatenate(pick(tile // bit % 2, (value, other)), 1)
        return value

    def tile_scatter(value):
        size = value.shape[1] // tiles
        blocks = [value[:, at * size : (at + 1) * size] for at in range(tiles)]
        total = lax.select_n(tile, *blocks).astype(f32)
        for step in range(1, tiles):
            sent = lax.select_n((tile + step) % tiles, *blocks)
            total = total + shift(sent, step).astype(f32)
        return total

    low_groups = [[g * low + d for d in range(low)] for g in range(8)]
    def low_gather(value):
        if low == 1:
            return value
        return lax.all_gather(value, "images", axis=0, tiled=True, axis_index_groups=low_groups)

    def low_scatter(value):
        if low == 1:
            return value
        return lax.psum_scatter(
            value, "images", scatter_dimension=0, tiled=True, axis_index_groups=low_groups
        )

    def part_of(value, at):
        return lax.dynamic_index_in_dim(value, at, 0, keepdims=False)


    slot_row = tile * rows_here + jnp.arange(cells) // cols
    slot_col = jnp.arange(cells) % cols
    valid = (slot_row[None, :] < heights[:, None]) & (slot_col[None, :] < widths[:, None])
    valid_mask = valid.reshape(slots, 1).astype(f32)
    grad_out = cotangent.astype(f32).reshape(slots, width) * valid_mask
    grad_mlp_own = grad_out.astype(bf16)


    gain_one, shift_one = ln1_gain.astype(f32), ln1_bias.astype(f32)
    gain_two, shift_two = ln2_gain.astype(f32), ln2_bias.astype(f32)
    flat_tokens = tokens.astype(f32).reshape(slots, width)
    normal_one, inverse_one = normalize(flat_tokens)
    normed = (normal_one * gain_one + shift_one).astype(bf16).reshape(tokens.shape)

    down = [(d, d + 1) for d in range(tiles - 1)]
    up = [(d + 1, d) for d in range(tiles - 1)]
    images = 2 * here


    spot = jnp.stack([tile, at_x, at_c, at_y]).astype(jnp.int32)
    w_qkv, w_out, w_fc1, w_fc2 = (low_gather(w) for w in (w_qkv, w_out, w_fc1, w_fc2))
    wide = 2 * ff_part
    padded = -(-(ff_part + 2 * wide) // LANES) * LANES

    def matrices(*dims):
        return [(dim, bf16) for dim in dims]

    qkv_parts = [w_qkv] + shifts(w_qkv)

    fc1_keep, fc1_send = on_blocks(
        split_core_kernel, spot, [w_fc1], matrices((chunk, wide), (chunk, wide)), "split_core"
    )
    fc1_got = swap(fc1_send, "c")
    keep1, keep2, send = on_blocks(
        split_side_kernel,
        spot,
        [fc1_keep, fc1_got, w_fc2],
        matrices((chunk, wide), (chunk, wide), (chunk, 2 * wide)),
        "split_side",
    )
    got = swap(send, "x")
    one, two = on_blocks(
        join_side_kernel,
        spot,
        [w_out, keep1, keep2, got],
        matrices((chunk, padded), (chunk, 2 * wide)),
        "join_side",
    )
    two = with_partner(two, "y")
    one_parts = tiles_all(one)
    two_parts = tiles_all(two)


    orders = [bits["c"], bits["x"], bits["y"]]
    orders += [1 << b for b in range(low.bit_length() - 1)]
    facts = with_partner(jnp.stack([timesteps, heights, widths], 1), "c")
    heights_all, widths_all = facts[:, 1], facts[:, 2]
    steps_all = facts[:, 0]
    for bit in orders[1:]:
        steps_all = jnp.concatenate([steps_all, partner(steps_all, bit)], 0)
    time_rows = w_time.shape[0]
    half_width = width // 2
    feature = place * time_rows + jnp.arange(time_rows)
    exponent = (feature % half_width).astype(f32)
    frequency = jnp.exp(-math.log(10000.0) * exponent / half_width)
    phases = steps_all.astype(f32)[:, None] * frequency[None, :]
    timing = jnp.where(feature[None, :] < half_width, jnp.cos(phases), jnp.sin(phases)).astype(bf16)
    time_part = dot(timing, after(w_time, *qkv_parts[1:]))
    for bit in orders[:0:-1]:
        half = time_part.shape[0] // 2
        time_part = time_part[:half] + partner(time_part[half:], bit)
    turned = jnp.concatenate([time_part[here:], time_part[:here]], 0)
    time_part = time_part + swap(turned, "c")
    qkv_keep, qkv_send = on_blocks(
        unpack_qkv_kernel,
        spot,
        qkv_parts,
        matrices((chunk, 12 * chunk), (chunk, 12 * chunk)),
        "unpack_qkv",
    )
    edges = [normed[:, rows_here - HALO :], normed[:, :HALO]]
    edges = all_after(edges, qkv_keep)
    above = lax.ppermute(edges[0], "rows", down)
    below = lax.ppermute(edges[1], "rows", up)
    normed_ext = jnp.concatenate([above, normed, below], 1)
    normed_all = with_partner(normed_ext, "c").reshape(images * keys, width)

    qkv_pair = jnp.concatenate([qkv_keep, swap(qkv_send, "c")], 0)
    qkv_pair = after(qkv_pair, time_part, two)
    qkv_x, qkv_y = swap(qkv_pair, "x"), swap(qkv_pair, "y")
    qkv_x, qkv_y = all_after([qkv_x, qkv_y], normed_all)
    qkv_far = [swap(qkv_x[:chunk], "y"), swap(qkv_y[chunk:], "x")]
    qkv_far = all_after(qkv_far, one_parts)
    spots = at_y * 4 + at_x * 2 + at_c
    qkv_full = place_rows(
        [qkv_pair[:chunk], qkv_pair[chunk:], qkv_x[:chunk], qkv_x[chunk:]]
        + [qkv_y[:chunk], qkv_y[chunk:]]
        + qkv_far,
        [jnp.bitwise_xor(spots, step) * chunk for step in range(8)],
        "place_qkv",
    )

    out_rows, fc1_rows = on_blocks(
        functools.partial(unpack_kernel, True, 1, 1),
        spot,
        [after(one_parts, qkv_full)],
        matrices((chunk, width), (4 * chunk, 4 * ff_part)),
        "unpack_fc1",
    )
    out_x, out_y = swap(out_rows, "x"), swap(out_rows, "y")
    out_xy = swap(out_y, "x")
    places = at_y * 2 + at_x
    out_full = place_rows(
        [out_rows, out_x, out_y, out_xy],
        [jnp.bitwise_xor(places, step) * chunk for step in range(4)],
        "place_out",
    )

    fc1_rows = after(fc1_rows, out_y)
    fc1_got = swap(fc1_rows, "y")
    fc1_full = place_rows(
        [fc1_rows, fc1_got], [at_y * 4 * chunk, (1 - at_y) * 4 * chunk], "place_fc1"
    )
    grad_mlp_x = with_partner(after(grad_mlp_own, qkv_full), "x")
    grad_mlp = with_partner(grad_mlp_x, "c")

    time_pairs = tile_gather(time_part).reshape(images, -1, 2, chunk)
    time_mine = pick(at_c, (time_pairs[:, :, 0], time_pairs[:, :, 1]))[0].reshape(images, width)
    half = width // 2
    time_all = jnp.concatenate(
        [time_mine[:, :half], jnp.zeros((images, half), f32), time_mine[:, half:]], 1
    )


    query_row = jnp.arange(cells) // cols
    query_col = jnp.arange(cells) % cols
    key_row = jnp.arange(keys) // cols - HALO
    key_col = jnp.arange(keys) % cols
    near = jnp.abs(key_row[None, :] - query_row[:, None]) <= HALO
    itself = jnp.arange(keys)[None, :] == jnp.arange(cells)[:, None] + HALO * cols
    global_key = tile * rows_here + key_row
    key_ok = (
        (global_key[None, :] >= 0)
        & (global_key[None, :] < heights_all[:, None])
        & (key_col[None, :] < widths_all[:, None])
    )
    allowed = (key_ok[:, None, :] & near[None] | itself[None]).astype(f32)
    heads = head_count // 2
    gaps = 2 * HALO + 1
    spans = 2 * cols - 1
    exact = lax.Precision.HIGHEST
    bucket_hits = (
        rel_index.reshape(-1)[:, None] == jnp.arange(rel_table.shape[0])[None, :]
    ).astype(f32)
    table_pairs = rel_table.astype(f32).reshape(rel_table.shape[0], -1, 2, 2)
    table_mine = pick(at_c, (table_pairs[:, :, 0], table_pairs[:, :, 1]))[0].reshape(-1, heads)
    offset_values = jnp.dot(bucket_hits, table_mine, precision=exact).T
    col_step = jnp.arange(cols)[None, :] - jnp.arange(cols)[:, None] + cols - 1
    step_hits = (jnp.arange(spans)[:, None] == col_step.reshape(1, -1)).astype(f32)
    spread = jnp.dot(offset_values.reshape(heads * gaps, spans), step_hits, precision=exact)
    strip = spread.reshape(heads, gaps, cols, cols).transpose(0, 2, 1, 3)
    strip = strip.reshape(heads, cols, gaps * cols).astype(bf16)
    bias = jnp.concatenate(
        [
            jnp.pad(strip, ((0, 0), (0, 0), (r * cols, keys - (r + gaps) * cols)))
            for r in range(rows_here)
        ],
        1,
    )


    normed_here = after(normed_all, out_rows)
    qkv = (
        dot(normed_here, qkv_full).reshape(images, keys, 3 * half) + time_all[:, None]
    ).astype(bf16)
    attended, prob = attend(after(qkv, out_x, out_y), bias, allowed, scale)
    attended = after(attended.reshape(images * cells, half), grad_mlp_x)

    def core_sum(left, right, dims=NN):
        size = left.shape[0] // 2
        sent = swap(dot(left[size:], right, dims).astype(bf16), "c")
        return dot(left[:size], right, dims) + sent.astype(f32)

    def quad_sum(left, right, dims=NN):
        part = core_sum(left, right, dims)
        size = part.shape[0] // 2
        return part[:size] + swap(part[size:].astype(bf16), "x").astype(f32)

    middle = flat_tokens + core_sum(attended, out_full) + out_bias.astype(f32)
    normal_two, inverse_two = normalize(middle)
    second = with_partner((normal_two * gain_two + shift_two).astype(bf16), "x")
    second = with_partner(after(second, fc1_full), "c")


    member = at_c * 2 + at_x
    bias_parts = fc1_bias.astype(f32).reshape(tiles, 4, ff_part)
    bias_mine = lax.dynamic_index_in_dim(bias_parts, member, 1, keepdims=False).reshape(-1)
    hidden_pre = dot(second, fc1_full) + bias_mine
    hidden_act, gelu_pull = jax.vjp(gelu_tanh, hidden_pre)
    hidden = hidden_act.astype(bf16)
    (fc2_full,) = on_blocks(
        functools.partial(unpack_kernel, False, 0, 2),
        spot,
        [after(two_parts, hidden)],
        matrices((8 * chunk, width)),
        "unpack_fc2",
    )
    grad_fc2 = dot(hidden, grad_mlp, TN).astype(bf16)
    grad_pre = gelu_pull(dot(after(grad_mlp, grad_fc2), fc2_full, NT))[0].astype(bf16)
    grad_second = quad_sum(grad_pre, fc1_full, NT)
    grad_fc1 = dot(second, grad_pre, TN).astype(bf16)
    grad_fc2_bias = jnp.sum(grad_mlp_own, 0, dtype=f32)
    grad_fc1_bias = jnp.sum(grad_pre, 0, dtype=f32)

    grad_gain_two = jnp.sum(grad_second * normal_two, 0)
    grad_shift_two = jnp.sum(grad_second, 0)
    grad_middle = grad_out + norm_back(grad_second * gain_two, normal_two, inverse_two)
    grad_branch_own = grad_middle.astype(bf16)
    grad_out_bias = jnp.sum(grad_branch_own, 0, dtype=f32)
    grad_branch = with_partner(grad_branch_own, "c")


    def add_bf16(one, two):
        return (one.astype(f32) + two.astype(f32)).astype(bf16)

    def sides(grad):
        return grad.reshape((2, -1) + grad.shape[1:])

    fc2_got = swap(part_of(sides(grad_fc2), 1 - at_y), "y")
    fc1_got = swap(part_of(sides(grad_fc1), 1 - at_y), "y")
    grad_att = dot(grad_branch, out_full, NT).astype(bf16)
    grad_out_weight = dot(attended, grad_branch, TN).astype(bf16)
    out_sides = sides(grad_out_weight)
    out_sent = part_of(out_sides, 1 - at_y)
    (two_packed,) = on_blocks(
        functools.partial(pack_kernel, False),
        spot,
        [grad_fc2, after(fc2_got, grad_att)],
        matrices((tiles, chunk, 2 * wide)),
        "pack_fc2",
    )
    grad_att = after(grad_att, out_sent, two_packed).reshape(images, cells, half)
    two_sum = tiles_sum(two_packed)
    out_got = swap(out_sent, "y")

    grad_proj, grad_strip = attend_back(qkv, prob, grad_att, scale, cols)
    flat_proj = grad_proj.reshape(images * keys, 3 * half)
    grad_qkv = row_major(dot(normed_all, flat_proj, TN).astype(bf16))
    blocks = grad_qkv.reshape(2, 2, 2, chunk, 12 * chunk)

    def blocks_at(y, x, core):
        first = [0 if at is None else at for at in (y, x, core)] + [0, 0]
        size = [2 if at is None else 1 for at in (y, x, core)] + list(blocks.shape[3:])
        return lax.dynamic_slice(blocks, first, size).reshape(-1, chunk, 12 * chunk)

    own_sent = blocks_at(1 - at_y, None, at_c)
    other_sent = blocks_at(None, 1 - at_x, 1 - at_c)
    own_got, other_got = swap(own_sent, "y"), swap(other_sent, "x")
    out_mine = sides(add_bf16(part_of(out_sides, at_y), after(out_got, grad_qkv)))
    out_got = swap(part_of(out_mine, 1 - at_x), "x")
    out_mine = add_bf16(part_of(out_mine, at_x), out_got)

    (one_packed,) = on_blocks(
        functools.partial(pack_kernel, True),
        spot,
        [grad_fc1, after(fc1_got, grad_qkv)],
        matrices((tiles, chunk, 2 * wide)),
        "pack_fc1",
    )
    one_sum = tiles_sum(one_packed)
    flat_proj = after(flat_proj, own_sent, other_sent, two_sum, one_packed)
    grad_ext = core_sum(flat_proj, qkv_full, NT).reshape(here, key_rows, cols, width)
    mlp_out = quad_sum(after(hidden, own_sent, other_sent), fc2_full) + fc2_bias.astype(f32)
    mixed = (valid_mask * (middle + mlp_out)).reshape(tokens.shape).astype(bf16)

    from_below = lax.ppermute(grad_ext[:, :HALO].astype(bf16), "rows", up).astype(f32)
    from_above = lax.ppermute(grad_ext[:, HALO + rows_here :].astype(bf16), "rows", down)
    from_above = from_above.astype(f32)
    rest = ((0, 0), (rows_here - HALO, 0), (0, 0), (0, 0))
    grad_normed = (
        grad_ext[:, HALO : HALO + rows_here]
        + jnp.pad(from_below, rest)
        + jnp.pad(from_above, (rest[0], rest[1][::-1], rest[2], rest[3]))
    ).reshape(slots, width)
    grad_gain_one = jnp.sum(grad_normed * normal_one, 0)
    grad_shift_one = jnp.sum(grad_normed, 0)
    grad_input = grad_middle + norm_back(grad_normed * gain_one, normal_one, inverse_one)
    grad_tokens = grad_input.reshape(tokens.shape).astype(bf16)


    grad_strip = grad_strip[:, :, : gaps * cols].reshape(heads, cols, gaps, cols)
    grad_strip = grad_strip.transpose(0, 2, 1, 3).reshape(heads * gaps, cols * cols)
    grad_offsets = lax.dot_general(grad_strip, step_hits, NT, precision=exact)
    grad_table = lax.dot_general(
        bucket_hits, grad_offsets.reshape(heads, gaps * spans), (((0,), (1,)), ((), ())),
        precision=exact,
    )


    sums = jnp.sum(grad_proj, 1, dtype=f32)
    sums = jnp.concatenate([sums[:, :half], sums[:, 2 * half :]], 1)
    sums = tile_scatter(sums).reshape(images, -1, 1, chunk)
    sums_other = swap(jnp.concatenate([sums[here:], sums[:here]], 0), "c")
    sums = jnp.concatenate(pick(at_c, (sums, sums_other)), 2).reshape(images, -1)
    for bit in orders[1:]:
        sums = jnp.concatenate([sums, partner(sums, bit)], 0)
    grad_time = lax.dot_general(timing.astype(f32), sums, TN, precision=exact)


    keep1, keep2, send = on_blocks(
        split_sums_kernel,
        spot,
        [one_sum, two_sum],
        matrices((chunk, wide), (chunk, wide), (chunk, 2 * wide)),
        "split_sums",
    )
    side_got = swap(send, "x")
    (send,) = on_blocks(
        turn_core_kernel, spot, [keep1, side_got], matrices((chunk, wide)), "turn_core"
    )
    fc1_own, fc2_own = on_blocks(
        finish_kernel,
        spot,
        [keep1, keep2, side_got, swap(send, "c")],
        [((chunk, 2 * wide), f32), ((4 * chunk, ff_part), f32)],
        "finish",
    )

    own_two = add_bf16(blocks_at(at_y, None, at_c), own_got)
    other_two = add_bf16(blocks_at(None, at_x, 1 - at_c), other_got)
    own_got = swap(part_of(own_two, 1 - at_x), "x")
    other_got = swap(part_of(other_two, 1 - at_y), "y")
    own_rows = add_bf16(part_of(own_two, at_x), own_got)
    other_rows = add_bf16(part_of(other_two, at_y), other_got)
    other_rows = swap(other_rows, "c")
    last_parts = on_blocks(
        pack_qkv_kernel,
        spot,
        [own_rows, other_rows, out_mine],
        matrices(*[(chunk, 6 * chunk + quarter)] * 4),
        "pack_qkv",
    )
    last = last_parts[0].astype(f32)
    for step in range(1, tiles):
        last = last + shift(last_parts[step], step).astype(f32)
    qkv_own, out_own = last[:, : 6 * chunk], last[:, 6 * chunk :]


    mine = (jnp.arange(4) == member).astype(f32)
    fc1_bias_all = grad_fc1_bias.reshape(tiles, 1, ff_part) * mine[None, :, None]
    core = (jnp.arange(2) == at_c).astype(f32)
    table_all = grad_table.reshape(-1, heads // 2, 1, 2) * core[None, None, :, None]
    small = [
        grad_gain_one,
        grad_shift_one,
        table_all.reshape(-1),
        grad_out_bias,
        grad_gain_two,
        grad_shift_two,
        fc1_bias_all.reshape(-1),
        grad_fc2_bias,
    ]
    total = jnp.concatenate(small)
    for bit in orders:
        total = total + partner(total, bit)
    for step in range(tiles.bit_length() - 1):
        route = [(d, d ^ (1 << step)) for d in range(tiles)]
        total = total + lax.ppermute(total, "rows", route)
    pieces = []
    for part in small:
        pieces.append(total[: part.shape[0]])
        total = total[part.shape[0] :]
    return (
        mixed,
        grad_tokens,
        pieces[0],
        pieces[1],
        low_scatter(qkv_own),
        grad_time,
        pieces[2].reshape(rel_table.shape),
        low_scatter(out_own),
        pieces[3],
        pieces[4],
        pieces[5],
        low_scatter(fc1_own),
        pieces[6],
        low_scatter(fc2_own),
        pieces[7],
    )


def solution(mesh):
    tokens, image, weight = P("images", "rows", None, None), P("images"), P("images", "rows")
    return jax.shard_map(
        shards,
        mesh=mesh,
        in_specs=(
            tokens, tokens, image, image, image, P(), P(), P(), weight, weight,
            P(), weight, P(), P(), P(), weight, P(), weight, P(),
        ),
        out_specs=(
            tokens, tokens, P(), P(), weight, weight, P(), weight, P(), P(),
            P(), weight, P(), weight, P(),
        ),
        check_vma=False,
    )
```

time: 613 us -> 449 us (0.73)
  the two profiles are of different devices: /device:TPU:9 before, /device:TPU:0 now
where the time goes in v2:
time: 449 us; the launch traced here: 441 us
  waiting for transfers between devices  142 us (32%)
  starting transfers between devices  66.8 us (15%)
  local copies, waits for them, and re-layouts  63.6 us (14%)
  matrix products  60 us (13%)
  other arithmetic  53.8 us (12%)
  Pallas kernels  39.9 us (9%)
  between operations  15.6 us (3%)
    ppermute x47, waiting for transfers between devices, partner(): return lax.ppermute(value, 'images', route)  106 us
    dot_general x17, matrix products, dot(): return lax.dot_general(left, right, dims, preferred_element_type=f32)  55.8 us
    ppermute x47, starting transfers between devices, partner(): return lax.ppermute(value, 'images', route)  38.7 us
    unnamed x200, local copies, waits for them, and re-layouts  29 us
    pallas_call x15, Pallas kernels, on_blocks(): pl.pallas_call(kernel, in_specs=[pl.BlockSpec(memory_space=pltpu.SMEM)] +...  19.2 us
    ppermute x9, waiting for transfers between devices, shift(): lax.ppermute(value, 'rows', [(d, (d + step) % tiles) for d in range(tiles)])  17.7 us
    ppermute x9, starting transfers between devices, shift(): lax.ppermute(value, 'rows', [(d, (d + step) % tiles) for d in range(tiles)])  14.9 us
    pallas_call x1, Pallas kernels, attend_back(): pl.pallas_call(functools.partial(attend_back_kernel, heads, scale, (keys...  12.3 us
  transfers between devices with their start and end apart: 68, of which 29 were waited for; matrix products, arithmetic and copies ran while one was open for 31% of the time, Pallas kernels for 8%

profile of v2, /device:TPU:0, one launch (start us, length us, event | category | flops | bytes accessed | tf_op | source)
XLA Modules:
  0.0 441.4 jit_solution(16871726145236149280)
XLA Ops:
  7.3 3.1 collective-permute-start
  10.3 2.6 collective-permute-start.1
  23.0 2.2 add_convert_fusion.2
  25.2 2.0 fusion.98
  32.6 2.0 collective-permute-done.10
  36.2 2.0 collective-permute-done.11
  40.2 2.3 collective-permute-done.12
  50.6 1.8 unpack_qkv.1
  53.7 4.6 %collective-permute-start.3 = (bf16[2,2,32,1152]{3,2,1,0:T(8,128)(2,1)}, bf16[2,2,32,1152]{3,2,1,0:T(8,128)(2,1)S(1)}, u32[]{:S(2)}, u32[]{:S(2)}) collective-permute-start(bf16[2,2,32,1152]{3,2,1,0:T(8,128)(2,1)} %get-tuple-element.63), channel_id=1, source_target_pairs={{0,1},{1,2},{2,3},{4,5},{5,6},{6,7},{8,9},{9,10},{10,11},{12,13},{... | collective-permute-start | bytes 884744 | tf_op jit(solution)/shard_map/ppermute | solution.py:571
  65.4 2.4 pad_maximum_fusion.1
  73.9 3.3 pad_maximum_fusion
  77.2 18.2 %collective-permute-done.16 = bf16[288,1728]{1,0:T(8,128)(2,1)} collective-permute-done((bf16[288,1728]{1,0:T(8,128)(2,1)S(1)}, bf16[288,1728]{1,0:T(8,128)(2,1)}, u32[]{:S(2)}, u32[]{:S(2)}) %collective-permute-start.16) | collective-permute-done | bytes 995360 | tf_op jit(solution)/shard_map/ppermute | solution.py:428
  101.5 2.2 fusion.97
  103.7 5.1 %collective-permute-done.18.refs_6_ = bf16[144,1728]{1,0:T(8,128)(2,1)} collective-permute-done((bf16[144,1728]{1,0:T(8,128)(2,1)S(1)}, bf16[144,1728]{1,0:T(8,128)(2,1)}, u32[]{:S(2)}, u32[]{:S(2)}) %collective-permute-start.18) | collective-permute-done | bytes 497696 | tf_op jit(solution)/shard_map/ppermute | solution.py:428
  108.8 2.5 collective-permute-done.19.refs_7_
  118.5 4.9 %fusion.104 = f32[1024,1728]{1,0:T(8,128)S(1)} fusion(bf16[1024,1152]{1,0:T(8,128)(2,1)S(1)} %bitcast.188, bf16[1152,1728]{1,0:T(8,128)(2,1)S(1)} %place_qkv.1), kind=kOutput, calls=%fused_computation.262 | convolution fusion | flops 4076863488 | bytes 13418496 | tf_op jit(solution)/shard_map/dot_general | solution.py:27
  127.2 8.4 %attend.1 = (bf16[4,128,576]{2,1,0:T(8,128)(2,1)S(1)}, bf16[4,8,128,256]{3,2,1,0:T(8,128)(2,1)S(1)}) custom-call(bf16[4,256,1728]{2,1,0:T(8,128)(2,1)S(1)} %add_convert_fusion.qkv_ref, bf16[8,128,256]{2,1,0:T(8,128)(2,1)S(1)} %fusion.45.bias_ref, f32[4,128,256]{2,1,0:T(8,128)S(1)} %or_convert_fusion.allow_ref), custom_call_target="tpu_custom_call" | custom-call | flops 1073741824 | bytes 4194304 | tf_op jit(solution)/shard_map/attend/pallas_call | solution.py:155
  135.7 4.1 collective-permute-done.24
  140.7 2.7 collective-permute-done.25.refs_3_
  147.9 2.0 fusion.103
  153.6 24.0 %collective-permute-done.28.refs_1_ = bf16[576,1152]{1,0:T(8,128)(2,1)} collective-permute-done((bf16[576,1152]{1,0:T(8,128)(2,1)S(1)}, bf16[576,1152]{1,0:T(8,128)(2,1)}, u32[]{:S(2)}, u32[]{:S(2)}) %collective-permute-start.28) | collective-permute-done | bytes 1327136 | tf_op jit(solution)/shard_map/ppermute | solution.py:428
  180.5 3.3 pad_maximum_fusion.2
  184.0 2.4 constant_dynamic-update-slice_fusion.6
  190.6 5.8 %multiply_convert_fusion = (bf16[1024,1152]{1,0:T(8,128)(2,1)}, f32[1024,1152]{1,0:T(8,128)}) fusion(f32[1152]{0:T(1024)S(1)} %add.449, bf16[1024,1152]{1,0:T(8,128)(2,1)S(1)} %constant_dynamic-update-slice_fusion.4, bf16[1152,1152]{1,0:T(8,128)(2,1)S(1)} %place_fc1.1), kind=kOutput, calls=%fused_computation.15 | convolution fusion | flops 2729705472 | bytes 12096000 | tf_op jit(solution)/shard_map/dot_general | solution.py:27
  196.4 6.8 %all-gather.7.cloned.1.call-done = bf16[1152,1152]{1,0:T(8,128)(2,1)} async-done(((bf16[288,1152]{1,0:T(8,128)(2,1)}), bf16[1152,1152]{1,0:T(8,128)(2,1)}) %all-gather.7.cloned.1.call-update) | async-done | bytes 2654224 | tf_op jit(solution)/shard_map/all_gather | solution.py:449
  207.3 3.3 convolution_convert_fusion.2.grad_ref
  210.7 6.2 %convert_reduce_fusion.1 = (f32[1152]{0:T(1024)S(1)}, bf16[1024,1152]{1,0:T(8,128)(2,1)S(1)}) fusion(f32[1024,1152]{1,0:T(8,128)S(1)} %bitcast.202, bf16[1024,1152]{1,0:T(8,128)(2,1)S(1)} %copy-done.57, bf16[1152,1152]{1,0:T(8,128)(2,1)S(1)} %unpack_fc2.1), kind=kOutput, calls=%fused_computation.14 | convolution fusion | flops 2743860224 | bytes 12096000 | tf_op jit(solution)/shard_map/dot_general | solution.py:27
  216.9 1.9 convolution_convert_fusion.6
  218.9 2.7 collective-permute-done.31
  221.7 1.9 convolution_add_fusion.2
  229.9 2.0 convert_reduce_fusion.2
  234.6 7.0 %collective-permute-done.32 = bf16[256,1152]{1,0:T(8,128)(2,1)} collective-permute-done((bf16[256,1152]{1,0:T(8,128)(2,1)}, bf16[256,1152]{1,0:T(8,128)(2,1)}, u32[]{:S(2)}, u32[]{:S(2)}) %collective-permute-start.32) | collective-permute-done | bytes 589856 | tf_op jit(solution)/shard_map/ppermute | solution.py:428
  241.6 2.7 multiply_reduce_fusion
  244.3 3.6 convert_reduce_fusion.3
  247.9 3.3 convolution_convert_fusion.1.grad_ref
  256.4 2.3 convolution_convert_fusion.3
  259.7 3.0 convolution_convert_fusion.8
  262.7 2.8 collective-permute-done.34.got_ref
  265.5 1.9 pack_fc2.1
  270.2 2.0 copy-done.3
  272.3 12.3 %attend_back.1 = (bf16[4,256,1728]{2,1,0:T(8,128)(2,1)S(1)}, f32[8,32,256]{2,1,0:T(8,128)S(1)}) custom-call(bf16[4,256,1728]{2,1,0:T(8,128)(2,1)S(1)} %copy-done.3, bf16[4,8,128,256]{3,2,1,0:T(8,128)(2,1)S(1)} %copy-done.31, bf16[4,128,576]{2,1,0:T(8,128)(2,1)S(1)} %bitcast.172), custom_call_target="tpu_custom_call" | custom-call | flops 2147483648 | bytes 4194304 | tf_op jit(solution)/shard_map/attend_back/pallas_call | solution.py:178
  285.1 2.4 copy-done.46
  287.6 4.9 %convolution_convert_fusion = bf16[1152,1728]{1,0:T(8,128)(2,1)S(1)} fusion(bf16[1024,1152]{1,0:T(8,128)(2,1)S(1)} %bitcast.189, bf16[1024,1728]{1,0:T(8,128)(2,1)S(1)} %bitcast.167), kind=kOutput, calls=%fused_computation | convolution fusion | flops 4078854144 | bytes 9879552 | tf_op jit(solution)/shard_map/dot_general | solution.py:27
  298.6 2.2 collective-permute-start.56
  300.8 2.9 convolution_convert_fusion.5
  311.7 6.8 %collective-permute-done.60 = f32[4,576]{1,0:T(4,128)S(1)} collective-permute-done((f32[4,576]{1,0:T(4,128)S(1)}, f32[4,576]{1,0:T(4,128)S(1)}, u32[]{:S(2)}, u32[]{:S(2)}) %collective-permute-start.60) | collective-permute-done | bytes 9248 | tf_op jit(solution)/shard_map/ppermute | solution.py:428
  320.1 2.1 broadcast_multiply_fusion
  322.2 1.9 pack_fc1.1
  325.2 2.6 mul.354
  327.8 13.6 %collective-permute-done.61 = f32[8,576]{1,0:T(8,128)S(1)} collective-permute-done((f32[8,576]{1,0:T(8,128)S(1)}, f32[8,576]{1,0:T(8,128)S(1)}, u32[]{:S(2)}, u32[]{:S(2)}) %collective-permute-start.61) | collective-permute-done | bytes 18464 | tf_op jit(solution)/shard_map/ppermute | solution.py:428
  345.6 2.7 fusion.9
  351.9 5.5 %convolution_convert_fusion.4 = bf16[512,1152]{1,0:T(8,128)(2,1)S(1)} fusion(bf16[1152,1728]{1,0:T(8,128)(2,1)} %copy-done.10, bf16[1024,1728]{1,0:T(8,128)(2,1)} %bitcast.168), kind=kOutput, calls=%fused_computation.20 | convolution fusion | flops 2039021568 | bytes 7143424 | tf_op jit(solution)/shard_map/dot_general | solution.py:27
  357.7 3.3 convert_add_fusion
  364.9 2.9 convolution_add_fusion.1
  369.4 4.0 collective-permute-start.40
  377.0 3.4 collective-permute-start.55
  383.2 2.2 collective-permute-done.39
  386.0 3.8 multiply_reduce_fusion.1
  390.1 2.2 fusion.19
  395.0 17.7 %collective-permute-done.54 = bf16[144,1152]{1,0:T(8,128)(2,1)} collective-permute-done((bf16[144,1152]{1,0:T(8,128)(2,1)S(1)}, bf16[144,1152]{1,0:T(8,128)(2,1)}, u32[]{:S(2)}, u32[]{:S(2)}) %collective-permute-start.54) | collective-permute-done | bytes 331808 | tf_op jit(solution)/shard_map/ppermute | solution.py:446
  418.9 3.7 collective-permute-done.43
  422.9 4.1 collective-permute-done.44
  427.2 2.6 fusion.26
  429.8 2.9 collective-permute-done.45
  (469 shorter events, 145.9 us)
Async XLA Ops:
  7.2 104.2 %all-gather.5.cloned.1.call-start = ((), (), s32[]{:S(2)}) async-start(), calls=%async_computation.4 | async-start | bytes 2211840 | tf_op jit(solution)/shard_map/all_gather | solution.py:449
  7.3 31.0 %collective-permute-start = (bf16[144,864]{1,0:T(8,128)(2,1)}, bf16[144,864]{1,0:T(8,128)(2,1)S(1)}, u32[]{:S(2)}, u32[]{:S(2)}) collective-permute-start(bf16[144,864]{1,0:T(8,128)(2,1)} %refs_0_.1), channel_id=1, source_target_pairs={{0,1},{1,2},{2,3},{3,0},{4,5},{5,6},{6,7},{7,4},{8,9},{9,10},{10,1... | collective-permute-start | bytes 746504 | tf_op jit(solution)/shard_map/ppermute | solution.py:446
  10.3 28.0 %collective-permute-start.1 = (bf16[144,864]{1,0:T(8,128)(2,1)}, bf16[144,864]{1,0:T(8,128)(2,1)S(1)}, u32[]{:S(2)}, u32[]{:S(2)}) collective-permute-start(bf16[144,864]{1,0:T(8,128)(2,1)} %refs_0_.1), channel_id=1, source_target_pairs={{0,2},{1,3},{2,0},{3,1},{4,6},{5,7},{6,4},{7,5},{8,10},{9,11},{10,... | collective-permute-start | bytes 746504 | tf_op jit(solution)/shard_map/ppermute | solution.py:446
  12.9 25.4 %collective-permute-start.2 = (bf16[144,864]{1,0:T(8,128)(2,1)}, bf16[144,864]{1,0:T(8,128)(2,1)S(1)}, u32[]{:S(2)}, u32[]{:S(2)}) collective-permute-start(bf16[144,864]{1,0:T(8,128)(2,1)} %refs_0_.1), channel_id=1, source_target_pairs={{0,3},{1,0},{2,1},{3,2},{4,7},{5,4},{6,5},{7,6},{8,11},{9,8},{10,9... | collective-permute-start | bytes 746504 | tf_op jit(solution)/shard_map/ppermute | solution.py:446
  16.0 32.2 %collective-permute-start.6 = (bf16[144,576]{1,0:T(8,128)(2,1)S(1)}, bf16[144,576]{1,0:T(8,128)(2,1)S(1)}, u32[]{:S(2)}, u32[]{:S(2)}) collective-permute-start(bf16[144,576]{1,0:T(8,128)(2,1)S(1)} %get-tuple-element.66), channel_id=1, source_target_pairs={{0,4},{4,0},{8,12},{12,8},{16,20},{20,16},{24,28},{28,24},{1,5},{5... | collective-permute-start | bytes 497672 | tf_op jit(solution)/shard_map/ppermute | solution.py:428
  16.8 14.2 %collective-permute-start.9 = (s32[2,3]{0,1:T(4,128)S(1)}, s32[2,3]{0,1:T(4,128)S(1)}, u32[]{:S(2)}, u32[]{:S(2)}) collective-permute-start(s32[2,3]{0,1:T(4,128)S(1)} %pad_add_fusion), channel_id=1, source_target_pairs={{0,4},{4,0},{8,12},{12,8},{16,20},{20,16},{24,28},{28,24},{1,5},{5... | collective-permute-start | bytes 80 | tf_op jit(solution)/shard_map/ppermute | solution.py:428
  31.1 3.5 collective-permute-start.10
  34.7 3.5 collective-permute-start.11
  38.6 3.8 collective-permute-start.12
  42.4 3.7 collective-permute-start.13
  47.5 10.8 %collective-permute-start.20 = (f32[4,576]{1,0:T(4,128)S(1)}, f32[4,576]{1,0:T(4,128)S(1)}, u32[]{:S(2)}, u32[]{:S(2)}) collective-permute-start(f32[4,576]{1,0:T(4,128)S(1)} %add.429), channel_id=1, source_target_pairs={{0,1},{1,0},{2,3},{3,2},{4,5},{5,4},{6,7},{7,6},{8,9},{9,8},{10,11... | collective-permute-start | bytes 27656 | tf_op jit(solution)/shard_map/ppermute | solution.py:459
  49.0 10.1 %collective-permute-start.7 = (bf16[144,1152]{1,0:T(8,128)(2,1)S(1)}, bf16[144,1152]{1,0:T(8,128)(2,1)S(1)}, u32[]{:S(2)}, u32[]{:S(2)}) collective-permute-start(bf16[144,1152]{1,0:T(8,128)(2,1)S(1)} %get-tuple-element.69), channel_id=1, source_target_pairs={{0,8},{4,12},{8,0},{12,4},{16,24},{20,28},{24,16},{28,20},{1,9},{5... | collective-permute-start | bytes 995336 | tf_op jit(solution)/shard_map/ppermute | solution.py:428
  52.4 15.4 %collective-permute-start.8 = (bf16[144,1728]{1,0:T(8,128)(2,1)}, bf16[144,1728]{1,0:T(8,128)(2,1)}, u32[]{:S(2)}, u32[]{:S(2)}) collective-permute-start(bf16[144,1728]{1,0:T(8,128)(2,1)} %get-tuple-element.71), channel_id=1, source_target_pairs={{0,4},{4,0},{8,12},{12,8},{16,20},{20,16},{24,28},{28,24},{1,5},{5... | collective-permute-start | bytes 1493000 | tf_op jit(solution)/shard_map/ppermute | solution.py:428
  52.4 11.5 %collective-permute-start.4 = (bf16[2,2,32,1152]{3,2,1,0:T(8,128)(2,1)}, bf16[2,2,32,1152]{3,2,1,0:T(8,128)(2,1)S(1)}, u32[]{:S(2)}, u32[]{:S(2)}) collective-permute-start(bf16[2,2,32,1152]{3,2,1,0:T(8,128)(2,1)} %get-tuple-element.64), channel_id=1, source_target_pairs={{1,0},{2,1},{3,2},{5,4},{6,5},{7,6},{9,8},{10,9},{11,10},{13,12},{... | collective-permute-start | bytes 884744 | tf_op jit(solution)/shard_map/ppermute | solution.py:572
  53.7 11.7 %collective-permute-start.3 = (bf16[2,2,32,1152]{3,2,1,0:T(8,128)(2,1)}, bf16[2,2,32,1152]{3,2,1,0:T(8,128)(2,1)S(1)}, u32[]{:S(2)}, u32[]{:S(2)}) collective-permute-start(bf16[2,2,32,1152]{3,2,1,0:T(8,128)(2,1)} %get-tuple-element.63), channel_id=1, source_target_pairs={{0,1},{1,2},{2,3},{4,5},{5,6},{6,7},{8,9},{9,10},{10,11},{12,13},{... | collective-permute-start | bytes 884744 | tf_op jit(solution)/shard_map/ppermute | solution.py:571
  58.4 15.1 %collective-permute-start.21 = (f32[4,1152]{1,0:T(4,128)S(1)}, f32[4,1152]{1,0:T(4,128)S(1)}, u32[]{:S(2)}, u32[]{:S(2)}) collective-permute-start(f32[4,1152]{1,0:T(4,128)S(1)} %pad_maximum_fusion.9), channel_id=1, source_target_pairs={{0,2},{1,3},{2,0},{3,1},{4,6},{5,7},{6,4},{7,5},{8,10},{9,11},{10,... | collective-permute-start | bytes 55304 | tf_op jit(solution)/shard_map/ppermute | solution.py:459
  60.7 142.5 %all-gather.7.cloned.1.call-start = ((), (), s32[]{:S(2)}) async-start(), calls=%async_computation.5 | async-start | bytes 3317760 | tf_op jit(solution)/shard_map/all_gather | solution.py:449
  60.9 9.7 %collective-permute-start.15 = (bf16[144,1152]{1,0:T(8,128)(2,1)S(1)}, bf16[144,1152]{1,0:T(8,128)(2,1)S(1)}, u32[]{:S(2)}, u32[]{:S(2)}) collective-permute-start(bf16[144,1152]{1,0:T(8,128)(2,1)S(1)} %get-tuple-element.73), channel_id=1, source_target_pairs={{0,16},{4,20},{8,24},{12,28},{16,0},{20,4},{24,8},{28,12},{1,17},{... | collective-permute-start | bytes 995336 | tf_op jit(solution)/shard_map/ppermute | solution.py:428
  67.8 6.1 %collective-permute-start.5 = (bf16[2,8,32,1152]{3,2,1,0:T(8,128)(2,1)}, bf16[2,8,32,1152]{3,2,1,0:T(8,128)(2,1)}, u32[]{:S(2)}, u32[]{:S(2)}) collective-permute-start(bf16[2,8,32,1152]{3,2,1,0:T(8,128)(2,1)} %pad_maximum_fusion.1), channel_id=1, source_target_pairs={{0,4},{4,0},{8,12},{12,8},{16,20},{20,16},{24,28},{28,24},{1,5},{5... | collective-permute-start | bytes 3538952 | tf_op jit(solution)/shard_map/ppermute | solution.py:428
  71.4 24.1 %collective-permute-start.16 = (bf16[288,1728]{1,0:T(8,128)(2,1)S(1)}, bf16[288,1728]{1,0:T(8,128)(2,1)}, u32[]{:S(2)}, u32[]{:S(2)}) collective-permute-start(bf16[288,1728]{1,0:T(8,128)(2,1)S(1)} %pad_maximum_fusion.4), channel_id=1, source_target_pairs={{0,8},{4,12},{8,0},{12,4},{16,24},{20,28},{24,16},{28,20},{1,9},{5... | collective-permute-start | bytes 2985992 | tf_op jit(solution)/shard_map/ppermute | solution.py:428
  71.9 23.6 %collective-permute-start.17 = (bf16[288,1728]{1,0:T(8,128)(2,1)S(1)}, bf16[288,1728]{1,0:T(8,128)(2,1)}, u32[]{:S(2)}, u32[]{:S(2)}) collective-permute-start(bf16[288,1728]{1,0:T(8,128)(2,1)S(1)} %pad_maximum_fusion.4), channel_id=1, source_target_pairs={{0,16},{4,20},{8,24},{12,28},{16,0},{20,4},{24,8},{28,12},{1,17},{... | collective-permute-start | bytes 2985992 | tf_op jit(solution)/shard_map/ppermute | solution.py:428
  96.7 12.1 %collective-permute-start.18 = (bf16[144,1728]{1,0:T(8,128)(2,1)S(1)}, bf16[144,1728]{1,0:T(8,128)(2,1)}, u32[]{:S(2)}, u32[]{:S(2)}) collective-permute-start(bf16[144,1728]{1,0:T(8,128)(2,1)S(1)} %get-tuple-element.160.refs_2_), channel_id=1, source_target_pairs={{0,16},{4,20},{8,24},{12,28},{16,0},{20,4},{24,8},{28,12},{1,17},{... | collective-permute-start | bytes 1493000 | tf_op jit(solution)/shard_map/ppermute | solution.py:428
  99.6 11.8 %collective-permute-start.19 = (bf16[144,1728]{1,0:T(8,128)(2,1)S(1)}, bf16[144,1728]{1,0:T(8,128)(2,1)}, u32[]{:S(2)}, u32[]{:S(2)}) collective-permute-start(bf16[144,1728]{1,0:T(8,128)(2,1)S(1)} %get-tuple-element.157.refs_5_), channel_id=1, source_target_pairs={{0,8},{4,12},{8,0},{12,4},{16,24},{20,28},{24,16},{28,20},{1,9},{5... | collective-permute-start | bytes 1493000 | tf_op jit(solution)/shard_map/ppermute | solution.py:428
  116.5 9.3 %collective-permute-start.22 = (bf16[144,1152]{1,0:T(8,128)(2,1)S(1)}, bf16[144,1152]{1,0:T(8,128)(2,1)S(1)}, u32[]{:S(2)}, u32[]{:S(2)}) collective-permute-start(bf16[144,1152]{1,0:T(8,128)(2,1)S(1)} %get-tuple-element.80.refs_0_), channel_id=1, source_target_pairs={{0,8},{4,12},{8,0},{12,4},{16,24},{20,28},{24,16},{28,20},{1,9},{5... | collective-permute-start | bytes 995336 | tf_op jit(solution)/shard_map/ppermute | solution.py:428
  118.0 7.8 %collective-permute-start.23 = (bf16[144,1152]{1,0:T(8,128)(2,1)S(1)}, bf16[144,1152]{1,0:T(8,128)(2,1)S(1)}, u32[]{:S(2)}, u32[]{:S(2)}) collective-permute-start(bf16[144,1152]{1,0:T(8,128)(2,1)S(1)} %get-tuple-element.80.refs_0_), channel_id=1, source_target_pairs={{0,16},{4,20},{8,24},{12,28},{16,0},{20,4},{24,8},{28,12},{1,17},{... | collective-permute-start | bytes 995336 | tf_op jit(solution)/shard_map/ppermute | solution.py:428
  123.5 16.3 %collective-permute-start.24 = (bf16[256,1152]{1,0:T(8,128)(2,1)S(1)}, bf16[256,1152]{1,0:T(8,128)(2,1)S(1)}, u32[]{:S(2)}, u32[]{:S(2)}) collective-permute-start(bf16[256,1152]{1,0:T(8,128)(2,1)S(1)} %copy-done.44), channel_id=1, source_target_pairs={{0,8},{4,12},{8,0},{12,4},{16,24},{20,28},{24,16},{28,20},{1,9},{5... | collective-permute-start | bytes 1769480 | tf_op jit(solution)/shard_map/ppermute | solution.py:428
  125.7 17.7 %collective-permute-start.25 = (bf16[144,1152]{1,0:T(8,128)(2,1)S(1)}, bf16[144,1152]{1,0:T(8,128)(2,1)S(1)}, u32[]{:S(2)}, u32[]{:S(2)}) collective-permute-start(bf16[144,1152]{1,0:T(8,128)(2,1)S(1)} %collective-permute-done.23.refs_2_), channel_id=1, source_target_pairs={{0,8},{4,12},{8,0},{12,4},{16,24},{20,28},{24,16},{28,20},{1,9},{5... | collective-permute-start | bytes 995336 | tf_op jit(solution)/shard_map/ppermute | solution.py:428
  145.6 206.3 %reduce-scatter.3.cloned.1.call-start = ((), (), s32[]{:S(2)}) async-start(), calls=%async_computation.2 | async-start | bytes 1658880 | tf_op jit(solution)/shard_map/reduce_scatter | solution.py:452
  145.9 31.7 %collective-permute-start.28 = (bf16[576,1152]{1,0:T(8,128)(2,1)S(1)}, bf16[576,1152]{1,0:T(8,128)(2,1)}, u32[]{:S(2)}, u32[]{:S(2)}) collective-permute-start(bf16[576,1152]{1,0:T(8,128)(2,1)S(1)} %get-tuple-element.87.refs_0_), channel_id=1, source_target_pairs={{0,16},{4,20},{8,24},{12,28},{16,0},{20,4},{24,8},{28,12},{1,17},{... | collective-permute-start | bytes 3981320 | tf_op jit(solution)/shard_map/ppermute | solution.py:428
  152.0 28.5 %collective-permute-start.27 = (bf16[256,1152]{1,0:T(8,128)(2,1)}, bf16[256,1152]{1,0:T(8,128)(2,1)}, u32[]{:S(2)}, u32[]{:S(2)}) collective-permute-start(bf16[256,1152]{1,0:T(8,128)(2,1)} %add_convert_fusion.1), channel_id=1, source_target_pairs={{0,8},{4,12},{8,0},{12,4},{16,24},{20,28},{24,16},{28,20},{1,9},{5... | collective-permute-start | bytes 1769480 | tf_op jit(solution)/shard_map/ppermute | solution.py:428
  153.5 30.5 %collective-permute-start.30 = (bf16[512,1152]{1,0:T(8,128)(2,1)}, bf16[512,1152]{1,0:T(8,128)(2,1)}, u32[]{:S(2)}, u32[]{:S(2)}) collective-permute-start(bf16[512,1152]{1,0:T(8,128)(2,1)} %get-tuple-element.164), channel_id=1, source_target_pairs={{0,4},{4,0},{8,12},{12,8},{16,20},{20,16},{24,28},{28,24},{1,5},{5... | collective-permute-start | bytes 3538952 | tf_op jit(solution)/shard_map/ppermute | solution.py:428
  183.7 4.0 collective-permute-start.29
  225.9 15.7 %collective-permute-start.32 = (bf16[256,1152]{1,0:T(8,128)(2,1)}, bf16[256,1152]{1,0:T(8,128)(2,1)}, u32[]{:S(2)}, u32[]{:S(2)}) collective-permute-start(bf16[256,1152]{1,0:T(8,128)(2,1)} %slice.377), channel_id=1, source_target_pairs={{0,8},{4,12},{8,0},{12,4},{16,24},{20,28},{24,16},{28,20},{1,9},{5... | collective-permute-start | bytes 1769480 | tf_op jit(solution)/shard_map/ppermute | solution.py:428
  233.1 32.3 %collective-permute-start.34 = (bf16[576,1152]{1,0:T(8,128)(2,1)}, bf16[576,1152]{1,0:T(8,128)(2,1)}, u32[]{:S(2)}, u32[]{:S(2)}) collective-permute-start(bf16[576,1152]{1,0:T(8,128)(2,1)} %dynamic-slice_bitcast_fusion.1), channel_id=1, source_target_pairs={{0,16},{4,20},{8,24},{12,28},{16,0},{20,4},{24,8},{28,12},{1,17},{... | collective-permute-start | bytes 3981320 | tf_op jit(solution)/shard_map/ppermute | solution.py:428
  247.9 8.5 %collective-permute-start.33 = (bf16[256,1152]{1,0:T(8,128)(2,1)}, bf16[256,1152]{1,0:T(8,128)(2,1)}, u32[]{:S(2)}, u32[]{:S(2)}) collective-permute-start(bf16[256,1152]{1,0:T(8,128)(2,1)} %get-tuple-element.150), channel_id=1, source_target_pairs={{0,4},{4,0},{8,12},{12,8},{16,20},{20,16},{24,28},{28,24},{1,5},{5... | collective-permute-start | bytes 1769480 | tf_op jit(solution)/shard_map/ppermute | solution.py:428
  254.0 68.2 %collective-permute-start.37 = (bf16[576,1152]{1,0:T(8,128)(2,1)}, bf16[576,1152]{1,0:T(8,128)(2,1)}, u32[]{:S(2)}, u32[]{:S(2)}) collective-permute-start(bf16[576,1152]{1,0:T(8,128)(2,1)} %dynamic-slice_bitcast_fusion), channel_id=1, source_target_pairs={{0,16},{4,20},{8,24},{12,28},{16,0},{20,4},{24,8},{28,12},{1,17},{... | collective-permute-start | bytes 3981320 | tf_op jit(solution)/shard_map/ppermute | solution.py:428
  268.5 112.7 %reduce-scatter.5.cloned.1.call-start = ((), (), s32[]{:S(2)}) async-start(), calls=%async_computation.3 | async-start | bytes 1658880 | tf_op jit(solution)/shard_map/reduce_scatter | solution.py:452
  295.5 50.1 %collective-permute-start.48 = (bf16[2,144,1728]{2,1,0:T(8,128)(2,1)}, bf16[2,144,1728]{2,1,0:T(8,128)(2,1)}, u32[]{:S(2)}, u32[]{:S(2)}) collective-permute-start(bf16[2,144,1728]{2,1,0:T(8,128)(2,1)} %dynamic-slice_bitcast_fusion.2), channel_id=1, source_target_pairs={{0,8},{4,12},{8,0},{12,4},{16,24},{20,28},{24,16},{28,20},{1,9},{5... | collective-permute-start | bytes 2985992 | tf_op jit(solution)/shard_map/ppermute | solution.py:428
  296.8 7.7 %collective-permute-start.58 = (f32[4,288]{1,0:T(4,128)}, f32[4,288]{1,0:T(4,128)S(1)}, u32[]{:S(2)}, u32[]{:S(2)}) collective-permute-start(f32[4,288]{1,0:T(4,128)} %select_select_fusion), channel_id=1, source_target_pairs={{0,3},{1,0},{2,1},{3,2},{4,7},{5,4},{6,5},{7,6},{8,11},{9,8},{10,9... | collective-permute-start | bytes 13832 | tf_op jit(solution)/shard_map/ppermute | solution.py:446
  298.3 7.8 %collective-permute-start.57 = (f32[4,288]{1,0:T(4,128)}, f32[4,288]{1,0:T(4,128)}, u32[]{:S(2)}, u32[]{:S(2)}) collective-permute-start(f32[4,288]{1,0:T(4,128)} %get-tuple-element.178), channel_id=1, source_target_pairs={{0,2},{1,3},{2,0},{3,1},{4,6},{5,7},{6,4},{7,5},{8,10},{9,11},{10,... | collective-permute-start | bytes 13832 | tf_op jit(solution)/shard_map/ppermute | solution.py:446
  298.6 8.0 %collective-permute-start.56 = (f32[4,288]{1,0:T(4,128)S(1)}, f32[4,288]{1,0:T(4,128)}, u32[]{:S(2)}, u32[]{:S(2)}) collective-permute-start(f32[4,288]{1,0:T(4,128)S(1)} %get-tuple-element.177), channel_id=1, source_target_pairs={{0,1},{1,2},{2,3},{3,0},{4,5},{5,6},{6,7},{7,4},{8,9},{9,10},{10,1... | collective-permute-start | bytes 13832 | tf_op jit(solution)/shard_map/ppermute | solution.py:446
  304.5 41.1 %collective-permute-start.46 = (bf16[2,144,1728]{2,1,0:T(8,128)(2,1)}, bf16[2,144,1728]{2,1,0:T(8,128)(2,1)}, u32[]{:S(2)}, u32[]{:S(2)}) collective-permute-start(bf16[2,144,1728]{2,1,0:T(8,128)(2,1)} %dynamic-slice_bitcast_fusion.3), channel_id=1, source_target_pairs={{0,16},{4,20},{8,24},{12,28},{16,0},{20,4},{24,8},{28,12},{1,17},{... | collective-permute-start | bytes 2985992 | tf_op jit(solution)/shard_map/ppermute | solution.py:428
  306.0 36.6 %collective-permute-start.51 = (bf16[288,1152]{1,0:T(8,128)(2,1)}, bf16[288,1152]{1,0:T(8,128)(2,1)}, u32[]{:S(2)}, u32[]{:S(2)}) collective-permute-start(bf16[288,1152]{1,0:T(8,128)(2,1)} %dynamic-slice_bitcast_fusion.4), channel_id=1, source_target_pairs={{0,16},{4,20},{8,24},{12,28},{16,0},{20,4},{24,8},{28,12},{1,17},{... | collective-permute-start | bytes 1990664 | tf_op jit(solution)/shard_map/ppermute | solution.py:428
  309.0 9.5 %collective-permute-start.60 = (f32[4,576]{1,0:T(4,128)S(1)}, f32[4,576]{1,0:T(4,128)S(1)}, u32[]{:S(2)}, u32[]{:S(2)}) collective-permute-start(f32[4,576]{1,0:T(4,128)S(1)} %reshape.653), channel_id=1, source_target_pairs={{0,8},{4,12},{8,0},{12,4},{16,24},{20,28},{24,16},{28,20},{1,9},{5... | collective-permute-start | bytes 27656 | tf_op jit(solution)/shard_map/ppermute | solution.py:428
  318.5 22.8 %collective-permute-start.61 = (f32[8,576]{1,0:T(8,128)S(1)}, f32[8,576]{1,0:T(8,128)S(1)}, u32[]{:S(2)}, u32[]{:S(2)}) collective-permute-start(f32[8,576]{1,0:T(8,128)S(1)} %pad_maximum_fusion.8), channel_id=1, source_target_pairs={{0,16},{4,20},{8,24},{12,28},{16,0},{20,4},{24,8},{28,12},{1,17},{... | collective-permute-start | bytes 55304 | tf_op jit(solution)/shard_map/ppermute | solution.py:428
  322.2 35.4 %collective-permute-start.35 = (bf16[512,1152]{1,0:T(8,128)(2,1)}, bf16[512,1152]{1,0:T(8,128)(2,1)}, u32[]{:S(2)}, u32[]{:S(2)}) collective-permute-start(bf16[512,1152]{1,0:T(8,128)(2,1)} %convolution_convert_fusion.5), channel_id=1, source_target_pairs={{0,4},{4,0},{8,12},{12,8},{16,20},{20,16},{24,28},{28,24},{1,5},{5... | collective-permute-start | bytes 3538952 | tf_op jit(solution)/shard_map/ppermute | solution.py:428
  344.7 12.8 %collective-permute-start.52 = (bf16[144,1152]{1,0:T(8,128)(2,1)}, bf16[144,1152]{1,0:T(8,128)(2,1)S(1)}, u32[]{:S(2)}, u32[]{:S(2)}) collective-permute-start(bf16[144,1152]{1,0:T(8,128)(2,1)} %dynamic-slice_bitcast_fusion.7), channel_id=1, source_target_pairs={{0,8},{4,12},{8,0},{12,4},{16,24},{20,28},{24,16},{28,20},{1,9},{5... | collective-permute-start | bytes 995336 | tf_op jit(solution)/shard_map/ppermute | solution.py:428
  349.1 25.5 %collective-permute-start.47 = (bf16[144,1728]{1,0:T(8,128)(2,1)}, bf16[144,1728]{1,0:T(8,128)(2,1)}, u32[]{:S(2)}, u32[]{:S(2)}) collective-permute-start(bf16[144,1728]{1,0:T(8,128)(2,1)} %dynamic-slice_bitcast_fusion.6), channel_id=1, source_target_pairs={{0,8},{4,12},{8,0},{12,4},{16,24},{20,28},{24,16},{28,20},{1,9},{5... | collective-permute-start | bytes 1493000 | tf_op jit(solution)/shard_map/ppermute | solution.py:428
  351.0 12.4 %collective-permute-start.49 = (bf16[144,1728]{1,0:T(8,128)(2,1)}, bf16[144,1728]{1,0:T(8,128)(2,1)}, u32[]{:S(2)}, u32[]{:S(2)}) collective-permute-start(bf16[144,1728]{1,0:T(8,128)(2,1)} %dynamic-slice_bitcast_fusion.5), channel_id=1, source_target_pairs={{0,16},{4,20},{8,24},{12,28},{16,0},{20,4},{24,8},{28,12},{1,17},{... | collective-permute-start | bytes 1493000 | tf_op jit(solution)/shard_map/ppermute | solution.py:428
  357.4 7.5 %collective-permute-start.38 = (bf16[512,1152]{1,0:T(8,128)(2,1)S(1)}, bf16[512,1152]{1,0:T(8,128)(2,1)S(1)}, u32[]{:S(2)}, u32[]{:S(2)}) collective-permute-start(bf16[512,1152]{1,0:T(8,128)(2,1)S(1)} %convolution_convert_fusion.4), channel_id=1, source_target_pairs={{0,4},{4,0},{8,12},{12,8},{16,20},{20,16},{24,28},{28,24},{1,5},{5... | collective-permute-start | bytes 3538952 | tf_op jit(solution)/shard_map/ppermute | solution.py:428
  361.9 28.0 %collective-permute-start.36 = (bf16[256,1152]{1,0:T(8,128)(2,1)}, bf16[256,1152]{1,0:T(8,128)(2,1)}, u32[]{:S(2)}, u32[]{:S(2)}) collective-permute-start(bf16[256,1152]{1,0:T(8,128)(2,1)} %slice.376), channel_id=1, source_target_pairs={{0,8},{4,12},{8,0},{12,4},{16,24},{20,28},{24,16},{28,20},{1,9},{5... | collective-permute-start | bytes 1769480 | tf_op jit(solution)/shard_map/ppermute | solution.py:428
  364.6 11.2 %collective-permute-start.50 = (bf16[144,1728]{1,0:T(8,128)(2,1)S(1)}, bf16[144,1728]{1,0:T(8,128)(2,1)S(1)}, u32[]{:S(2)}, u32[]{:S(2)}) collective-permute-start(bf16[144,1728]{1,0:T(8,128)(2,1)S(1)} %fusion.41), channel_id=1, source_target_pairs={{0,4},{4,0},{8,12},{12,8},{16,20},{20,16},{24,28},{28,24},{1,5},{5... | collective-permute-start | bytes 1493000 | tf_op jit(solution)/shard_map/ppermute | solution.py:428
  369.4 13.5 %collective-permute-start.40 = (bf16[2,2,32,1152]{3,2,1,0:T(8,128)(2,1)}, bf16[2,2,32,1152]{3,2,1,0:T(8,128)(2,1)}, u32[]{:S(2)}, u32[]{:S(2)}) collective-permute-start(bf16[2,2,32,1152]{3,2,1,0:T(8,128)(2,1)} %get-tuple-element.156), channel_id=1, source_target_pairs={{0,1},{1,2},{2,3},{4,5},{5,6},{6,7},{8,9},{9,10},{10,11},{12,13},{... | collective-permute-start | bytes 884744 | tf_op jit(solution)/shard_map/ppermute | solution.py:765
  373.3 12.1 %collective-permute-start.39 = (bf16[2,2,32,1152]{3,2,1,0:T(8,128)(2,1)}, bf16[2,2,32,1152]{3,2,1,0:T(8,128)(2,1)}, u32[]{:S(2)}, u32[]{:S(2)}) collective-permute-start(bf16[2,2,32,1152]{3,2,1,0:T(8,128)(2,1)} %get-tuple-element.155), channel_id=1, source_target_pairs={{1,0},{2,1},{3,2},{5,4},{6,5},{7,6},{9,8},{10,9},{11,10},{13,12},{... | collective-permute-start | bytes 884744 | tf_op jit(solution)/shard_map/ppermute | solution.py:764
  377.0 18.0 %collective-permute-start.55 = (bf16[144,1152]{1,0:T(8,128)(2,1)S(1)}, bf16[144,1152]{1,0:T(8,128)(2,1)S(1)}, u32[]{:S(2)}, u32[]{:S(2)}) collective-permute-start(bf16[144,1152]{1,0:T(8,128)(2,1)S(1)} %get-tuple-element.103), channel_id=1, source_target_pairs={{0,3},{1,0},{2,1},{3,2},{4,7},{5,4},{6,5},{7,6},{8,11},{9,8},{10,9... | collective-permute-start | bytes 995336 | tf_op jit(solution)/shard_map/ppermute | solution.py:446
  380.4 32.2 %collective-permute-start.54 = (bf16[144,1152]{1,0:T(8,128)(2,1)S(1)}, bf16[144,1152]{1,0:T(8,128)(2,1)}, u32[]{:S(2)}, u32[]{:S(2)}) collective-permute-start(bf16[144,1152]{1,0:T(8,128)(2,1)S(1)} %get-tuple-element.102), channel_id=1, source_target_pairs={{0,2},{1,3},{2,0},{3,1},{4,6},{5,7},{6,4},{7,5},{8,10},{9,11},{10,... | collective-permute-start | bytes 995336 | tf_op jit(solution)/shard_map/ppermute | solution.py:446
  382.9 29.8 %collective-permute-start.53 = (bf16[144,1152]{1,0:T(8,128)(2,1)S(1)}, bf16[144,1152]{1,0:T(8,128)(2,1)S(1)}, u32[]{:S(2)}, u32[]{:S(2)}) collective-permute-start(bf16[144,1152]{1,0:T(8,128)(2,1)S(1)} %get-tuple-element.101), channel_id=1, source_target_pairs={{0,1},{1,2},{2,3},{3,0},{4,5},{5,6},{6,7},{7,4},{8,9},{9,10},{10,1... | collective-permute-start | bytes 995336 | tf_op jit(solution)/shard_map/ppermute | solution.py:446
  385.4 8.0 %collective-permute-start.62 = (bf16[144,1152]{1,0:T(8,128)(2,1)S(1)}, bf16[144,1152]{1,0:T(8,128)(2,1)S(1)}, u32[]{:S(2)}, u32[]{:S(2)}) collective-permute-start(bf16[144,1152]{1,0:T(8,128)(2,1)S(1)} %get-tuple-element.106), channel_id=1, source_target_pairs={{0,8},{4,12},{8,0},{12,4},{16,24},{20,28},{24,16},{28,20},{1,9},{5... | collective-permute-start | bytes 995336 | tf_op jit(solution)/shard_map/ppermute | solution.py:428
  390.0 4.1 collective-permute-start.41
  394.0 21.5 %collective-permute-start.63 = (bf16[144,576]{1,0:T(8,128)(2,1)S(1)}, bf16[144,576]{1,0:T(8,128)(2,1)S(1)}, u32[]{:S(2)}, u32[]{:S(2)}) collective-permute-start(bf16[144,576]{1,0:T(8,128)(2,1)S(1)} %turn_core.1), channel_id=1, source_target_pairs={{0,4},{4,0},{8,12},{12,8},{16,20},{20,16},{24,28},{28,24},{1,5},{5... | collective-permute-start | bytes 497672 | tf_op jit(solution)/shard_map/ppermute | solution.py:428
  394.1 24.2 %collective-permute-start.42 = (f32[15616]{0:T(1024)S(1)}, f32[15616]{0:T(1024)S(1)}, u32[]{:S(2)}, u32[]{:S(2)}) collective-permute-start(f32[15616]{0:T(1024)S(1)} %add.473), channel_id=1, source_target_pairs={{0,8},{4,12},{8,0},{12,4},{16,24},{20,28},{24,16},{28,20},{1,9},{5... | collective-permute-start | bytes 187400 | tf_op jit(solution)/shard_map/ppermute | solution.py:428
  418.3 4.3 collective-permute-start.43
  422.7 4.3 collective-permute-start.44
  427.0 5.6 %collective-permute-start.45 = (f32[15616]{0:T(1024)S(1)}, f32[15616]{0:T(1024)S(1)}, u32[]{:S(2)}, u32[]{:S(2)}) collective-permute-start(f32[15616]{0:T(1024)S(1)} %add.476), channel_id=1, source_target_pairs={{0,2},{1,3},{2,0},{3,1},{4,6},{5,7},{6,4},{7,5},{8,10},{9,11},{10,... | collective-permute-start | bytes 187400 | tf_op jit(solution)/shard_map/ppermute | solution.py:856
  (97 other events, 740.5 us)
Sparse Core Ops, SparseCore 0:
  60.8 39.9 all-gather.4
  145.7 57.3 all-gather.6
  268.6 29.4 reduce-scatter.2
  327.9 29.2 reduce-scatter.4
